TPU v7x, 128 devices: a whole 4x4x4 slice. The times are simulated.
128 devices in a mesh: ctx: 16 (over x, y), fsdp: 8 (over z, core).
Axes of the slice: x: 4, y: 4, z: 4, core: 2. Of those that a mesh axis runs over, the one named last changes fastest.
Arguments:
- tokens: bfloat16 [8, 2048, 1024], P('fsdp', 'ctx'), may hold values from -6 to 6
- gain_one: bfloat16 [1024], P('fsdp'), may hold values from 0.5 to 1.5
- w_mamba_in: bfloat16 [1024, 3328], P('fsdp'), may hold values from -0.1875 to 0.1875
- conv_weight: bfloat16 [1792, 4], P('fsdp'), may hold values from -4 to 4
- w_mamba_out: bfloat16 [1536, 1024], P('fsdp'), may hold values from -0.15625 to 0.15625
- w_qkv: bfloat16 [1024, 768], P('fsdp'), may hold values from -0.1875 to 0.1875
- w_attn_out: bfloat16 [512, 1024], P('fsdp'), may hold values from -2 to 2
- gain_two: bfloat16 [1024], P('fsdp'), may hold values from 0.5 to 1.5
- w_gate_up: bfloat16 [1024, 4096], P('fsdp'), may hold values from -0.1875 to 0.1875
- w_down: bfloat16 [2048, 1024], P('fsdp'), may hold values from -0.125 to 0.125
- decays: float32 [8, 2048, 24], P('fsdp', 'ctx'), may hold values from 0.4 to 1, as said below
- input_gates: float32 [8, 2048, 24], P('fsdp', 'ctx'), may hold values from 0 to 2.5
- grad_out: bfloat16 [8, 2048, 1024], P('fsdp', 'ctx'), may hold values from -6 to 6
Outputs:
- output: bfloat16 [8, 2048, 1024], P('fsdp', 'ctx')
- grad_tokens: float32 [8, 2048, 1024], P('fsdp', 'ctx')
- grad_gain_one: float32 [1024], P('fsdp')
- grad_w_mamba_in: float32 [1024, 3328], P('fsdp')
- grad_conv_weight: float32 [1792, 4], P('fsdp')
- grad_w_mamba_out: float32 [1536, 1024], P('fsdp')
- grad_w_qkv: float32 [1024, 768], P('fsdp')
- grad_w_attn_out: float32 [512, 1024], P('fsdp')
- grad_gain_two: float32 [1024], P('fsdp')
- grad_w_gate_up: float32 [1024, 4096], P('fsdp')
- grad_w_down: float32 [2048, 1024], P('fsdp')
Inputs may be any that keep to these rules, and one draw needn't show every extreme that they name: `decays`: each entry is exp(-r) with r > 0.
All inputs are finite; a program needn't handle non-finite values.
Results may differ from a plain program's by a relative error of at most 0.025.
Values may be sent and summed in bfloat16 or wider, within the bound.
No kernel may reach another device: no remote copies, remote signals or barrier semaphores. Data moves between devices by JAX's collectives and lax.ppermute only.
A program may use at most 128 MiB of HBM per device.

v0:
```python
import jax
import jax.numpy as jnp
from jax import lax
from jax.sharding import PartitionSpec as P

QH = 8
KH = 2
HD = 64
MIXER_HEADS = 24
MP = 64
NS = 128
CONV = 4
FF = 2048
SSD_BLOCK = 128
KEY_BLOCK = 512


epsilon = 1e-05
rope_base = 10000.0
masked_value = -1e30
highest = lax.Precision.HIGHEST


def passed_along(value, axis, steps):
    count = lax.axis_size(axis)
    leading, last = (max(0, -steps), min(count, count - steps))
    return lax.ppermute(value, axis, [(source, source + steps) for source in range(leading, last)])


def prefix(value, axis, combine, identity, reverse):
    length, mine = (lax.axis_size(axis), lax.axis_index(axis))
    everything = jax.tree.map(
        lambda part, kind: lax.all_gather(part.astype(kind), axis),
        value,
        (jnp.bfloat16, jnp.bfloat16),
    )
    start = jax.tree.map(
        lambda part, zero: jnp.broadcast_to(jnp.asarray(zero, part.dtype), part.shape),
        value,
        identity,
    )

    def hop(k, before):
        at = length - 1 - k if reverse else k
        reached = at > mine if reverse else at < mine
        new = combine(
            before, jax.tree.map(lambda part, own: part[at].astype(own.dtype), everything, value)
        )
        return jax.tree.map(lambda a, b: jnp.where(reached, a, b), new, before)

    return lax.fori_loop(0, length, hop, start)


def silu(entries):
    return entries * jax.nn.sigmoid(entries)


def silu_slope(entries):
    logistic = jax.nn.sigmoid(entries)
    return logistic * (1.0 + entries * (1.0 - logistic))


def rotate(values, positions, direction):
    half_dim = HD // 2
    frequency = jnp.exp(-jnp.log(rope_base) * (2.0 * jnp.arange(half_dim).astype(jnp.float32) / HD))
    angles = positions[:, None] * frequency[None, :]
    cosine = jnp.cos(angles)[:, None, :]
    sine_part = jnp.sin(angles)[:, None, :]
    front_half = values[..., :half_dim]
    back_half = values[..., half_dim:]
    return jnp.concatenate(
        [
            front_half * cosine - direction * back_half * sine_part,
            back_half * cosine + direction * front_half * sine_part,
        ],
        axis=-1,
    )


def ssd_step(state_in, pieces):
    inputs_x, input_b, input_c, gate_vals, log_decay = pieces
    cumulative = jnp.cumsum(log_decay, axis=0)
    length = log_decay.shape[0]
    row_ids = lax.broadcasted_iota(jnp.int32, (length, length), 0)
    col_ids = lax.broadcasted_iota(jnp.int32, (length, length), 1)
    causal = (col_ids <= row_ids)[None]
    spread = cumulative.T[:, :, None] - cumulative.T[:, None, :]
    weights = jnp.where(causal, jnp.exp(jnp.where(causal, spread, 0.0)), 0.0)
    products_cb = jnp.dot(
        input_c.astype(jnp.bfloat16),
        input_b.T.astype(jnp.bfloat16),
        preferred_element_type=jnp.float32,
    )
    mixing = weights * products_cb[None] * gate_vals.T[:, None, :]
    outputs = jnp.einsum("hts,shp->thp", mixing, inputs_x, precision=highest)
    carried = jnp.exp(cumulative)[:, :, None] * jnp.einsum(
        "hpn,tn->thp", state_in, input_c, precision=highest
    )
    remain = jnp.exp(cumulative[-1][None, :] - cumulative) * gate_vals
    new_state = jnp.exp(cumulative[-1])[:, None, None] * state_in + jnp.einsum(
        "sh,shp,sn->hpn", remain, inputs_x, input_b, precision=highest
    )
    return (new_state, outputs + carried)


def ssd_run(inputs_x, input_b, input_c, gate_vals, log_decay, state_in):
    row_count = inputs_x.shape[0]
    block_total = row_count // SSD_BLOCK
    pieces = (
        inputs_x.reshape(block_total, SSD_BLOCK, inputs_x.shape[1], inputs_x.shape[2]),
        input_b.reshape(block_total, SSD_BLOCK, input_b.shape[1]),
        input_c.reshape(block_total, SSD_BLOCK, input_c.shape[1]),
        gate_vals.reshape(block_total, SSD_BLOCK, gate_vals.shape[1]),
        log_decay.reshape(block_total, SSD_BLOCK, log_decay.shape[1]),
    )
    final_state, outputs = lax.scan(jax.checkpoint(ssd_step), state_in, pieces)
    return (outputs.reshape(inputs_x.shape), final_state)


def chain_step(earlier, later):
    return (earlier[0] * later[0], later[0][:, None, None] * earlier[1] + later[1])


def rms_back(grad_normed, normed, inverse, gain):
    scaled = grad_normed * gain
    return inverse * (scaled - normed * jnp.mean(scaled * normed, axis=-1, keepdims=True))


def block_scores(grouped_q, query_pos, block_idx, key_block):
    scores = jnp.einsum(
        "tgrd,kgd->grtk",
        grouped_q,
        key_block.reshape(KEY_BLOCK, KH, HD),
        preferred_element_type=jnp.float32,
    ) * HD ** (-0.5)
    key_pos = block_idx * KEY_BLOCK + jnp.arange(KEY_BLOCK)
    allowed = key_pos[None, :] <= query_pos[:, None]
    return jnp.where(allowed, scores, masked_value)


def forward_attend(grouped_q, query_pos, key_all, value_all):
    rows = grouped_q.shape[0]
    group_size = QH // KH
    last_row = jnp.max(query_pos)
    block_count = key_all.shape[0] // KEY_BLOCK

    def total_step(block_idx, carried):

        def total_update(state_pair):
            row_max, row_sum = state_pair
            key_block = lax.dynamic_slice_in_dim(key_all, block_idx * KEY_BLOCK, KEY_BLOCK, 0)
            scores = block_scores(grouped_q, query_pos, block_idx, key_block)
            new_max = jnp.maximum(row_max, jnp.max(scores, axis=-1))
            new_sum = row_sum * jnp.exp(row_max - new_max) + jnp.sum(
                jnp.exp(scores - new_max[..., None]), axis=-1
            )
            return (new_max, new_sum)

        return lax.cond(
            block_idx * KEY_BLOCK <= last_row, total_update, lambda unchanged: unchanged, carried
        )

    start_pair = (
        jnp.full((KH, group_size, rows), masked_value, jnp.float32),
        jnp.zeros((KH, group_size, rows), jnp.float32),
    )
    row_max, row_sum = lax.fori_loop(0, block_count, total_step, start_pair)
    log_total = row_max + jnp.log(row_sum)

    def mix_step(block_idx, totals):

        def mix_update(running):
            key_block = lax.dynamic_slice_in_dim(key_all, block_idx * KEY_BLOCK, KEY_BLOCK, 0)
            value_block = lax.dynamic_slice_in_dim(value_all, block_idx * KEY_BLOCK, KEY_BLOCK, 0)
            scores = block_scores(grouped_q, query_pos, block_idx, key_block)
            probabilities = jnp.exp(scores - log_total[..., None]).astype(jnp.bfloat16)
            return running + jnp.einsum(
                "grtk,kgd->tgrd",
                probabilities,
                value_block.reshape(KEY_BLOCK, KH, HD),
                preferred_element_type=jnp.float32,
            )

        return lax.cond(
            block_idx * KEY_BLOCK <= last_row, mix_update, lambda unchanged: unchanged, totals
        )

    mixer_output = lax.fori_loop(
        0, block_count, mix_step, jnp.zeros((rows, KH, group_size, HD), jnp.float32)
    )
    return (log_total, mixer_output)


def backward_attend(
    grouped_q,
    mixer_gradient,
    mixer_output,
    log_total,
    query_pos,
    key_all,
    value_all,
    grad_keys,
    grad_values,
):
    rows = grouped_q.shape[0]
    group_size = QH // KH
    kv_width = KH * HD
    last_row = jnp.max(query_pos)
    block_count = key_all.shape[0] // KEY_BLOCK
    row_difference = jnp.einsum("apoz,apoz->poa", mixer_gradient.astype(jnp.float32), mixer_output)

    def back_step(block_idx, carried):

        def back_update(triple):
            grad_query, keys_sum, values_sum = triple
            start = block_idx * KEY_BLOCK
            key_block = lax.dynamic_slice_in_dim(key_all, start, KEY_BLOCK, 0)
            value_block = lax.dynamic_slice_in_dim(value_all, start, KEY_BLOCK, 0)
            probabilities = jnp.exp(
                block_scores(grouped_q, query_pos, block_idx, key_block) - log_total[..., None]
            )
            rounded = probabilities.astype(jnp.bfloat16)
            grad_probs = jnp.einsum(
                "tgrd,kgd->grtk",
                mixer_gradient,
                value_block.reshape(KEY_BLOCK, KH, HD),
                preferred_element_type=jnp.float32,
            )
            grad_scores = (probabilities * (grad_probs - row_difference[..., None])).astype(
                jnp.bfloat16
            )
            grad_query = grad_query + jnp.einsum(
                "grtk,kgd->tgrd",
                grad_scores,
                key_block.reshape(KEY_BLOCK, KH, HD),
                preferred_element_type=jnp.float32,
            )
            key_part = jnp.einsum(
                "grtk,tgrd->kgd", grad_scores, grouped_q, preferred_element_type=jnp.float32
            ).reshape(KEY_BLOCK, kv_width)
            value_part = jnp.einsum(
                "grtk,tgrd->kgd", rounded, mixer_gradient, preferred_element_type=jnp.float32
            ).reshape(KEY_BLOCK, kv_width)
            keys_sum = lax.dynamic_update_slice_in_dim(
                keys_sum,
                lax.dynamic_slice_in_dim(keys_sum, start, KEY_BLOCK, 0) + key_part,
                start,
                0,
            )
            values_sum = lax.dynamic_update_slice_in_dim(
                values_sum,
                lax.dynamic_slice_in_dim(values_sum, start, KEY_BLOCK, 0) + value_part,
                start,
                0,
            )
            return (grad_query, keys_sum, values_sum)

        return lax.cond(
            block_idx * KEY_BLOCK <= last_row, back_update, lambda unchanged: unchanged, carried
        )

    start_triple = (jnp.zeros((rows, KH, group_size, HD), jnp.float32), grad_keys, grad_values)
    return lax.fori_loop(0, block_count, back_step, start_triple)


def on_device(
    tokens,
    gain_one,
    w_mamba_in,
    conv_weight,
    w_mamba_out,
    w_qkv,
    w_attn_out,
    gain_two,
    w_gate_up,
    w_down,
    decays,
    input_gates,
    grad_out,
):
    tokens = tokens[0]
    decays = decays[0]
    input_gates = input_gates[0]
    grad_out = grad_out[0]
    tok_rows = tokens.shape[0]
    inner_width = MIXER_HEADS * MP
    q_width = QH * HD
    kv_width = KH * HD
    group_size = QH // KH
    score_scale = HD ** (-0.5)
    offset = lax.axis_index("ctx") * tok_rows
    g_one, w_min, w_conv, w_mout, w_proj, w_aout, g_two, w_gu, w_dn = (
        lax.all_gather(gain_one, "fsdp", axis=0, tiled=True),
        lax.all_gather(w_mamba_in, "fsdp", axis=0, tiled=True),
        lax.all_gather(conv_weight, "fsdp", axis=0, tiled=True),
        lax.all_gather(w_mamba_out, "fsdp", axis=0, tiled=True),
        lax.all_gather(w_qkv, "fsdp", axis=0, tiled=True),
        lax.all_gather(w_attn_out, "fsdp", axis=0, tiled=True),
        lax.all_gather(gain_two, "fsdp", axis=0, tiled=True),
        lax.all_gather(w_gate_up, "fsdp", axis=0, tiled=True),
        lax.all_gather(w_down, "fsdp", axis=0, tiled=True),
    )
    gain_first = g_one.astype(jnp.float32)
    gain_second = g_two.astype(jnp.float32)
    hidden_in = tokens.astype(jnp.float32)
    inverse_one = lax.rsqrt(jnp.mean(hidden_in * hidden_in, axis=-1, keepdims=True) + epsilon)
    normed = hidden_in * inverse_one
    shared = (normed * gain_first).astype(jnp.bfloat16)
    projected = jnp.dot(shared, w_min, preferred_element_type=jnp.float32)
    gating = projected[:, :inner_width]
    conv_in = projected[:, inner_width:].astype(jnp.bfloat16)
    prior_rows = passed_along(conv_in[tok_rows - (CONV - 1) :], "ctx", 1)
    padded = jnp.concatenate([prior_rows, conv_in], axis=0)
    conv_taps = w_conv.astype(jnp.float32)
    conv_out = jnp.zeros((tok_rows, conv_in.shape[1]), jnp.float32)
    for tap_index in range(CONV):
        conv_out = (
            conv_out
            + padded[tap_index : tap_index + tok_rows].astype(jnp.float32)
            * conv_taps[:, tap_index][None, :]
        )
    activated = silu(conv_out).astype(jnp.bfloat16).astype(jnp.float32)
    inputs_x = activated[:, :inner_width].reshape(tok_rows, MIXER_HEADS, MP)
    input_b = activated[:, inner_width : inner_width + NS]
    input_c = activated[:, inner_width + NS :]
    log_decay = jnp.log(decays)
    zero_state = jnp.zeros((MIXER_HEADS, MP, NS), jnp.float32)

    def local_states(part_x, part_b, part_c):
        return ssd_run(part_x, part_b, part_c, input_gates, log_decay, zero_state)

    (local_out, local_end), pull_states = jax.vjp(local_states, inputs_x, input_b, input_c)
    cumulative = jnp.cumsum(log_decay, axis=0)
    whole_decay = jnp.exp(cumulative[-1])
    identity = (jnp.ones_like(whole_decay), jnp.zeros_like(local_end))
    start_state = prefix((whole_decay, local_end), "ctx", chain_step, identity, False)[1]
    reach_decay = jnp.exp(cumulative)
    ssd_out = local_out + reach_decay[:, :, None] * jnp.einsum(
        "hpn,tn->thp", start_state, input_c, precision=highest
    )
    ssd_flat = ssd_out.reshape(tok_rows, inner_width)
    gate_act = silu(gating)
    mamba_in = (ssd_flat * gate_act).astype(jnp.bfloat16)
    mamba_out = jnp.dot(mamba_in, w_mout, preferred_element_type=jnp.float32)
    projections = jnp.dot(shared, w_proj, preferred_element_type=jnp.float32)
    positions = (offset + jnp.arange(tok_rows)).astype(jnp.float32)
    queries = rotate(projections[:, :q_width].reshape(tok_rows, QH, HD), positions, 1.0).astype(
        jnp.bfloat16
    )
    key_local = rotate(
        projections[:, q_width : q_width + kv_width].reshape(tok_rows, KH, HD), positions, 1.0
    )
    key_local = key_local.astype(jnp.bfloat16).reshape(tok_rows, kv_width)
    value_local = projections[:, q_width + kv_width :].astype(jnp.bfloat16)
    key_all, value_all = (
        lax.all_gather(key_local, "ctx", axis=0, tiled=True),
        lax.all_gather(value_local, "ctx", axis=0, tiled=True),
    )
    grouped = queries.reshape(tok_rows, KH, group_size, HD)
    query_pos = offset + jnp.arange(tok_rows)
    log_total, mixer_output = forward_attend(grouped, query_pos, key_all, value_all)
    attended = mixer_output.reshape(tok_rows, q_width).astype(jnp.bfloat16)
    attn_out = jnp.dot(attended, w_aout, preferred_element_type=jnp.float32)
    residual = hidden_in + attn_out + mamba_out
    inverse_two = lax.rsqrt(jnp.mean(residual * residual, axis=-1, keepdims=True) + epsilon)
    normed_two = residual * inverse_two
    second = (normed_two * gain_second).astype(jnp.bfloat16)
    gate_up = jnp.dot(second, w_gu, preferred_element_type=jnp.float32)
    gate_part = gate_up[:, :FF]
    up_part = gate_up[:, FF:]
    hidden_act = (silu(gate_part) * up_part).astype(jnp.bfloat16)
    result = residual + jnp.dot(hidden_act, w_dn, preferred_element_type=jnp.float32)
    output = result.astype(jnp.bfloat16)
    grad_dn = jnp.einsum("tf,td->fd", hidden_act, grad_out, preferred_element_type=jnp.float32)
    grad_hidden = jnp.einsum("td,fd->tf", grad_out, w_dn, preferred_element_type=jnp.float32)
    grad_gu_low = jnp.concatenate(
        [grad_hidden * up_part * silu_slope(gate_part), grad_hidden * silu(gate_part)], axis=1
    ).astype(jnp.bfloat16)
    grad_gu = jnp.einsum("td,tf->df", second, grad_gu_low, preferred_element_type=jnp.float32)
    grad_second = jnp.einsum("tf,df->td", grad_gu_low, w_gu, preferred_element_type=jnp.float32)
    grad_g_two = jnp.sum(grad_second * normed_two, axis=0)
    grad_residual = grad_out.astype(jnp.float32) + rms_back(
        grad_second, normed_two, inverse_two, gain_second
    )
    branch_grad = grad_residual.astype(jnp.bfloat16)
    grad_aout = jnp.einsum("tq,td->qd", attended, branch_grad, preferred_element_type=jnp.float32)
    grad_attended = jnp.einsum("td,qd->tq", branch_grad, w_aout, preferred_element_type=jnp.float32)
    grad_mixed = grad_attended.astype(jnp.bfloat16).reshape(tok_rows, KH, group_size, HD)
    grad_mout = jnp.einsum("ti,td->id", mamba_in, branch_grad, preferred_element_type=jnp.float32)
    grad_mamba_in = jnp.einsum("td,id->ti", branch_grad, w_mout, preferred_element_type=jnp.float32)
    grad_ssd = lax.optimization_barrier((grad_mamba_in * gate_act).astype(jnp.bfloat16)).astype(
        jnp.float32
    )
    grad_ssd = grad_ssd.reshape(tok_rows, MIXER_HEADS, MP)
    grad_gating = grad_mamba_in * ssd_flat * silu_slope(gating)
    direct = jnp.einsum("th,thp,tn->hpn", reach_decay, grad_ssd, input_c, precision=highest)
    carried_back = prefix((whole_decay, direct), "ctx", chain_step, identity, True)[1]
    grad_x_ssd, grad_b, grad_c = pull_states((grad_ssd, carried_back))
    grad_c = grad_c + jnp.einsum(
        "th,thp,hpn->tn", reach_decay, grad_ssd, start_state, precision=highest
    )
    grad_act = jnp.concatenate([grad_x_ssd.reshape(tok_rows, inner_width), grad_b, grad_c], axis=1)
    grad_conv_out = (grad_act * silu_slope(conv_out)).astype(jnp.bfloat16)
    ahead_rows = passed_along(grad_conv_out[: CONV - 1], "ctx", -1)
    extended = jnp.concatenate([grad_conv_out, ahead_rows], axis=0)
    grad_conv_in = jnp.zeros((tok_rows, conv_in.shape[1]), jnp.float32)
    grad_tap_list = []
    for tap_index in range(CONV):
        lead = CONV - 1 - tap_index
        grad_conv_in = (
            grad_conv_in
            + extended[lead : lead + tok_rows].astype(jnp.float32)
            * conv_taps[:, tap_index][None, :]
        )
        grad_tap_list.append(
            jnp.sum(
                grad_conv_out.astype(jnp.float32)
                * padded[tap_index : tap_index + tok_rows].astype(jnp.float32),
                axis=0,
            )
        )
    grad_conv = jnp.stack(grad_tap_list, axis=1)
    grad_proj_m = jnp.concatenate([grad_gating, grad_conv_in], axis=1).astype(jnp.bfloat16)
    grad_min = jnp.einsum("td,tc->dc", shared, grad_proj_m, preferred_element_type=jnp.float32)
    grad_shared = jnp.einsum("tc,dc->td", grad_proj_m, w_min, preferred_element_type=jnp.float32)
    empty_grads = jnp.zeros((key_all.shape[0], kv_width), jnp.float32)
    grad_query, grad_keys, grad_values = backward_attend(
        grouped,
        grad_mixed,
        mixer_output,
        log_total,
        query_pos,
        key_all,
        value_all,
        empty_grads,
        empty_grads,
    )
    grad_query = grad_query.reshape(tok_rows, q_width)
    key_share, value_share = (
        lax.psum_scatter(
            grad_keys.astype(jnp.bfloat16), "ctx", scatter_dimension=0, tiled=True
        ).astype(jnp.float32),
        lax.psum_scatter(
            grad_values.astype(jnp.bfloat16), "ctx", scatter_dimension=0, tiled=True
        ).astype(jnp.float32),
    )
    grad_q_pre = rotate(grad_query.reshape(tok_rows, QH, HD) * score_scale, positions, -1.0)
    grad_k_pre = rotate((key_share * score_scale).reshape(tok_rows, KH, HD), positions, -1.0)
    grad_proj_a = jnp.concatenate(
        [
            grad_q_pre.reshape(tok_rows, q_width),
            grad_k_pre.reshape(tok_rows, kv_width),
            value_share,
        ],
        axis=1,
    ).astype(jnp.bfloat16)
    grad_proj = jnp.einsum("td,tc->dc", shared, grad_proj_a, preferred_element_type=jnp.float32)
    grad_shared = grad_shared + jnp.einsum(
        "tc,dc->td", grad_proj_a, w_proj, preferred_element_type=jnp.float32
    )
    grad_g_one = jnp.sum(grad_shared * normed, axis=0)
    grad_tokens = grad_residual + rms_back(grad_shared, normed, inverse_one, gain_first)
    partials = (
        lax.psum_scatter(
            grad_g_one.astype(jnp.bfloat16), "fsdp", scatter_dimension=0, tiled=True
        ).astype(jnp.float32),
        lax.psum_scatter(
            grad_min.astype(jnp.bfloat16), "fsdp", scatter_dimension=0, tiled=True
        ).astype(jnp.float32),
        lax.psum_scatter(
            grad_conv.astype(jnp.bfloat16), "fsdp", scatter_dimension=0, tiled=True
        ).astype(jnp.float32),
        lax.psum_scatter(
            grad_mout.astype(jnp.bfloat16), "fsdp", scatter_dimension=0, tiled=True
        ).astype(jnp.float32),
        lax.psum_scatter(
            grad_proj.astype(jnp.bfloat16), "fsdp", scatter_dimension=0, tiled=True
        ).astype(jnp.float32),
        lax.psum_scatter(
            grad_aout.astype(jnp.bfloat16), "fsdp", scatter_dimension=0, tiled=True
        ).astype(jnp.float32),
        lax.psum_scatter(
            grad_g_two.astype(jnp.bfloat16), "fsdp", scatter_dimension=0, tiled=True
        ).astype(jnp.float32),
        lax.psum_scatter(
            grad_gu.astype(jnp.bfloat16), "fsdp", scatter_dimension=0, tiled=True
        ).astype(jnp.float32),
        lax.psum_scatter(
            grad_dn.astype(jnp.bfloat16), "fsdp", scatter_dimension=0, tiled=True
        ).astype(jnp.float32),
    )
    shares = (
        lax.psum(partials[0].astype(jnp.bfloat16), "ctx").astype(jnp.float32),
        lax.psum(partials[1].astype(jnp.bfloat16), "ctx").astype(jnp.float32),
        lax.psum(partials[2].astype(jnp.bfloat16), "ctx").astype(jnp.float32),
        lax.psum(partials[3].astype(jnp.bfloat16), "ctx").astype(jnp.float32),
        lax.psum(partials[4].astype(jnp.bfloat16), "ctx").astype(jnp.float32),
        lax.psum(partials[5].astype(jnp.bfloat16), "ctx").astype(jnp.float32),
        lax.psum(partials[6].astype(jnp.bfloat16), "ctx").astype(jnp.float32),
        lax.psum(partials[7].astype(jnp.bfloat16), "ctx").astype(jnp.float32),
        lax.psum(partials[8].astype(jnp.bfloat16), "ctx").astype(jnp.float32),
    )
    return (
        output[None],
        grad_tokens[None],
        shares[0],
        shares[1],
        shares[2],
        shares[3],
        shares[4],
        shares[5],
        shares[6],
        shares[7],
        shares[8],
    )


def solution(mesh):
    in_specs = (
        P("fsdp", "ctx", None),
        P("fsdp"),
        P("fsdp", None),
        P("fsdp", None),
        P("fsdp", None),
        P("fsdp", None),
        P("fsdp", None),
        P("fsdp"),
        P("fsdp", None),
        P("fsdp", None),
        P("fsdp", "ctx", None),
        P("fsdp", "ctx", None),
        P("fsdp", "ctx", None),
    )
    out_specs = (
        P("fsdp", "ctx", None),
        P("fsdp", "ctx", None),
        P("fsdp"),
        P("fsdp", None),
        P("fsdp", None),
        P("fsdp", None),
        P("fsdp", None),
        P("fsdp", None),
        P("fsdp"),
        P("fsdp", None),
        P("fsdp", None),
    )
    return jax.shard_map(
        on_device, mesh=mesh, in_specs=in_specs, out_specs=out_specs, check_vma=False
    )
```

profile of v0, /device:TPU:38, one launch (start us, length us, event | category | flops | bytes accessed | tf_op | source)
XLA Modules:
  0.0 932.9 jit_solution(7320381882858710663)
XLA Ops:
  11.5 12.6 %all-gather.3 = bf16[8,224,4]{1,2,0:T(4,128)(2,1)S(1)} all-gather(bf16[1,224,4]{1,2,0:T(4,128)(2,1)} %bitcast.329), channel_id=1, replica_groups=mesh['ctx'=16,'fsdp'=8] {'fsdp'}, dimensions={0}, use_global_device_ids=true | all-gather | bytes 16128 | tf_op jit(solution)/shard_map/all_gather | solution.py:295
  24.2 8.3 all-gather.2
  33.4 20.6 %all-gather.19.cloned.1.call-done = bf16[1024,3328]{1,0:T(8,128)(2,1)} async-done(((bf16[128,3328]{1,0:T(8,128)(2,1)}), bf16[1024,3328]{1,0:T(8,128)(2,1)}) %all-gather.19.cloned.1.call-update) | async-done | bytes 6815760 | tf_op jit(solution)/shard_map/all_gather | solution.py:294
  54.0 5.2 fusion.147
  59.3 3.4 collective-permute-start
  62.9 4.1 collective-permute-done
  74.1 18.1 %all-gather.4 = bf16[16,1,24]{2,1,0:T(2,128)(2,1)S(1)} all-gather(bf16[1,1,24]{2,1,0:T(2,128)(2,1)S(1)} %get-tuple-element.1276), channel_id=1, replica_groups=mesh['ctx'=16,'fsdp'=8] {'ctx'}, dimensions={0}, use_global_device_ids=true | all-gather | bytes 816 | tf_op jit(solution)/shard_map/all_gather | solution.py:33
  92.3 9.3 all-gather.5
  103.6 23.9 %all_gather.53 = bf16[2048,128]{1,0:T(8,128)(2,1)S(1)} all-gather(bf16[128,128]{1,0:T(8,128)(2,1)S(1)} %slice.276), channel_id=1, replica_groups=mesh['ctx'=16,'fsdp'=8] {'ctx'}, dimensions={0}, use_global_device_ids=true | all-gather | bytes 557056 | tf_op jit(solution)/shard_map/all_gather | solution.py:357
  128.7 24.8 %all_gather.54 = bf16[2048,128]{0,1:T(8,128)(2,1)S(1)} all-gather(bf16[128,128]{0,1:T(8,128)(2,1)S(1)} %bitcast.326), channel_id=1, replica_groups=mesh['ctx'=16,'fsdp'=8] {'ctx'}, dimensions={0}, use_global_device_ids=true | all-gather | bytes 557056 | tf_op jit(solution)/shard_map/all_gather | solution.py:356
  153.7 7.5 while.96
  161.8 13.3 %while.97 = (s32[]{:T(128)}, f32[128,2,4,64]{0,3,2,1:T(8,128)S(1)}, s32[]{:T(128)}, bf16[2048,128]{0,1:T(8,128)(2,1)}, bf16[2048,128]{0,1:T(8,128)(2,1)S(1)}, /*...) while((s32[]{:T(128)}, f32[128,2,4,64]{0,3,2,1:T(8,128)S(1)}, ...), condition=%wide.region_11.12_spmd.clone, body=%wide.region_8.11_spmd.clone.sunk | while | flops 136446592 | bytes 1583369 | solution.py:188
  162.5 2.7 conditional.10
  165.8 2.7 conditional.10
  169.1 2.7 conditional.10
  172.4 2.7 conditional.10
  175.2 2.4 convolution_add_fusion.1
  178.7 3.9 fusion.44
  182.6 19.7 %while.99 = (s32[]{:T(128)}, f32[24,64,128]{2,1,0:T(8,128)S(1)}, s32[]{:T(128)}, bf16[16,24]{1,0:T(8,128)(2,1)S(1)}, bf16[16,24,64,128]{3,2,1,0:T(8,128)(2,1)}, /*index=5*/s32[]{:T(128)}, s32[]{:T(128)}) while((s32[]{:T(128)}, f32[24,64,128]{2,1,0:T(8,128)S(1)}, s32[]{:T(128)}, bf16[16,24]{1,0:T(8,128)(2,1)S(1)}, ...), condition=%wide.region_14.15_spmd.clone, body=%wide.region_13.14_spmd.clone.sunk | while | flops 983068 | bytes 1966433 | solution.py:51
  204.7 2.3 copy.152
  208.7 2.8 multiply_reduce_fusion.3
  211.5 39.8 %all-gather.23.cloned.1.call-done = bf16[1024,4096]{1,0:T(8,128)(2,1)} async-done(((bf16[128,4096]{1,0:T(8,128)(2,1)}), bf16[1024,4096]{1,0:T(8,128)(2,1)}) %all-gather.23.cloned.1.call-update) | async-done | bytes 8388624 | tf_op jit(solution)/shard_map/all_gather | solution.py:300
  251.3 6.1 fusion.136
  257.3 27.8 %all-gather.25.cloned.1.call-done = bf16[2048,1024]{1,0:T(8,128)(2,1)} async-done(((bf16[256,1024]{1,0:T(8,128)(2,1)}), bf16[2048,1024]{1,0:T(8,128)(2,1)}) %all-gather.25.cloned.1.call-update) | async-done | bytes 4194320 | tf_op jit(solution)/shard_map/all_gather | solution.py:301
  285.2 5.4 multiply_convert_fusion.1
  290.6 3.5 multiply_reduce_fusion.1
  298.8 27.0 %while.98 = (s32[]{:T(128)}, f32[128,2,4,64]{0,3,2,1:T(8,128)S(1)}, f32[2048,128]{0,1:T(8,128)}, f32[2048,128]{0,1:T(8,128)}, s32[]{:T(128)}, /*index=5*/bf16[20...) while((s32[]{:T(128)}, f32[128,2,4,64]{0,3,2,1:T(8,128)S(1)}, ...), condition=%wide.region_24.25_spmd.clone, body=%wide.region_21.24_spmd.clone.sunk | while | flops 339477120 | bytes 13646209 | solution.py:263
  299.6 6.1 conditional.11
  303.8 1.9 constant_dynamic-update-slice_fusion
  306.3 6.1 conditional.11
  310.5 1.9 constant_dynamic-update-slice_fusion
  313.0 6.1 conditional.11
  317.2 1.9 constant_dynamic-update-slice_fusion
  319.7 6.1 conditional.11
  323.9 1.9 constant_dynamic-update-slice_fusion
  328.2 2.1 convert_element_type.378
  330.3 2.0 copy.197
  332.4 4.2 multiply_convert_fusion.5
  340.8 60.0 %reduce-scatter.30.cloned.1.call-done = bf16[128,128]{1,0:T(8,128)(2,1)} async-done(((bf16[2048,128]{1,0:T(8,128)(2,1)}), bf16[128,128]{1,0:T(8,128)(2,1)}) %reduce-scatter.30.cloned.1.call-update) | async-done | bytes 32784
  401.7 74.7 %reduce-scatter.28.cloned.1.call-done = bf16[128,128]{1,0:T(8,128)(2,1)} async-done(((bf16[2048,128]{1,0:T(8,128)(2,1)}), bf16[128,128]{1,0:T(8,128)(2,1)}) %reduce-scatter.28.cloned.1.call-update) | async-done | bytes 32784
  480.0 2.7 convolution_convert_fusion.2
  483.8 3.3 convolution_convert_fusion.3
  488.2 6.8 convolution_convert_fusion.1
  497.8 2.7 convolution_bitcast_fusion.1
  500.6 39.4 %all-gather.29.cloned.1.call-done = bf16[384,64,128]{2,1,0:T(8,128)(2,1)} async-done(((bf16[24,64,128]{2,1,0:T(8,128)(2,1)}), bf16[384,64,128]{2,1,0:T(8,128)(2,1)}) %all-gather.29.cloned.1.call-update) | async-done | bytes 6291472 | tf_op jit(solution)/shard_map/all_gather | solution.py:33
  540.0 30.6 %while.100 = (s32[]{:T(128)}, f32[24,64,128]{2,1,0:T(8,128)S(1)}, s32[]{:T(128)}, bf16[16,24]{1,0:T(8,128)(2,1)}, bf16[16,24,64,128]{3,2,1,0:T(8,128)(2,1)}, /*index=5*/s32[]{:T(128)}, s32[]{:T(128)}, s32[]{:T(128)}, s32[]{:T(128)}) while((s32[]{:T(128)}, f32[24,64,128]{2,1,0:T(8,128)S(1)}, s32[]{:T(128)}, ...), condition=%wide.region_18.19_spmd.clone, body=%wide.region_17.18_spmd.clone.sunk | while | flops 983072 | bytes 1966495 | solution.py:51
  574.5 2.6 fusion.43
  577.1 2.3 copy.166
  579.4 3.8 multiply_reduce_fusion
  588.1 3.5 collective-permute-start.1
  591.7 2.1 collective-permute-done.1
  594.2 4.8 convolution_convert_fusion
  600.3 5.6 reduce-scatter.20.cloned.1.call-done
  606.0 36.7 %reduce-scatter.18.cloned.1.call-done = bf16[192,1024]{1,0:T(8,128)(2,1)} async-done(((bf16[1536,1024]{1,0:T(8,128)(2,1)}), bf16[192,1024]{1,0:T(8,128)(2,1)}) %reduce-scatter.18.cloned.1.call-update) | async-done | bytes 393232 | tf_op jit(solution)/shard_map/reduce_scatter | solution.py:473
  642.7 39.0 %reduce-scatter.26.cloned.1.call-done = bf16[256,1024]{1,0:T(8,128)(2,1)} async-done(((bf16[2048,1024]{1,0:T(8,128)(2,1)}), bf16[256,1024]{1,0:T(8,128)(2,1)}) %reduce-scatter.26.cloned.1.call-update) | async-done | bytes 524304 | tf_op jit(solution)/shard_map/reduce_scatter | solution.py:488
  681.7 54.9 %reduce-scatter.24.cloned.1.call-done = bf16[128,4096]{1,0:T(8,128)(2,1)} async-done(((bf16[1024,4096]{1,0:T(8,128)(2,1)}), bf16[128,4096]{1,0:T(8,128)(2,1)}) %reduce-scatter.24.cloned.1.call-update) | async-done | bytes 1048592 | tf_op jit(solution)/shard_map/reduce_scatter | solution.py:485
  736.5 46.9 %reduce-scatter.16.cloned.1.call-done = bf16[128,3328]{1,0:T(8,128)(2,1)} async-done(((bf16[1024,3328]{1,0:T(8,128)(2,1)}), bf16[128,3328]{1,0:T(8,128)(2,1)}) %reduce-scatter.16.cloned.1.call-update) | async-done | bytes 851984 | tf_op jit(solution)/shard_map/reduce_scatter | solution.py:467
  784.7 3.6 fusion.49
  788.3 5.3 fusion.91
  794.6 13.1 %all-reduce.4 = (bf16[1024]{0:T(1024)(128)(2,1)S(1)}, bf16[1024]{0:T(1024)(128)(2,1)S(1)}) all-reduce(bf16[1024]{0:T(1024)(128)(2,1)S(1)} %get-tuple-element.1157, bf16[1024]{0:T(1024)(128)(2,1)S(1)} %copy-done.70), channel_id=6, replica_groups=mesh['ctx'=16,'fsdp'=8] {'fsdp'}, use_global_device_ids=true, to_apply=%region_29.30.clone | all-reduce | flops 2048 | bytes 8192
  808.9 7.3 reduce-scatter.32.cloned.1.call-done
  817.0 34.0 %all-reduce.2 = (bf16[128]{0:T(256)(128)(2,1)S(1)}, bf16[224,4]{0,1:T(4,128)(2,1)S(1)}, bf16[128]{0:T(256)(128)(2,1)S(1)}) all-reduce(bf16[128]{0:T(256)(128)(2,1)S(1)} %dynamic-slice.4, bf16[224,4]{0,1:T(4,128)(2,1)S(1)} %copy.202, bf16[128]{0:T(256)(128)(2,1)S(1)} %dynamic-slice.6), channel_id=1, replica_groups=mesh['ctx'=16,'fsdp'=8] {'ctx'}, use_global_device_ids=true, to_apply=%region_30.31 | all-reduce | flops 1152 | bytes 4608 | tf_op jit(solution)/shard_map/psum | solution.py:493
  852.7 65.5 %all-reduce.7.cloned.1.call-done = (bf16[128,3328]{1,0:T(8,128)(2,1)}, bf16[192,1024]{1,0:T(8,128)(2,1)}, bf16[128,768]{1,0:T(8,128)(2,1)}, bf16[64,1024]{1,0:T(...) async-done(((bf16[128,3328]{1,0:T(8,128)(2,1)}, bf16[192,1024]{1,0:T(8,128)(2,1)}, bf16[128,768]{1,0:T(8,128)(2,1)}, bf16[64,1024]{1,0:T(8,128)(2,1)}, ...) | async-done | bytes 3145744 | tf_op jit(solution)/shard_map/psum | solution.py:494
  918.1 2.6 convert_element_type.384
  (486 shorter events, 147.6 us)
Async XLA Ops:
  7.2 46.8 %copy-start.1 = (bf16[1,128,1024]{2,1,0:T(8,128)(2,1)S(1)}, bf16[1,128,1024]{2,1,0:T(8,128)(2,1)}, u32[]{:S(2)}) copy-start(bf16[1,128,1024]{2,1,0:T(8,128)(2,1)} %param.29) | copy-start | bytes 786436
  7.2 46.8 %all-gather.19.cloned.1.call-start = ((), (), s32[]{:S(2)}) async-start(), calls=%async_computation.11 | async-start | bytes 7667712 | tf_op jit(solution)/shard_map/all_gather | solution.py:294
  7.9 93.8 %all-gather.15.cloned.1.call-start = ((), (), s32[]{:S(2)}) async-start(), calls=%async_computation.9 | async-start | bytes 1769472 | tf_op jit(solution)/shard_map/all_gather | solution.py:297
  8.7 166.5 %all-gather.17.cloned.1.call-start = ((), (), s32[]{:S(2)}) async-start(), calls=%async_computation.10 | async-start | bytes 1179648 | tf_op jit(solution)/shard_map/all_gather | solution.py:298
  9.4 173.1 %all-gather.27.cloned.1.call-start = ((), (), s32[]{:S(2)}) async-start(), calls=%async_computation.21 | async-start | bytes 6684672 | tf_op jit(solution)/shard_map/all_gather | solution.py:33
  11.3 48.0 %copy-start.54 = (f32[128,24]{0,1:T(8,128)}, f32[128,24]{0,1:T(8,128)S(1)}, u32[]{:S(2)}) copy-start(f32[128,24]{0,1:T(8,128)S(1)} %log_bitcast_fusion) | copy-start | bytes 36868
  24.2 77.6 %copy-start.59 = (f32[128]{0:T(128)}, f32[128]{0:T(128)S(1)}, u32[]{:S(2)}) copy-start(f32[128]{0:T(128)S(1)} %add_rsqrt_fusion.1) | copy-start | bytes 1540
  33.4 25.9 %copy-start.29 = (f32[1,128,24]{2,1,0:T(8,128)}, f32[1,128,24]{2,1,0:T(8,128)S(1)}, u32[]{:S(2)}) copy-start(f32[1,128,24]{2,1,0:T(8,128)S(1)} %copy.146) | copy-start | bytes 36868
  59.2 10.8 %copy-start.13 = (bf16[128,3328]{1,0:T(8,128)(2,1)}, bf16[128,3328]{1,0:T(8,128)(2,1)S(1)}, u32[]{:S(2)}) copy-start(bf16[128,3328]{1,0:T(8,128)(2,1)S(1)} %get-tuple-element.1280) | copy-start | bytes 2555908
  59.3 7.7 collective-permute-start
  62.8 7.3 copy-start.45
  62.8 7.3 copy-start.47
  62.8 7.3 copy-start.49
  62.9 4.7 copy-start.11
  67.0 4.4 copy-start.56
  67.6 270.2 %copy-start.2 = (bf16[128,1792]{1,0:T(8,128)(2,1)}, bf16[128,1792]{1,0:T(8,128)(2,1)S(1)}, u32[]{:S(2)}) copy-start(bf16[128,1792]{1,0:T(8,128)(2,1)S(1)} %get-tuple-element.1251) | copy-start | bytes 1376260
  70.1 22.2 %copy-start.74 = (bf16[128]{0:T(256)(128)(2,1)S(1)}, bf16[128]{0:T(256)(128)(2,1)}, u32[]{:S(2)}) copy-start(bf16[128]{0:T(256)(128)(2,1)} %param.36) | copy-start | bytes 772
  71.4 137.3 %all-gather.21.cloned.1.call-start = ((), (), s32[]{:S(2)}) async-start(), calls=%async_computation.12 | async-start | bytes 3538944 | tf_op jit(solution)/shard_map/all_gather | solution.py:296
  72.0 179.3 %all-gather.23.cloned.1.call-start = ((), (), s32[]{:S(2)}) async-start(), calls=%async_computation.13 | async-start | bytes 9437184 | tf_op jit(solution)/shard_map/all_gather | solution.py:300
  72.5 212.6 %all-gather.25.cloned.1.call-start = ((), (), s32[]{:S(2)}) async-start(), calls=%async_computation.14 | async-start | bytes 4718592 | tf_op jit(solution)/shard_map/all_gather | solution.py:301
  73.3 327.5 %reduce-scatter.30.cloned.1.call-start = ((), (), s32[]{:S(2)}) async-start(), calls=%async_computation.24 | async-start | bytes 557056
  74.0 104.6 %copy-start.65 = (pred[128,128]{1,0:T(8,128)(4,1)}, pred[128,128]{1,0:T(8,128)(4,1)S(1)}, u32[]{:S(2)}) copy-start(pred[128,128]{1,0:T(8,128)(4,1)S(1)} %iota_compare_fusion) | copy-start | bytes 49156
  92.2 245.6 %copy-start.35 = (f32[128,24]{0,1:T(8,128)}, f32[128,24]{0,1:T(8,128)S(1)}, u32[]{:S(2)}) copy-start(f32[128,24]{0,1:T(8,128)S(1)} %copy.149) | copy-start | bytes 36868
  101.7 239.0 %copy-start.33 = (f32[128,32]{0,1:T(8,128)}, f32[128,32]{0,1:T(8,128)S(1)}, u32[]{:S(2)}) copy-start(f32[128,32]{0,1:T(8,128)S(1)} %get-tuple-element.1279) | copy-start | bytes 49156
  101.7 239.0 %copy-start.44 = (f32[128,32]{0,1:T(8,128)}, f32[128,32]{0,1:T(8,128)S(1)}, u32[]{:S(2)}) copy-start(f32[128,32]{0,1:T(8,128)S(1)} %get-tuple-element.1277) | copy-start | bytes 49156
  175.1 7.4 copy-start.21
  202.2 4.8 copy-start.71
  211.5 82.7 %copy-start.62 = (f32[128]{0:T(128)}, f32[128]{0:T(128)S(1)}, u32[]{:S(2)}) copy-start(f32[128]{0:T(128)S(1)} %add_rsqrt_fusion) | copy-start | bytes 1540
  251.3 33.9 %copy-start.19 = (bf16[1,128,1024]{2,1,0:T(8,128)(2,1)S(1)}, bf16[1,128,1024]{2,1,0:T(8,128)(2,1)}, u32[]{:S(2)}) copy-start(bf16[1,128,1024]{2,1,0:T(8,128)(2,1)} %param.41) | copy-start | bytes 786436
  285.2 5.4 copy-start
  290.6 4.4 copy-start.10
  328.1 4.3 copy-start.17
  328.1 148.3 %reduce-scatter.28.cloned.1.call-start = ((), (), s32[]{:S(2)}) async-start(), calls=%async_computation.23 | async-start | bytes 557056
  332.4 207.6 %all-gather.29.cloned.1.call-start = ((), (), s32[]{:S(2)}) async-start(), calls=%async_computation.22 | async-start | bytes 6684672 | tf_op jit(solution)/shard_map/all_gather | solution.py:33
  339.1 138.9 %copy-start.60 = (f32[128]{0:T(128)S(1)}, f32[128]{0:T(128)}, u32[]{:S(2)}) copy-start(f32[128]{0:T(128)} %copy-done.59) | copy-start | bytes 1540
  339.1 261.2 %reduce-scatter.22.cloned.1.call-start = ((), (), s32[]{:S(2)}) async-start(), calls=%async_computation.18 | async-start | bytes 1179648 | tf_op jit(solution)/shard_map/reduce_scatter | solution.py:479
  340.6 265.4 %reduce-scatter.20.cloned.1.call-start = ((), (), s32[]{:S(2)}) async-start(), calls=%async_computation.17 | async-start | bytes 1769472 | tf_op jit(solution)/shard_map/reduce_scatter | solution.py:476
  340.7 139.2 %copy-start.16 = (bf16[128,1536]{1,0:T(8,128)(2,1)S(1)}, bf16[128,1536]{1,0:T(8,128)(2,1)}, u32[]{:S(2)}) copy-start(bf16[128,1536]{1,0:T(8,128)(2,1)} %copy-done.15) | copy-start | bytes 1179652
  401.7 78.3 %copy-start.36 = (bf16[128,128]{0,1:T(8,128)(2,1)}, bf16[128,128]{0,1:T(8,128)(2,1)S(1)}, u32[]{:S(2)}) copy-start(bf16[128,128]{0,1:T(8,128)(2,1)S(1)} %copy.200) | copy-start | bytes 98308
  479.9 162.7 %reduce-scatter.18.cloned.1.call-start = ((), (), s32[]{:S(2)}) async-start(), calls=%async_computation.16 | async-start | bytes 3538944 | tf_op jit(solution)/shard_map/reduce_scatter | solution.py:473
  482.7 198.9 %reduce-scatter.26.cloned.1.call-start = ((), (), s32[]{:S(2)}) async-start(), calls=%async_computation.20 | async-start | bytes 4718592 | tf_op jit(solution)/shard_map/reduce_scatter | solution.py:488
  487.1 249.4 %reduce-scatter.24.cloned.1.call-start = ((), (), s32[]{:S(2)}) async-start(), calls=%async_computation.19 | async-start | bytes 9437184 | tf_op jit(solution)/shard_map/reduce_scatter | solution.py:485
  495.0 288.5 %reduce-scatter.16.cloned.1.call-start = ((), (), s32[]{:S(2)}) async-start(), calls=%async_computation.15 | async-start | bytes 7667712 | tf_op jit(solution)/shard_map/reduce_scatter | solution.py:467
  540.0 30.6 %copy-start.30 = (f32[1,128,24]{2,1,0:T(8,128)S(1)}, f32[1,128,24]{2,1,0:T(8,128)}, u32[]{:S(2)}) copy-start(f32[1,128,24]{2,1,0:T(8,128)} %copy-done.29) | copy-start | bytes 36868
  540.0 30.7 %copy-start.55 = (f32[128,24]{0,1:T(8,128)S(1)}, f32[128,24]{0,1:T(8,128)}, u32[]{:S(2)}) copy-start(f32[128,24]{0,1:T(8,128)} %copy-done.54) | copy-start | bytes 36868
  540.0 32.5 %copy-start.27 = (f32[128,128]{1,0:T(8,128)S(1)}, f32[128,128]{1,0:T(8,128)}, u32[]{:S(2)}) copy-start(f32[128,128]{1,0:T(8,128)} %slice.167) | copy-start | bytes 196612
  540.0 32.5 %copy-start.40 = (bf16[128,128]{1,0:T(8,128)(2,1)S(1)}, bf16[128,128]{1,0:T(8,128)(2,1)}, u32[]{:S(2)}) copy-start(bf16[128,128]{1,0:T(8,128)(2,1)} %slice.166) | copy-start | bytes 98308
  540.0 32.6 %copy-start.66 = (pred[128,128]{1,0:T(8,128)(4,1)S(1)}, pred[128,128]{1,0:T(8,128)(4,1)}, u32[]{:S(2)}) copy-start(pred[128,128]{1,0:T(8,128)(4,1)} %copy-done.65) | copy-start | bytes 49156
  574.5 4.9 copy-start.4
  586.7 7.5 copy-start.25
  586.7 7.5 copy-start.61
  588.1 5.6 collective-permute-start.1
  599.0 217.1 %reduce-scatter.32.cloned.1.call-start = ((), (), s32[]{:S(2)}) async-start(), calls=%async_computation.25 | async-start | bytes 516096
  599.1 184.4 %copy-start.75 = (u32[128]{0:T(128)S(1)}, u32[128]{0:T(128)}, u32[]{:S(2)}) copy-start(u32[128]{0:T(128)} %constant.252) | copy-start | bytes 1540
  599.1 185.6 %copy-start.9 = (bf16[128,2048]{1,0:T(8,128)(2,1)S(1)}, bf16[128,2048]{1,0:T(8,128)(2,1)}, u32[]{:S(2)}) copy-start(bf16[128,2048]{1,0:T(8,128)(2,1)} %get-tuple-element.1262) | copy-start | bytes 1572868
  600.3 317.9 %all-reduce.7.cloned.1.call-start = ((), (), s32[]{:S(2)}) async-start(), calls=%async_computation.26 | async-start | bytes 6291456 | tf_op jit(solution)/shard_map/psum | solution.py:494
  788.3 5.4 copy-start.5
  788.3 5.4 copy-start.37
  788.3 5.4 copy-start.39
  793.7 14.1 %copy-start.7 = (f32[128,1024]{1,0:T(8,128)S(1)}, f32[128,1024]{1,0:T(8,128)}, u32[]{:S(2)}) copy-start(f32[128,1024]{1,0:T(8,128)} %copy-done.6) | copy-start | bytes 1572868
  793.7 14.0 %copy-start.64 = (f32[128]{0:T(128)S(1)}, f32[128]{0:T(128)}, u32[]{:S(2)}) copy-start(f32[128]{0:T(128)} %copy-done.62) | copy-start | bytes 1540
  793.7 14.0 %copy-start.73 = (f32[128]{0:T(128)S(1)}, f32[128]{0:T(128)}, u32[]{:S(2)}) copy-start(f32[128]{0:T(128)} %copy-done.72) | copy-start | bytes 1540
  918.1 4.3 copy-start.51
  918.1 5.1 copy-start.26
  (32 other events, 79.4 us)
Sparse Core Ops, SparseCore 0:
  9.7 44.2 all-gather.18
  55.7 23.9 all-gather.14
  81.4 23.5 all-gather.16
  107.5 63.9 all-gather.26
  173.1 26.5 all-gather.20
  201.3 49.9 all-gather.22
  253.0 32.1 all-gather.24
  328.2 72.5 reduce-scatter.29
  404.9 71.4 reduce-scatter.27
  479.0 60.9 all-gather.28
  542.9 28.6 reduce-scatter.21
  574.4 31.4 reduce-scatter.19
  608.4 34.2 reduce-scatter.17
  644.9 36.7 reduce-scatter.25
  683.9 52.5 reduce-scatter.23
  738.8 44.5 reduce-scatter.15
  786.2 29.8 reduce-scatter.31
  820.6 97.5 all-reduce.6
where the time goes:
time: 943 us; the launch traced here: 933 us
  waiting for transfers between devices  528 us (56%)
  blocking collectives  144 us (15%)
  matrix products  105 us (11%)
  other arithmetic  83.2 us (9%)
  local copies, waits for them, and re-layouts  37.7 us (4%)
  between operations  16.4 us (2%)
  loops' own time  10.3 us (1%)
    unnamed x21, waiting for transfers between devices  146 us
    psum x1, waiting for transfers between devices, on_device(): lax.psum(partials[1].astype(jnp.bfloat16), 'ctx').astype(jnp.float32)  65.5 us
    reduce_scatter x1, waiting for transfers between devices, on_device(): lax.psum_scatter(grad_gu.astype(jnp.bfloat16), 'fsdp', scatter_dimension=...  54.9 us
    reduce_scatter x1, waiting for transfers between devices, on_device(): lax.psum_scatter(grad_min.astype(jnp.bfloat16), 'fsdp', scatter_dimension...  46.9 us
    all_gather x1, waiting for transfers between devices, on_device(): lax.all_gather(w_gate_up, 'fsdp', axis=0, tiled=True)  39.8 us
    all_gather x2, waiting for transfers between devices, prefix(): lax.all_gather(part.astype(kind), axis)  39.4 us
    reduce_scatter x1, waiting for transfers between devices, on_device(): lax.psum_scatter(grad_dn.astype(jnp.bfloat16), 'fsdp', scatter_dimension=...  39 us
    select_n x32, other arithmetic, hop(): return jax.tree.map(lambda a, b: jnp.where(reached, a, b), new, before)  37.9 us
  transfers between devices with their start and end apart: 20, of which 15 were waited for; matrix products, arithmetic and copies ran while one was open for 19% of the time, Pallas kernels for 0%

commit v1 on v0

v1 whole, which is shorter than its diff:
```python
import functools

import jax
import jax.numpy as jnp
from jax import lax
from jax.experimental import pallas as pl
from jax.experimental.pallas import tpu as pltpu
from jax.sharding import PartitionSpec as P

D = 1024
QH = 8
KH = 2
HD = 64
MIXER_HEADS = 24
MP = 64
NS = 128
CONV = 4
FF = 2048
SSD_BLOCK = 128
KEY_BLOCK = 512
MI = MIXER_HEADS * MP
XBC = MI + 2 * NS
Q_WIDTH = QH * HD
KV_WIDTH = KH * HD
CTX = 16
OWNERS = 8
HALO = 8
STATE_ROWS = MI // CTX

epsilon = 1e-05
rope_base = 10000.0
masked_value = -1e30
highest = lax.Precision.HIGHEST
bf16 = jnp.bfloat16
f32 = jnp.float32


def passed_along(value, axis, steps):
    count = lax.axis_size(axis)
    leading, last = (max(0, -steps), min(count, count - steps))
    return lax.ppermute(value, axis, [(source, source + steps) for source in range(leading, last)])


def swap(value, axis):
    return lax.all_to_all(value, axis, 0, 0, tiled=True)


def silu(entries):
    return entries * jax.nn.sigmoid(entries)


def silu_slope(entries):
    logistic = jax.nn.sigmoid(entries)
    return logistic * (1.0 + entries * (1.0 - logistic))


def rotate(values, positions, direction):
    half_dim = HD // 2
    frequency = jnp.exp(-jnp.log(rope_base) * (2.0 * jnp.arange(half_dim).astype(jnp.float32) / HD))
    angles = positions[:, None] * frequency[None, :]
    cosine = jnp.cos(angles)[:, None, :]
    sine_part = jnp.sin(angles)[:, None, :]
    front_half = values[..., :half_dim]
    back_half = values[..., half_dim:]
    return jnp.concatenate(
        [
            front_half * cosine - direction * back_half * sine_part,
            back_half * cosine + direction * front_half * sine_part,
        ],
        axis=-1,
    )


def ssd_local(inputs_x, input_b, input_c, gate_vals, cumulative):
    length = cumulative.shape[0]
    row_ids = lax.broadcasted_iota(jnp.int32, (length, length), 0)
    col_ids = lax.broadcasted_iota(jnp.int32, (length, length), 1)
    causal = (col_ids <= row_ids)[None]
    spread = cumulative.T[:, :, None] - cumulative.T[:, None, :]
    weights = jnp.where(causal, jnp.exp(jnp.where(causal, spread, 0.0)), 0.0)
    products_cb = jnp.dot(
        input_c.astype(jnp.bfloat16),
        input_b.T.astype(jnp.bfloat16),
        preferred_element_type=jnp.float32,
    )
    mixing = weights * products_cb[None] * gate_vals.T[:, None, :]
    outputs = jnp.einsum("hts,shp->thp", mixing, inputs_x, precision=highest)
    remain = jnp.exp(cumulative[-1][None, :] - cumulative) * gate_vals
    new_state = jnp.einsum("sh,shp,sn->hpn", remain, inputs_x, input_b, precision=highest)
    return (outputs, new_state)


def rms_back(grad_normed, normed, inverse, gain):
    scaled = grad_normed * gain
    return inverse * (scaled - normed * jnp.mean(scaled * normed, axis=-1, keepdims=True))


def block_scores(grouped_q, query_pos, block_idx, key_block):
    scores = jnp.einsum(
        "tgrd,kgd->grtk",
        grouped_q,
        key_block.reshape(KEY_BLOCK, KH, HD),
        preferred_element_type=jnp.float32,
    ) * HD ** (-0.5)
    key_pos = block_idx * KEY_BLOCK + jnp.arange(KEY_BLOCK)
    allowed = key_pos[None, :] <= query_pos[:, None]
    return jnp.where(allowed, scores, masked_value)


def forward_attend(grouped_q, query_pos, key_all, value_all):
    rows = grouped_q.shape[0]
    group_size = QH // KH
    last_row = jnp.max(query_pos)
    block_count = key_all.shape[0] // KEY_BLOCK

    def total_step(block_idx, carried):

        def total_update(state_pair):
            row_max, row_sum = state_pair
            key_block = lax.dynamic_slice_in_dim(key_all, block_idx * KEY_BLOCK, KEY_BLOCK, 0)
            scores = block_scores(grouped_q, query_pos, block_idx, key_block)
            new_max = jnp.maximum(row_max, jnp.max(scores, axis=-1))
            new_sum = row_sum * jnp.exp(row_max - new_max) + jnp.sum(
                jnp.exp(scores - new_max[..., None]), axis=-1
            )
            return (new_max, new_sum)

        return lax.cond(
            block_idx * KEY_BLOCK <= last_row, total_update, lambda unchanged: unchanged, carried
        )

    start_pair = (
        jnp.full((KH, group_size, rows), masked_value, jnp.float32),
        jnp.zeros((KH, group_size, rows), jnp.float32),
    )
    row_max, row_sum = lax.fori_loop(0, block_count, total_step, start_pair)
    log_total = row_max + jnp.log(row_sum)

    def mix_step(block_idx, totals):

        def mix_update(running):
            key_block = lax.dynamic_slice_in_dim(key_all, block_idx * KEY_BLOCK, KEY_BLOCK, 0)
            value_block = lax.dynamic_slice_in_dim(value_all, block_idx * KEY_BLOCK, KEY_BLOCK, 0)
            scores = block_scores(grouped_q, query_pos, block_idx, key_block)
            probabilities = jnp.exp(scores - log_total[..., None]).astype(jnp.bfloat16)
            return running + jnp.einsum(
                "grtk,kgd->tgrd",
                probabilities,
                value_block.reshape(KEY_BLOCK, KH, HD),
                preferred_element_type=jnp.float32,
            )

        return lax.cond(
            block_idx * KEY_BLOCK <= last_row, mix_update, lambda unchanged: unchanged, totals
        )

    mixer_output = lax.fori_loop(
        0, block_count, mix_step, jnp.zeros((rows, KH, group_size, HD), jnp.float32)
    )
    return (log_total, mixer_output)


def backward_attend(
    grouped_q,
    mixer_gradient,
    mixer_output,
    log_total,
    query_pos,
    key_all,
    value_all,
    grad_keys,
    grad_values,
):
    rows = grouped_q.shape[0]
    group_size = QH // KH
    kv_width = KH * HD
    last_row = jnp.max(query_pos)
    block_count = key_all.shape[0] // KEY_BLOCK
    row_difference = jnp.einsum("apoz,apoz->poa", mixer_gradient.astype(jnp.float32), mixer_output)

    def back_step(block_idx, carried):

        def back_update(triple):
            grad_query, keys_sum, values_sum = triple
            start = block_idx * KEY_BLOCK
            key_block = lax.dynamic_slice_in_dim(key_all, start, KEY_BLOCK, 0)
            value_block = lax.dynamic_slice_in_dim(value_all, start, KEY_BLOCK, 0)
            probabilities = jnp.exp(
                block_scores(grouped_q, query_pos, block_idx, key_block) - log_total[..., None]
            )
            rounded = probabilities.astype(jnp.bfloat16)
            grad_probs = jnp.einsum(
                "tgrd,kgd->grtk",
                mixer_gradient,
                value_block.reshape(KEY_BLOCK, KH, HD),
                preferred_element_type=jnp.float32,
            )
            grad_scores = (probabilities * (grad_probs - row_difference[..., None])).astype(
                jnp.bfloat16
            )
            grad_query = grad_query + jnp.einsum(
                "grtk,kgd->tgrd",
                grad_scores,
                key_block.reshape(KEY_BLOCK, KH, HD),
                preferred_element_type=jnp.float32,
            )
            key_part = jnp.einsum(
                "grtk,tgrd->kgd", grad_scores, grouped_q, preferred_element_type=jnp.float32
            ).reshape(KEY_BLOCK, kv_width)
            value_part = jnp.einsum(
                "grtk,tgrd->kgd", rounded, mixer_gradient, preferred_element_type=jnp.float32
            ).reshape(KEY_BLOCK, kv_width)
            keys_sum = lax.dynamic_update_slice_in_dim(
                keys_sum,
                lax.dynamic_slice_in_dim(keys_sum, start, KEY_BLOCK, 0) + key_part,
                start,
                0,
            )
            values_sum = lax.dynamic_update_slice_in_dim(
                values_sum,
                lax.dynamic_slice_in_dim(values_sum, start, KEY_BLOCK, 0) + value_part,
                start,
                0,
            )
            return (grad_query, keys_sum, values_sum)

        return lax.cond(
            block_idx * KEY_BLOCK <= last_row, back_update, lambda unchanged: unchanged, carried
        )

    start_triple = (jnp.zeros((rows, KH, group_size, HD), jnp.float32), grad_keys, grad_values)
    return lax.fori_loop(0, block_count, back_step, start_triple)


def whole(shape):
    return pl.BlockSpec(shape, lambda *_: (0,) * len(shape))


def params():
    return pltpu.CompilerParams(vmem_limit_bytes=48 * 1024 * 1024)


def cross(left, right):
    return lax.dot_general(left, right, (((0,), (0,)), ((), ())), preferred_element_type=f32)


def prefix_kernel(reverse, parts_ref, decay_ref, out_ref):
    running = jnp.zeros(out_ref.shape[1:], f32)
    for at in range(CTX - 1, -1, -1) if reverse else range(CTX):
        out_ref[at] = running.astype(bf16)
        running = decay_ref[at] * running + parts_ref[at].astype(f32)


def prefix(parts, decay_rows, reverse):
    shape = (CTX, STATE_ROWS, NS)
    return pl.pallas_call(
        functools.partial(prefix_kernel, reverse),
        out_shape=jax.ShapeDtypeStruct(shape, bf16),
        compiler_params=params(),
        name="state_prefix",
    )(parts, decay_rows)


def ffn_grads_kernel(hidden_ref, grad_out_ref, second_ref, grad_gu_ref, out_ref):
    rows = hidden_ref.shape[1]
    out_ref[0, :rows] = cross(hidden_ref[...], grad_out_ref[...]).astype(bf16)
    for block in range(4):
        cols = slice(D * block, D * (block + 1))
        part = cross(second_ref[...], grad_gu_ref[:, cols]).astype(bf16)
        out_ref[0, rows + 128 * block : rows + 128 * (block + 1)] = part


def ffn_grads(hidden_act, grad_out, second, grad_gu):
    rows = hidden_act.shape[0]
    return pl.pallas_call(
        ffn_grads_kernel,
        grid=(OWNERS,),
        in_specs=[
            pl.BlockSpec((rows, FF // OWNERS), lambda f: (0, f)),
            whole((rows, D)),
            pl.BlockSpec((rows, D // OWNERS), lambda f: (0, f)),
            whole((rows, 2 * FF)),
        ],
        out_specs=pl.BlockSpec((1, 768, D), lambda f: (f, 0, 0)),
        out_shape=jax.ShapeDtypeStruct((OWNERS, 768, D), bf16),
        compiler_params=params(),
        name="ffn_grads",
    )(hidden_act, grad_out, second, grad_gu)


def mix_grads_kernel(mamba_ref, attended_ref, branch_ref, shared_ref, grad_m_ref, grad_a_ref, out_ref):
    mamba = cross(mamba_ref[...], branch_ref[...]).astype(bf16)
    attended = cross(attended_ref[...], branch_ref[...]).astype(bf16)
    for owner in range(2):
        out_ref[owner, :192] = mamba[192 * owner : 192 * (owner + 1)]
        out_ref[owner, 192:256] = attended[64 * owner : 64 * (owner + 1)]
        held = shared_ref[:, 128 * owner : 128 * (owner + 1)]
        for block in range(3):
            cols = slice(D * block, D * (block + 1))
            part = cross(held, grad_m_ref[:, cols]).astype(bf16)
            out_ref[owner, 256 + 128 * block : 384 + 128 * block] = part
        out_ref[owner, 640:768, :256] = cross(held, grad_m_ref[:, 3072:3328]).astype(bf16)
        out_ref[owner, 640:768, 256:] = cross(held, grad_a_ref[...]).astype(bf16)


def mix_grads(mamba_in, attended, branch_grad, shared, grad_m, grad_a):
    rows = mamba_in.shape[0]
    return pl.pallas_call(
        mix_grads_kernel,
        grid=(OWNERS // 2,),
        in_specs=[
            pl.BlockSpec((rows, 384), lambda f: (0, f)),
            pl.BlockSpec((rows, 128), lambda f: (0, f)),
            whole((rows, D)),
            pl.BlockSpec((rows, 256), lambda f: (0, f)),
            whole((rows, MI + XBC)),
            whole((rows, 768)),
        ],
        out_specs=pl.BlockSpec((2, 768, D), lambda f: (f, 0, 0)),
        out_shape=jax.ShapeDtypeStruct((OWNERS, 768, D), bf16),
        compiler_params=params(),
        name="mix_grads",
    )(mamba_in, attended, branch_grad, shared, grad_m, grad_a)


def ctx_sum(chunks):
    got = swap(chunks, "ctx")
    mine = jnp.sum(got.astype(f32), axis=0).astype(bf16)
    return swap(jnp.broadcast_to(mine[None], chunks.shape), "ctx")


def on_device(
    tokens,
    gain_one,
    w_mamba_in,
    conv_weight,
    w_mamba_out,
    w_qkv,
    w_attn_out,
    gain_two,
    w_gate_up,
    w_down,
    decays,
    input_gates,
    grad_out,
):
    tokens = tokens[0]
    decays = decays[0]
    input_gates = input_gates[0]
    grad_out = grad_out[0]
    tok_rows = tokens.shape[0]
    group_size = QH // KH
    score_scale = HD ** (-0.5)
    ctx_index = lax.axis_index("ctx")
    offset = ctx_index * tok_rows

    first_weights = lax.all_gather(
        jnp.concatenate([w_mamba_in, w_qkv], axis=1), "fsdp", axis=0, tiled=True
    )
    rest = jnp.concatenate(
        [w_mamba_out, w_attn_out, w_down]
        + [w_gate_up[:, D * block : D * (block + 1)] for block in range(4)],
        axis=0,
    )
    rest_weights = lax.all_gather(rest, "fsdp", axis=0, tiled=False)
    small = jnp.concatenate([gain_one, gain_two, conv_weight.T.reshape(-1)])
    small_all = lax.all_gather(small[None], "fsdp", axis=0, tiled=True)
    gain_first = small_all[:, :128].reshape(D).astype(f32)
    gain_second = small_all[:, 128:256].reshape(D).astype(f32)
    conv_taps = small_all[:, 256:].reshape(OWNERS, CONV, XBC // OWNERS).transpose(1, 0, 2)
    conv_taps = conv_taps.reshape(CONV, XBC).astype(f32)

    log_decay = jnp.log(decays)
    cumulative = jnp.cumsum(log_decay, axis=0)
    whole_decay = jnp.exp(cumulative[-1])
    reach_decay = jnp.exp(cumulative)
    decays_all = lax.all_gather(whole_decay[None], "ctx", axis=0, tiled=True)
    decay_rows = lax.dynamic_slice_in_dim(
        jnp.repeat(decays_all, MP, axis=1), ctx_index * STATE_ROWS, STATE_ROWS, 1
    )[:, :, None]

    halo = passed_along(tokens[tok_rows - HALO :], "ctx", 1)
    hidden_ext = jnp.concatenate([halo, tokens], axis=0).astype(f32)
    inverse_ext = lax.rsqrt(jnp.mean(hidden_ext * hidden_ext, axis=-1, keepdims=True) + epsilon)
    normed_ext = hidden_ext * inverse_ext
    shared_ext = (normed_ext * gain_first).astype(bf16)
    hidden_in, inverse_one = hidden_ext[HALO:], inverse_ext[HALO:]
    normed, shared = normed_ext[HALO:], shared_ext[HALO:]

    projected = jnp.dot(shared_ext, first_weights, preferred_element_type=f32)
    gating = projected[HALO:, :MI]
    padded = projected[HALO - (CONV - 1) :, MI : MI + XBC].astype(bf16)
    projections = projected[HALO:, MI + XBC :]

    conv_out = jnp.zeros((tok_rows, XBC), f32)
    for tap_index in range(CONV):
        conv_out = conv_out + padded[tap_index : tap_index + tok_rows].astype(f32) * conv_taps[tap_index][None, :]
    activated = silu(conv_out).astype(bf16).astype(f32)
    inputs_x = activated[:, :MI].reshape(tok_rows, MIXER_HEADS, MP)
    input_b = activated[:, MI : MI + NS]
    input_c = activated[:, MI + NS :]

    def local_states(part_x, part_b, part_c):
        return ssd_local(part_x, part_b, part_c, input_gates, cumulative)

    (local_out, local_end), pull_states = jax.vjp(local_states, inputs_x, input_b, input_c)

    positions = (offset + jnp.arange(tok_rows)).astype(f32)
    queries = rotate(projections[:, :Q_WIDTH].reshape(tok_rows, QH, HD), positions, 1.0).astype(bf16)
    key_local = rotate(
        projections[:, Q_WIDTH : Q_WIDTH + KV_WIDTH].reshape(tok_rows, KH, HD), positions, 1.0
    )
    key_local = key_local.astype(bf16).reshape(tok_rows, KV_WIDTH)
    value_local = projections[:, Q_WIDTH + KV_WIDTH :].astype(bf16)

    key_value = jnp.concatenate([key_local, value_local], axis=0)
    sent = jnp.concatenate(
        [
            local_end.astype(bf16).reshape(CTX, STATE_ROWS, NS),
            jnp.broadcast_to(key_value[None], (CTX, 2 * tok_rows, KV_WIDTH)),
        ],
        axis=1,
    )
    got = swap(sent, "ctx")
    starts = swap(prefix(got[:, :STATE_ROWS], decay_rows, False), "ctx")
    start_state = starts.reshape(MIXER_HEADS, MP, NS).astype(f32)
    key_all = got[:, STATE_ROWS : STATE_ROWS + tok_rows].reshape(CTX * tok_rows, KV_WIDTH)
    value_all = got[:, STATE_ROWS + tok_rows :].reshape(CTX * tok_rows, KV_WIDTH)

    ssd_out = local_out + reach_decay[:, :, None] * jnp.einsum(
        "hpn,tn->thp", start_state, input_c, precision=highest
    )
    ssd_flat = ssd_out.reshape(tok_rows, MI)
    gate_act = silu(gating)
    mamba_in = (ssd_flat * gate_act).astype(bf16)

    grouped = queries.reshape(tok_rows, KH, group_size, HD)
    query_pos = offset + jnp.arange(tok_rows)
    log_total, mixer_output = forward_attend(grouped, query_pos, key_all, value_all)
    attended = mixer_output.reshape(tok_rows, Q_WIDTH).astype(bf16)

    w_mout = rest_weights[:, :192].reshape(MI, D)
    w_aout = rest_weights[:, 192:256].reshape(Q_WIDTH, D)
    w_dn = rest_weights[:, 256:512].reshape(FF, D)
    w_gu = [
        rest_weights[:, 512 + 128 * block : 640 + 128 * block].reshape(D, D) for block in range(4)
    ]
    mamba_out = jnp.dot(mamba_in, w_mout, preferred_element_type=f32)
    attn_out = jnp.dot(attended, w_aout, preferred_element_type=f32)
    residual = hidden_in + attn_out + mamba_out
    inverse_two = lax.rsqrt(jnp.mean(residual * residual, axis=-1, keepdims=True) + epsilon)
    normed_two = residual * inverse_two
    second = (normed_two * gain_second).astype(bf16)
    gate_up = [jnp.dot(second, block, preferred_element_type=f32) for block in w_gu]
    gate_part = jnp.concatenate(gate_up[:2], axis=1)
    up_part = jnp.concatenate(gate_up[2:], axis=1)
    hidden_act = (silu(gate_part) * up_part).astype(bf16)
    result = residual + jnp.dot(hidden_act, w_dn, preferred_element_type=f32)
    output = result.astype(bf16)

    grad_hidden = jnp.einsum("td,fd->tf", grad_out, w_dn, preferred_element_type=f32)
    grad_gu = jnp.concatenate(
        [grad_hidden * up_part * silu_slope(gate_part), grad_hidden * silu(gate_part)], axis=1
    ).astype(bf16)
    first_share = lax.psum_scatter(
        ffn_grads(hidden_act, grad_out, second, grad_gu), "fsdp", scatter_dimension=0, tiled=True
    )[0]
    grad_second = sum(
        jnp.einsum(
            "tf,df->td",
            grad_gu[:, D * block : D * (block + 1)],
            w_gu[block],
            preferred_element_type=f32,
        )
        for block in range(4)
    )
    grad_g_two = jnp.sum(grad_second * normed_two, axis=0)
    grad_residual = grad_out.astype(f32) + rms_back(
        grad_second, normed_two, inverse_two, gain_second
    )
    branch_grad = grad_residual.astype(bf16)
    grad_attended = jnp.einsum("td,qd->tq", branch_grad, w_aout, preferred_element_type=f32)
    grad_mixed = grad_attended.astype(bf16).reshape(tok_rows, KH, group_size, HD)
    grad_mamba_in = jnp.einsum("td,id->ti", branch_grad, w_mout, preferred_element_type=f32)
    grad_ssd = lax.optimization_barrier((grad_mamba_in * gate_act).astype(bf16)).astype(f32)
    grad_ssd = grad_ssd.reshape(tok_rows, MIXER_HEADS, MP)
    grad_gating = grad_mamba_in * ssd_flat * silu_slope(gating)
    direct = jnp.einsum("th,thp,tn->hpn", reach_decay, grad_ssd, input_c, precision=highest)

    empty_grads = jnp.zeros((key_all.shape[0], KV_WIDTH), f32)
    grad_query, grad_keys, grad_values = backward_attend(
        grouped,
        grad_mixed,
        mixer_output,
        log_total,
        query_pos,
        key_all,
        value_all,
        empty_grads,
        empty_grads,
    )
    grad_query = grad_query.reshape(tok_rows, Q_WIDTH)
    sent_back = jnp.concatenate(
        [
            direct.astype(bf16).reshape(CTX, STATE_ROWS, NS),
            grad_keys.astype(bf16).reshape(CTX, tok_rows, KV_WIDTH),
            grad_values.astype(bf16).reshape(CTX, tok_rows, KV_WIDTH),
        ],
        axis=1,
    )
    got_back = swap(sent_back, "ctx")
    ends = swap(prefix(got_back[:, :STATE_ROWS], decay_rows, True), "ctx")
    carried_back = ends.reshape(MIXER_HEADS, MP, NS).astype(f32)
    shares = jnp.sum(got_back[:, STATE_ROWS:].astype(f32), axis=0)
    key_share, value_share = shares[:tok_rows], shares[tok_rows:]

    grad_x_ssd, grad_b, grad_c = pull_states((grad_ssd, carried_back))
    grad_c = grad_c + jnp.einsum(
        "th,thp,hpn->tn", reach_decay, grad_ssd, start_state, precision=highest
    )
    grad_act = jnp.concatenate([grad_x_ssd.reshape(tok_rows, MI), grad_b, grad_c], axis=1)
    grad_conv_out = (grad_act * silu_slope(conv_out)).astype(bf16)
    ahead_rows = passed_along(grad_conv_out[: CONV - 1], "ctx", -1)
    extended = jnp.concatenate([grad_conv_out, ahead_rows], axis=0)
    grad_conv_in = jnp.zeros((tok_rows, XBC), f32)
    grad_tap_list = []
    for tap_index in range(CONV):
        lead = CONV - 1 - tap_index
        grad_conv_in = grad_conv_in + extended[lead : lead + tok_rows].astype(f32) * conv_taps[tap_index][None, :]
        grad_tap_list.append(
            jnp.sum(
                grad_conv_out.astype(f32) * padded[tap_index : tap_index + tok_rows].astype(f32),
                axis=0,
            )
        )
    grad_conv = jnp.stack(grad_tap_list, axis=0)
    grad_proj_m = jnp.concatenate([grad_gating, grad_conv_in], axis=1).astype(bf16)

    grad_q_pre = rotate(grad_query.reshape(tok_rows, QH, HD) * score_scale, positions, -1.0)
    grad_k_pre = rotate((key_share * score_scale).reshape(tok_rows, KH, HD), positions, -1.0)
    grad_proj_a = jnp.concatenate(
        [
            grad_q_pre.reshape(tok_rows, Q_WIDTH),
            grad_k_pre.reshape(tok_rows, KV_WIDTH),
            value_share,
        ],
        axis=1,
    ).astype(bf16)
    second_share = lax.psum_scatter(
        mix_grads(mamba_in, attended, branch_grad, shared, grad_proj_m, grad_proj_a),
        "fsdp",
        scatter_dimension=0,
        tiled=True,
    )[0]
    grad_proj = jnp.concatenate([grad_proj_m, grad_proj_a], axis=1)
    grad_shared = jnp.einsum("tc,dc->td", grad_proj, first_weights, preferred_element_type=f32)
    grad_g_one = jnp.sum(grad_shared * normed, axis=0)
    grad_tokens = grad_residual + rms_back(grad_shared, normed, inverse_one, gain_first)

    conv_owned = grad_conv.reshape(CONV, OWNERS, XBC // OWNERS).transpose(1, 0, 2)
    small_grads = jnp.concatenate(
        [
            grad_g_one.reshape(OWNERS, 128),
            conv_owned.reshape(OWNERS, 896),
            grad_g_two.reshape(OWNERS, 128),
            jnp.zeros((OWNERS, 896), f32),
        ],
        axis=1,
    ).astype(bf16).reshape(OWNERS, 2, D)
    small_got = jnp.sum(swap(small_grads, "fsdp").astype(f32), axis=0).astype(bf16)
    small_rows = jnp.concatenate([small_got, jnp.zeros((14, D), bf16)], axis=0)

    first_sum = ctx_sum(first_share.reshape(CTX, 48, D)).reshape(768, D).astype(f32)
    second_chunks = jnp.concatenate(
        [second_share.reshape(CTX, 48, D), small_rows.reshape(CTX, 1, D)], axis=1
    )
    second_sum = ctx_sum(second_chunks).astype(f32)
    small_sum = second_sum[:2, 48]
    second_sum = second_sum[:, :48].reshape(768, D)

    def widened(blocks):
        return blocks.reshape(4, 128, D).transpose(1, 0, 2).reshape(128, 4 * D)

    in_grads = widened(second_sum[256:])
    return (
        output[None],
        grad_tokens[None],
        small_sum[0, :128],
        in_grads[:, : MI + XBC],
        small_sum[0, 128:].reshape(CONV, XBC // OWNERS).T,
        second_sum[:192],
        in_grads[:, MI + XBC :],
        second_sum[192:256],
        small_sum[1, :128],
        widened(first_sum[256:]),
        first_sum[:256],
    )


def solution(mesh):
    in_specs = (
        P("fsdp", "ctx", None),
        P("fsdp"),
        P("fsdp", None),
        P("fsdp", None),
        P("fsdp", None),
        P("fsdp", None),
        P("fsdp", None),
        P("fsdp"),
        P("fsdp", None),
        P("fsdp", None),
        P("fsdp", "ctx", None),
        P("fsdp", "ctx", None),
        P("fsdp", "ctx", None),
    )
    out_specs = (
        P("fsdp", "ctx", None),
        P("fsdp", "ctx", None),
        P("fsdp"),
        P("fsdp", None),
        P("fsdp", None),
        P("fsdp", None),
        P("fsdp", None),
        P("fsdp", None),
        P("fsdp"),
        P("fsdp", None),
        P("fsdp", None),
    )
    return jax.shard_map(
        on_device, mesh=mesh, in_specs=in_specs, out_specs=out_specs, check_vma=False
    )
```

time: 943 us -> 511 us (0.54)
  waiting for transfers between devices: 528 us -> 150 us
  blocking collectives: 144 us -> 53.3 us
  starting transfers between devices: 7.67 us -> 61.4 us
  local copies, waits for them, and re-layouts: 37.7 us -> 79.2 us
  matrix products: 105 us -> 65.9 us
  other arithmetic: 83.2 us -> 49.6 us
  Pallas kernels: 0 us -> 16.6 us
    unnamed x21 -> x4, waiting for transfers between devices: 146 us -> 0.07 us
    reduce_scatter x6 -> x2, waiting for transfers between devices: 183 us -> 47.8 us  [the longest x1 47.8 us: on_device(): lax.psum_scatter(mix_grads(mamba_in, attended, branch_grad, shared, grad_...]
    all_gather x8 -> x2, waiting for transfers between devices: 128 us -> 24.6 us  [the longest x1 24.6 us: on_device(): lax.all_gather(jnp.concatenate([w_mamba_in, w_qkv], axis=1), 'fsdp', axis...]
    all_to_all x0 -> x8, waiting for transfers between devices: none -> 75.2 us  [swap(): return lax.all_to_all(value, axis, 0, 0, tiled=True)]
    psum x1 -> x0, waiting for transfers between devices: 65.5 us -> none  [on_device(): lax.psum(partials[1].astype(jnp.bfloat16), 'ctx').astype(jnp.float32)]
    all_to_all x0 -> x8, starting transfers between devices: none -> 54.4 us  [swap(): return lax.all_to_all(value, axis, 0, 0, tiled=True)]
    all_gather x6 -> x2, blocking collectives: 96.9 us -> 44.8 us  [the longest x1 31 us: on_device(): decays_all = lax.all_gather(whole_decay[None], 'ctx', axis=0, tiled=True)]
    select_n x32 -> x0, other arithmetic: 37.9 us -> none  [hop(): return jax.tree.map(lambda a, b: jnp.where(reached, a, b), new, before)]
  transfers between devices with their start and end apart: 20 -> 14, of which waited for: 15 -> 8; matrix products, arithmetic and copies ran while one was open for 19% -> 30% of each run, Pallas kernels for 0% -> 2%
where the time goes in v1:
time: 511 us; the launch traced here: 501 us
  waiting for transfers between devices  150 us (29%)
  local copies, waits for them, and re-layouts  79.2 us (15%)
  matrix products  65.9 us (13%)
  starting transfers between devices  61.4 us (12%)
  blocking collectives  53.3 us (10%)
  other arithmetic  49.6 us (10%)
  Pallas kernels  16.6 us (3%)
  between operations  16 us (3%)
  loops' own time  8.82 us (2%)
    all_to_all x8, waiting for transfers between devices, swap(): return lax.all_to_all(value, axis, 0, 0, tiled=True)  75.2 us
    all_to_all x8, starting transfers between devices, swap(): return lax.all_to_all(value, axis, 0, 0, tiled=True)  54.4 us
    reduce_scatter x1, waiting for transfers between devices, on_device(): lax.psum_scatter(mix_grads(mamba_in, attended, branch_grad, shared, grad_...  47.8 us
    all_gather x1, blocking collectives, on_device(): decays_all = lax.all_gather(whole_decay[None], 'ctx', axis=0, tiled=True)  31 us
    all_gather x1, waiting for transfers between devices, on_device(): lax.all_gather(jnp.concatenate([w_mamba_in, w_qkv], axis=1), 'fsdp', axis...  24.6 us
    all_gather x1, blocking collectives, on_device(): small_all = lax.all_gather(small[None], 'fsdp', axis=0, tiled=True)  13.7 us
    unnamed x195, local copies, waits for them, and re-layouts  13 us
  transfers between devices with their start and end apart: 14, of which 8 were waited for; matrix products, arithmetic and copies ran while one was open for 30% of the time, Pallas kernels for 2%

profile of v1, /device:TPU:38, one launch (start us, length us, event | category | flops | bytes accessed | tf_op | source)
XLA Modules:
  0.0 501.1 jit_solution(13281915086820443974)
XLA Ops:
  7.3 2.4 pad_maximum_fusion.3
  15.2 3.5 collective-permute-start
  18.9 13.7 %all-gather.2 = bf16[8,1,1152]{2,1,0:T(2,128)(2,1)S(1)} all-gather(bf16[1,1,1152]{2,1,0:T(2,128)(2,1)S(1)} %reshape.399), channel_id=2, replica_groups=mesh['ctx'=16,'fsdp'=8] {'fsdp'}, dimensions={0}, use_global_device_ids=true | all-gather | bytes 20736 | tf_op jit(solution)/shard_map/all_gather | solution.py:367
  36.8 24.6 %all-gather.7.cloned.1.call-done = bf16[1024,4096]{1,0:T(8,128)(2,1)} async-done(((bf16[128,4096]{1,0:T(8,128)(2,1)}), bf16[1024,4096]{1,0:T(8,128)(2,1)}) %all-gather.7.cloned.1.call-update) | async-done | bytes 8388624 | tf_op jit(solution)/shard_map/all_gather | solution.py:357
  61.4 4.7 fusion.102
  68.6 1.9 copy.161
  73.7 7.4 %all-to-all-start = ((bf16[16,352,128]{2,1,0:T(8,128)(2,1)}), bf16[16,352,128]{2,1,0:T(8,128)(2,1)}, u32[]{:S(2)}, u32[]{:S(2)}) async-start(bf16[16,352,128]{2,1,0:T(8,128)(2,1)} %pad_maximum_fusion.1), calls=%async_computation | async-start | bytes 2883584 | tf_op jit(solution)/shard_map/all_to_all | solution.py:45
  81.1 31.0 %all-gather.3 = f32[16,1,24]{2,1,0:T(1,128)S(1)} all-gather(f32[1,1,24]{2,1,0:T(1,128)S(1)} %get-tuple-element.874), channel_id=1, replica_groups=mesh['ctx'=16,'fsdp'=8] {'ctx'}, dimensions={0}, use_global_device_ids=true | all-gather | bytes 1632 | tf_op jit(solution)/shard_map/all_gather | solution.py:377
  120.7 5.8 %all-to-all-start.1 = ((bf16[16,96,128]{2,1,0:T(8,128)(2,1)}), bf16[16,96,128]{2,1,0:T(8,128)(2,1)S(1)}, u32[]{:S(2)}, u32[]{:S(2)}) async-start(bf16[16,96,128]{2,1,0:T(8,128)(2,1)} %state_prefix.2), calls=%async_computation.1 | async-start | bytes 786432 | tf_op jit(solution)/shard_map/all_to_all | solution.py:45
  128.5 7.5 %while.51 = (s32[]{:T(128)}, f32[2,4,128]{2,1,0:T(4,128)S(1)}, f32[2,4,128]{2,1,0:T(4,128)S(1)}, s32[]{:T(128)}, bf16[2048,128]{0,1:T(8,128)(2,1)S(1)}, /*index=...) while((s32[]{:T(128)}, f32[2,4,128]{2,1,0:T(4,128)S(1)}, ...), condition=%wide.region_8.9_spmd.clone, body=%wide.region_3.8_spmd.clone.sunk | while | flops 70847104 | bytes 4974865 | solution.py:136
  136.1 7.0 %while.52 = (s32[]{:T(128)}, f32[128,2,4,64]{0,3,2,1:T(8,128)S(1)}, s32[]{:T(128)}, bf16[2048,128]{0,1:T(8,128)(2,1)S(1)}, bf16[2048,128]{0,1:T(8,128)(2,1)S(1)}...) while((s32[]{:T(128)}, f32[128,2,4,64]{0,3,2,1:T(8,128)S(1)}, ...), condition=%wide.region_12.13_spmd.clone, body=%wide.region_9.12_spmd.clone.sunk | while | flops 136446592 | bytes 1583361 | solution.py:157
  144.3 3.6 fusion.29
  152.3 2.6 slice.348
  154.9 5.0 %fusion.99 = (bf16[8,128,1024]{2,1,0:T(8,128)(2,1)S(1)}, bf16[8,128,1024]{2,1,0:T(8,128)(2,1)S(1)}, bf16[8,128,1024]{2,1,0:T(8,128)(2,1)S(1)}, bf16[8,128,1024]{2,1,0:T(8,128)(2,1)S(1)}) fusion(bf16[8,1024,1024]{2,1,0:T(8,128)(2,1)} %bitcast.300), kind=kLoop, calls=%fused_computation.248 | loop fusion | bytes 16777216 | tf_op jit(solution)/shard_map/slice | solution.py:446
  160.0 5.5 %slice.354 = bf16[8,256,1024]{2,1,0:T(8,128)(2,1)S(1)} slice(bf16[8,1024,1024]{2,1,0:T(8,128)(2,1)} %bitcast.301), slice={[0:8], [256:512], [0:1024]} | slice | bytes 8388608 | tf_op jit(solution)/shard_map/slice | solution.py:444
  169.2 1.7 multiply_convert_fusion
  171.8 8.1 %ffn_grads.1 = bf16[8,768,1024]{2,1,0:T(8,128)(2,1)} custom-call(bf16[128,2048]{1,0:T(8,128)(2,1)S(1)} %get-tuple-element.859.hidden_ref, bf16[128,1024]{1,0:T(8,128)(2,1)S(1)} %bitcast.288, bf16[128,1024]{1,0:T(8,128)(2,1)S(1)} %multiply_convert_fusion.8.second_ref, bf16[128,4096]{1,0:T(8,128)(2,1)S(1)} %pad_maximum_fusion.6.grad_gu_ref), custom_call_target="tpu_custom_call" | custom-call | tf_op jit(solution)/shard_map/ffn_grads/pallas_call | solution.py:275
  181.0 2.6 fusion.72
  183.7 1.9 convolution_add_fusion.3
  190.4 2.2 constant_dynamic-update-slice_fusion.9
  193.5 1.9 copy.176
  195.5 1.8 convolution_convert_fusion.2
  201.2 30.6 %while.53 = (s32[]{:T(128)}, f32[128,2,4,64]{0,3,2,1:T(8,128)}, f32[2048,128]{0,1:T(8,128)}, f32[2048,128]{0,1:T(8,128)}, s32[]{:T(128)}, /*index=5*/bf16[2048,1...) while((s32[]{:T(128)}, f32[128,2,4,64]{0,3,2,1:T(8,128)}, ...), condition=%wide.region_18.19_spmd.clone, body=%wide.region_15.18_spmd.clone.sunk | while | flops 339477120 | bytes 15743409 | solution.py:232
  201.9 7.0 %conditional.11 = ((f32[128,2,4,64]{0,3,2,1:T(8,128)}, f32[2048,128]{0,1:T(8,128)}, f32[2048,128]{0,1:T(8,128)})) conditional(s32[]{:T(128)} %convert_element_type.398, (f32[128,2,4,64]{0,3,2,1:T(8,128)}, f32[2048,128]{0,1:T(8,128)}, f32[2048,128]{0,1:T(8,128)}) %tuple.174, (s32[]{:T(128)}, bf16[2048,128]{0,1:T(8,128)(2,1)}, s32[]{:T(128)}, ...), branch_computations={%region_16.16_spmd, %region_17.17_spmd} | conditional | flops 339477120 | bytes 15742618 | solution.py:227
  206.0 1.9 constant_dynamic-update-slice_fusion
  209.5 7.0 %conditional.11 = ((f32[128,2,4,64]{0,3,2,1:T(8,128)}, f32[2048,128]{0,1:T(8,128)}, f32[2048,128]{0,1:T(8,128)})) conditional(s32[]{:T(128)} %convert_element_type.398, (f32[128,2,4,64]{0,3,2,1:T(8,128)}, f32[2048,128]{0,1:T(8,128)}, f32[2048,128]{0,1:T(8,128)}) %tuple.174, (s32[]{:T(128)}, bf16[2048,128]{0,1:T(8,128)(2,1)}, s32[]{:T(128)}, ...), branch_computations={%region_16.16_spmd, %region_17.17_spmd} | conditional | flops 339477120 | bytes 15742618 | solution.py:227
  213.6 1.9 constant_dynamic-update-slice_fusion
  217.2 7.0 %conditional.11 = ((f32[128,2,4,64]{0,3,2,1:T(8,128)}, f32[2048,128]{0,1:T(8,128)}, f32[2048,128]{0,1:T(8,128)})) conditional(s32[]{:T(128)} %convert_element_type.398, (f32[128,2,4,64]{0,3,2,1:T(8,128)}, f32[2048,128]{0,1:T(8,128)}, f32[2048,128]{0,1:T(8,128)}) %tuple.174, (s32[]{:T(128)}, bf16[2048,128]{0,1:T(8,128)(2,1)}, s32[]{:T(128)}, ...), branch_computations={%region_16.16_spmd, %region_17.17_spmd} | conditional | flops 339477120 | bytes 15742618 | solution.py:227
  221.3 1.9 constant_dynamic-update-slice_fusion
  224.8 7.0 %conditional.11 = ((f32[128,2,4,64]{0,3,2,1:T(8,128)}, f32[2048,128]{0,1:T(8,128)}, f32[2048,128]{0,1:T(8,128)})) conditional(s32[]{:T(128)} %convert_element_type.398, (f32[128,2,4,64]{0,3,2,1:T(8,128)}, f32[2048,128]{0,1:T(8,128)}, f32[2048,128]{0,1:T(8,128)}) %tuple.174, (s32[]{:T(128)}, bf16[2048,128]{0,1:T(8,128)(2,1)}, s32[]{:T(128)}, ...), branch_computations={%region_16.16_spmd, %region_17.17_spmd} | conditional | flops 339477120 | bytes 15742618 | solution.py:227
  228.9 1.9 constant_dynamic-update-slice_fusion
  231.8 2.1 convert_element_type.248
  234.0 2.1 copy.180
  236.1 2.1 convert_element_type.249
  238.2 2.1 copy.181
  241.6 2.4 pad_maximum_fusion.2
  244.0 6.9 %all-to-all-start.2 = ((bf16[16,352,128]{2,1,0:T(8,128)(2,1)}), bf16[16,352,128]{2,1,0:T(8,128)(2,1)}, u32[]{:S(2)}, u32[]{:S(2)}) async-start(bf16[16,352,128]{2,1,0:T(8,128)(2,1)} %pad_maximum_fusion.2), calls=%async_computation.2 | async-start | bytes 2883584 | tf_op jit(solution)/shard_map/all_to_all | solution.py:45
  251.9 1.9 multiply_reduce_fusion
  257.7 11.5 %all-to-all-done.2 = bf16[16,352,128]{2,1,0:T(8,128)(2,1)} async-done(((bf16[16,352,128]{2,1,0:T(8,128)(2,1)}), bf16[16,352,128]{2,1,0:T(8,128)(2,1)}, u32[]{:S(2)}, u32[]{:S(2)}) %all-to-all-start.2) | async-done | bytes 1441824 | tf_op jit(solution)/shard_map/all_to_all | solution.py:45
  271.3 5.8 %all-to-all-start.3 = ((bf16[16,96,128]{2,1,0:T(8,128)(2,1)}), bf16[16,96,128]{2,1,0:T(8,128)(2,1)S(1)}, u32[]{:S(2)}, u32[]{:S(2)}) async-start(bf16[16,96,128]{2,1,0:T(8,128)(2,1)} %state_prefix.3), calls=%async_computation.3 | async-start | bytes 786432 | tf_op jit(solution)/shard_map/all_to_all | solution.py:45
  279.5 4.9 all-to-all-done.3
  285.5 3.1 fusion.31
  290.0 1.8 fusion.34
  291.8 3.0 fusion.44
  295.7 2.9 collective-permute-start.1
  298.7 2.6 collective-permute-done.1
  301.3 3.0 constant_dynamic-update-slice_fusion.8
  308.1 6.5 %mix_grads.1 = bf16[8,768,1024]{2,1,0:T(8,128)(2,1)} custom-call(bf16[128,1536]{1,0:T(8,128)(2,1)S(1)} %multiply_convert_fusion.6.mamba_ref, bf16[128,512]{1,0:T(8,128)(2,1)S(1)} %copy.193.attended_ref, bf16[128,1024]{1,0:T(8,128)(2,1)S(1)} %fusion.95.branch_ref, bf16[128,1024]{1,0:T(8,128)(2,1)S(1)} %slice.373.shared_ref, ...), custom_call_target="tpu_custom_call" | custom-call | tf_op jit(solution)/shard_map/mix_grads/pallas_call | solution.py:308
  315.7 6.7 %multiply_reduce_fusion.3 = (bf16[1024]{0:T(1024)(128)(2,1)S(1)}, f32[128]{0:T(128)S(1)}, f32[128,1024]{1,0:T(8,128)S(1)}) fusion(f32[136,1024]{1,0:T(8,128)S(1)} %copy-done.22, f32[1024]{0:T(1024)S(1)} %copy-done.69, bf16[128,4096]{1,0:T(8,128)(2,1)} %get-tuple-element.839, bf16[1024,4096]{1,0:T(8,128)(2,1)} %all-gather.7.cloned.1.call-done), kind=kOutput, calls=%fused_computation.140 | convolution fusion | flops 1074396032 | bytes 10492416 | tf_op jit(solution)/shard_map/tc,dc->td/dot_general | solution.py:556
  322.5 8.6 %all_to_all.45 = bf16[8,2,1024]{2,1,0:T(2,128)(2,1)S(1)} all-to-all(bf16[8,2,1024]{2,1,0:T(2,128)(2,1)S(1)} %copy.195), channel_id=1, replica_groups=mesh['ctx'=16,'fsdp'=8] {'fsdp'}, dimensions={0} | all-to-all | bytes 65536 | tf_op jit(solution)/shard_map/all_to_all | solution.py:45
  331.0 7.1 %all-to-all-start.7 = ((bf16[16,48,1024]{2,1,0:T(8,128)(2,1)}), bf16[16,48,1024]{2,1,0:T(8,128)(2,1)}, u32[]{:S(2)}, u32[]{:S(2)}) async-start(bf16[16,48,1024]{2,1,0:T(8,128)(2,1)} %bitcast.329), calls=%async_computation.9 | async-start | bytes 3145728 | tf_op jit(solution)/shard_map/all_to_all | solution.py:45
  338.2 47.8 %reduce-scatter.3.cloned.1.call-done = bf16[1,768,1024]{2,1,0:T(8,128)(2,1)} async-done(((bf16[8,768,1024]{2,1,0:T(8,128)(2,1)}), bf16[1,768,1024]{2,1,0:T(8,128)(2,1)}) %reduce-scatter.3.cloned.1.call-update) | async-done | bytes 1572880 | tf_op jit(solution)/shard_map/reduce_scatter | solution.py:549
  386.1 2.9 pad_maximum_fusion
  389.0 7.3 %all-to-all-start.5 = ((bf16[16,49,1024]{2,1,0:T(8,128)(2,1)}), bf16[16,49,1024]{2,1,0:T(8,128)(2,1)}, u32[]{:S(2)}, u32[]{:S(2)}) async-start(bf16[16,49,1024]{2,1,0:T(8,128)(2,1)} %pad_maximum_fusion), calls=%async_computation.6 | async-start | bytes 3670016 | tf_op jit(solution)/shard_map/all_to_all | solution.py:45
  397.9 25.9 %all-to-all-done.5 = bf16[16,49,1024]{2,1,0:T(8,128)(2,1)} async-done(((bf16[16,49,1024]{2,1,0:T(8,128)(2,1)}), bf16[16,49,1024]{2,1,0:T(8,128)(2,1)}, u32[]{:S(2)}, u32[]{:S(2)}) %all-to-all-start.5) | async-done | bytes 1605664 | tf_op jit(solution)/shard_map/all_to_all | solution.py:45
  425.2 6.7 %all-to-all-start.8 = ((bf16[16,48,1024]{2,1,0:T(8,128)(2,1)}), bf16[16,48,1024]{2,1,0:T(8,128)(2,1)}, u32[]{:S(2)}, u32[]{:S(2)}) async-start(bf16[16,48,1024]{2,1,0:T(8,128)(2,1)} %broadcast_in_dim.138), calls=%async_computation.10 | async-start | bytes 3145728 | tf_op jit(solution)/shard_map/all_to_all | solution.py:45
  431.9 1.9 reduce_sum.170
  433.8 20.1 %all-to-all-done.8 = bf16[16,48,1024]{2,1,0:T(8,128)(2,1)} async-done(((bf16[16,48,1024]{2,1,0:T(8,128)(2,1)}), bf16[16,48,1024]{2,1,0:T(8,128)(2,1)}, u32[]{:S(2)}, u32[]{:S(2)}) %all-to-all-start.8) | async-done | bytes 1572896 | tf_op jit(solution)/shard_map/all_to_all | solution.py:45
  455.3 7.4 %all-to-all-start.6 = ((bf16[16,49,1024]{2,1,0:T(8,128)(2,1)}), bf16[16,49,1024]{2,1,0:T(8,128)(2,1)}, u32[]{:S(2)}, u32[]{:S(2)}) async-start(bf16[16,49,1024]{2,1,0:T(8,128)(2,1)} %broadcast_in_dim.84), calls=%async_computation.7 | async-start | bytes 3670016 | tf_op jit(solution)/shard_map/all_to_all | solution.py:45
  462.8 3.7 fusion.33
  467.6 1.8 bitcast_convert_fusion
  472.1 12.8 %all-to-all-done.6 = bf16[16,49,1024]{2,1,0:T(8,128)(2,1)} async-done(((bf16[16,49,1024]{2,1,0:T(8,128)(2,1)}), bf16[16,49,1024]{2,1,0:T(8,128)(2,1)}, u32[]{:S(2)}, u32[]{:S(2)}) %all-to-all-start.6) | async-done | bytes 1605664 | tf_op jit(solution)/shard_map/all_to_all | solution.py:45
  485.0 1.8 slice.376
  492.1 2.0 slice.380
  (476 shorter events, 116.5 us)
Async XLA Ops:
  7.2 54.2 %all-gather.7.cloned.1.call-start = ((), (), s32[]{:S(2)}) async-start(), calls=%async_computation.11 | async-start | bytes 9437184 | tf_op jit(solution)/shard_map/all_gather | solution.py:357
  9.7 141.3 %all-gather.9.cloned.1.call-start = ((), (), s32[]{:S(2)}) async-start(), calls=%async_computation.14 | async-start | bytes 18874368 | tf_op jit(solution)/shard_map/all_gather | solution.py:365
  9.9 8.9 %copy-start.89 = (bf16[224,4]{0,1:T(4,128)(2,1)S(1)}, bf16[224,4]{0,1:T(4,128)(2,1)}, u32[]{:S(2)}) copy-start(bf16[224,4]{0,1:T(4,128)(2,1)} %param.28) | copy-start | bytes 5380
  9.9 8.9 %copy-start.90 = (bf16[128]{0:T(256)(128)(2,1)S(1)}, bf16[128]{0:T(256)(128)(2,1)}, u32[]{:S(2)}) copy-start(bf16[128]{0:T(256)(128)(2,1)} %param.32) | copy-start | bytes 772
  9.9 8.9 %copy-start.91 = (bf16[128]{0:T(256)(128)(2,1)S(1)}, bf16[128]{0:T(256)(128)(2,1)}, u32[]{:S(2)}) copy-start(bf16[128]{0:T(256)(128)(2,1)} %param.26) | copy-start | bytes 772
  10.9 21.8 %copy-start.79 = (f32[1,128,24]{1,2,0:T(8,128)S(1)}, f32[1,128,24]{1,2,0:T(8,128)}, u32[]{:S(2)}) copy-start(f32[1,128,24]{1,2,0:T(8,128)} %param.35) | copy-start | bytes 36868
  10.9 21.9 %copy-start.74 = (f32[1,128,24]{1,2,0:T(8,128)S(1)}, f32[1,128,24]{1,2,0:T(8,128)}, u32[]{:S(2)}) copy-start(f32[1,128,24]{1,2,0:T(8,128)} %param.36) | copy-start | bytes 36868
  15.2 20.4 %collective-permute-start = (bf16[8,1024]{1,0:T(8,128)(2,1)S(1)}, bf16[8,1024]{1,0:T(8,128)(2,1)S(1)}, u32[]{:S(2)}, u32[]{:S(2)}) collective-permute-start(bf16[8,1024]{1,0:T(8,128)(2,1)S(1)} %slice_bitcast_fusion), channel_id=1, source_target_pairs={{0,8},{8,16},{16,24},{24,32},{32,40},{40,48},{48,56},{56,64},{64,7... | collective-permute-start | bytes 49160 | tf_op jit(solution)/shard_map/ppermute | solution.py:41
  34.4 31.7 %copy-start.68 = (f32[1024]{0:T(1024)}, f32[1024]{0:T(1024)S(1)}, u32[]{:S(2)}) copy-start(f32[1024]{0:T(1024)S(1)} %get-tuple-element.877) | copy-start | bytes 12292
  35.1 35.5 %copy-start.51 = (f32[128,32]{0,1:T(8,128)}, f32[128,32]{0,1:T(8,128)S(1)}, u32[]{:S(2)}) copy-start(f32[128,32]{0,1:T(8,128)S(1)} %get-tuple-element.881) | copy-start | bytes 49156
  35.3 30.8 %copy-start.53 = (f32[1792]{0:T(1024)}, f32[1792]{0:T(1024)S(1)}, u32[]{:S(2)}) copy-start(f32[1792]{0:T(1024)S(1)} %mul.521) | copy-start | bytes 21508
  35.4 30.8 %copy-start.55 = (f32[1792]{0:T(1024)}, f32[1792]{0:T(1024)S(1)}, u32[]{:S(2)}) copy-start(f32[1792]{0:T(1024)S(1)} %mul.524) | copy-start | bytes 21508
  35.5 30.7 %copy-start.57 = (f32[1792]{0:T(1024)}, f32[1792]{0:T(1024)S(1)}, u32[]{:S(2)}) copy-start(f32[1792]{0:T(1024)S(1)} %mul.527) | copy-start | bytes 21508
  35.6 30.6 %copy-start.59 = (f32[1792]{0:T(1024)}, f32[1792]{0:T(1024)S(1)}, u32[]{:S(2)}) copy-start(f32[1792]{0:T(1024)S(1)} %mul.530) | copy-start | bytes 21508
  35.6 35.2 %copy-start.62 = (f32[128,24]{0,1:T(8,128)}, f32[128,24]{0,1:T(8,128)S(1)}, u32[]{:S(2)}) copy-start(f32[128,24]{0,1:T(8,128)S(1)} %copy.160) | copy-start | bytes 36868
  35.6 30.5 %copy-start.48 = (bf16[8,1024]{1,0:T(8,128)(2,1)}, bf16[8,1024]{1,0:T(8,128)(2,1)S(1)}, u32[]{:S(2)}) copy-start(bf16[8,1024]{1,0:T(8,128)(2,1)S(1)} %collective-permute-done) | copy-start | bytes 49156
  35.8 30.3 %copy-start.83 = (f32[136]{0:T(256)}, f32[136]{0:T(256)S(1)}, u32[]{:S(2)}) copy-start(f32[136]{0:T(256)S(1)} %add_rsqrt_fusion) | copy-start | bytes 1636
  36.8 29.4 %copy-start.23 = (bf16[136,1024]{1,0:T(8,128)(2,1)}, bf16[136,1024]{1,0:T(8,128)(2,1)S(1)}, u32[]{:S(2)}) copy-start(bf16[136,1024]{1,0:T(8,128)(2,1)S(1)} %get-tuple-element.867) | copy-start | bytes 835588
  66.1 50.8 %copy-start.17 = (f32[136,4096]{1,0:T(8,128)}, f32[136,4096]{1,0:T(8,128)S(1)}, u32[]{:S(2)}) copy-start(f32[136,4096]{1,0:T(8,128)S(1)} %get-tuple-element.884) | copy-start | bytes 6684676
  67.7 6.0 %copy-start.28 = (bf16[128,1792]{1,0:T(8,128)(2,1)}, bf16[128,1792]{1,0:T(8,128)(2,1)S(1)}, u32[]{:S(2)}) copy-start(bf16[128,1792]{1,0:T(8,128)(2,1)S(1)} %multiply_convert_fusion.3) | copy-start | bytes 1376260
  73.7 42.3 %copy-start.49 = (bf16[8,1024]{1,0:T(8,128)(2,1)S(1)}, bf16[8,1024]{1,0:T(8,128)(2,1)}, u32[]{:S(2)}) copy-start(bf16[8,1024]{1,0:T(8,128)(2,1)} %copy-done.48) | copy-start | bytes 49156
  73.7 44.9 %all-to-all-start = ((bf16[16,352,128]{2,1,0:T(8,128)(2,1)}), bf16[16,352,128]{2,1,0:T(8,128)(2,1)}, u32[]{:S(2)}, u32[]{:S(2)}) async-start(bf16[16,352,128]{2,1,0:T(8,128)(2,1)} %pad_maximum_fusion.1), calls=%async_computation | async-start | bytes 2883584 | tf_op jit(solution)/shard_map/all_to_all | solution.py:45
  81.1 35.9 %copy-start.52 = (f32[128,32]{0,1:T(8,128)S(1)}, f32[128,32]{0,1:T(8,128)}, u32[]{:S(2)}) copy-start(f32[128,32]{0,1:T(8,128)} %copy-done.51) | copy-start | bytes 49156
  120.7 22.4 %all-to-all-start.1 = ((bf16[16,96,128]{2,1,0:T(8,128)(2,1)}), bf16[16,96,128]{2,1,0:T(8,128)(2,1)S(1)}, u32[]{:S(2)}, u32[]{:S(2)}) async-start(bf16[16,96,128]{2,1,0:T(8,128)(2,1)} %state_prefix.2), calls=%async_computation.1 | async-start | bytes 786432 | tf_op jit(solution)/shard_map/all_to_all | solution.py:45
  126.5 204.5 %reduce-scatter.5.cloned.1.call-start = ((), (), s32[]{:S(2)}) async-start(), calls=%async_computation.13 | async-start | bytes 14155776 | tf_op jit(solution)/shard_map/reduce_scatter | solution.py:465
  136.0 7.1 %copy-start.64 = (f32[128,24]{0,1:T(8,128)S(1)}, f32[128,24]{0,1:T(8,128)}, u32[]{:S(2)}) copy-start(f32[128,24]{0,1:T(8,128)} %copy.171) | copy-start | bytes 36868
  136.0 8.2 %copy-start.36 = (bf16[128,1536]{0,1:T(8,128)(2,1)S(1)}, bf16[128,1536]{0,1:T(8,128)(2,1)}, u32[]{:S(2)}) copy-start(bf16[128,1536]{0,1:T(8,128)(2,1)} %copy.161) | copy-start | bytes 1179652
  136.0 8.2 %copy-start.72 = (pred[128,128]{1,0:T(8,128)(4,1)S(1)}, pred[128,128]{1,0:T(8,128)(4,1)}, u32[]{:S(2)}) copy-start(pred[128,128]{1,0:T(8,128)(4,1)} %iota_compare_fusion) | copy-start | bytes 49156
  136.0 8.2 %copy-start.75 = (f32[1,128,24]{1,2,0:T(8,128)S(1)}, f32[1,128,24]{1,2,0:T(8,128)}, u32[]{:S(2)}) copy-start(f32[1,128,24]{1,2,0:T(8,128)} %param.36) | copy-start | bytes 36868
  136.1 8.2 %copy-start.77 = (f32[24,128]{1,0:T(8,128)S(1)}, f32[24,128]{1,0:T(8,128)}, u32[]{:S(2)}) copy-start(f32[24,128]{1,0:T(8,128)} %copy.168) | copy-start | bytes 36868
  149.3 5.6 %copy-start.25 = (f32[128,1536]{1,0:T(8,128)}, f32[128,1536]{1,0:T(8,128)S(1)}, u32[]{:S(2)}) copy-start(f32[128,1536]{1,0:T(8,128)S(1)} %copy.173) | copy-start | bytes 2359300
  152.3 13.2 %copy-start.16 = (bf16[8,64,1024]{2,1,0:T(8,128)(2,1)}, bf16[8,64,1024]{2,1,0:T(8,128)(2,1)S(1)}, u32[]{:S(2)}) copy-start(bf16[8,64,1024]{2,1,0:T(8,128)(2,1)S(1)} %slice.344) | copy-start | bytes 3145732
  154.9 11.0 %copy-start.13 = (bf16[8,192,1024]{2,1,0:T(8,128)(2,1)}, bf16[8,192,1024]{2,1,0:T(8,128)(2,1)S(1)}, u32[]{:S(2)}) copy-start(bf16[8,192,1024]{2,1,0:T(8,128)(2,1)S(1)} %slice.348) | copy-start | bytes 9437188
  160.0 6.9 %copy-start.4 = (bf16[8,128,1024]{2,1,0:T(8,128)(2,1)}, bf16[8,128,1024]{2,1,0:T(8,128)(2,1)S(1)}, u32[]{:S(2)}) copy-start(bf16[8,128,1024]{2,1,0:T(8,128)(2,1)S(1)} %get-tuple-element.855) | copy-start | bytes 6291460
  160.0 7.3 %copy-start.2 = (bf16[8,128,1024]{2,1,0:T(8,128)(2,1)}, bf16[8,128,1024]{2,1,0:T(8,128)(2,1)S(1)}, u32[]{:S(2)}) copy-start(bf16[8,128,1024]{2,1,0:T(8,128)(2,1)S(1)} %get-tuple-element.854) | copy-start | bytes 6291460
  160.0 7.8 %copy-start.8 = (bf16[8,128,1024]{2,1,0:T(8,128)(2,1)}, bf16[8,128,1024]{2,1,0:T(8,128)(2,1)S(1)}, u32[]{:S(2)}) copy-start(bf16[8,128,1024]{2,1,0:T(8,128)(2,1)S(1)} %get-tuple-element.853) | copy-start | bytes 6291460
  160.0 8.2 %copy-start.6 = (bf16[8,128,1024]{2,1,0:T(8,128)(2,1)}, bf16[8,128,1024]{2,1,0:T(8,128)(2,1)S(1)}, u32[]{:S(2)}) copy-start(bf16[8,128,1024]{2,1,0:T(8,128)(2,1)S(1)} %get-tuple-element.856) | copy-start | bytes 6291460
  160.0 5.9 %copy-start.31 = (f32[136,1024]{1,0:T(8,128)S(1)}, f32[136,1024]{1,0:T(8,128)}, u32[]{:S(2)}) copy-start(f32[136,1024]{1,0:T(8,128)} %maximum_convert_fusion) | copy-start | bytes 1671172
  166.7 22.1 %copy-start.81 = (f32[128]{0:T(128)}, f32[128]{0:T(128)S(1)}, u32[]{:S(2)}) copy-start(f32[128]{0:T(128)S(1)} %add_rsqrt_fusion.1) | copy-start | bytes 1540
  170.9 9.0 %copy-start.32 = (bf16[128,2048]{1,0:T(8,128)(2,1)}, bf16[128,2048]{1,0:T(8,128)(2,1)S(1)}, u32[]{:S(2)}) copy-start(bf16[128,2048]{1,0:T(8,128)(2,1)S(1)} %get-tuple-element.857) | copy-start | bytes 1572868
  233.9 6.3 %copy-start.38 = (bf16[128,1536]{0,1:T(8,128)(2,1)S(1)}, bf16[128,1536]{0,1:T(8,128)(2,1)}, u32[]{:S(2)}) copy-start(bf16[128,1536]{0,1:T(8,128)(2,1)} %copy.176) | copy-start | bytes 1179652
  244.0 7.0 %copy-start.12 = (f32[128,2,4,64]{0,3,2,1:T(8,128)S(1)}, f32[128,2,4,64]{0,3,2,1:T(8,128)}, u32[]{:S(2)}) copy-start(f32[128,2,4,64]{0,3,2,1:T(8,128)} %get-tuple-element.586) | copy-start | bytes 786436
  244.0 7.0 %copy-start.50 = (f32[128,32]{0,1:T(8,128)S(1)}, f32[128,32]{0,1:T(8,128)}, u32[]{:S(2)}) copy-start(f32[128,32]{0,1:T(8,128)} %get-tuple-element.880) | copy-start | bytes 49156
  244.0 7.8 %copy-start.73 = (pred[128,128]{1,0:T(8,128)(4,1)S(1)}, pred[128,128]{1,0:T(8,128)(4,1)}, u32[]{:S(2)}) copy-start(pred[128,128]{1,0:T(8,128)(4,1)} %iota_compare_fusion) | copy-start | bytes 49156
  244.0 7.8 %copy-start.76 = (f32[1,128,24]{1,2,0:T(8,128)S(1)}, f32[1,128,24]{1,2,0:T(8,128)}, u32[]{:S(2)}) copy-start(f32[1,128,24]{1,2,0:T(8,128)} %param.36) | copy-start | bytes 36868
  244.0 7.8 %copy-start.78 = (f32[24,128]{1,0:T(8,128)S(1)}, f32[24,128]{1,0:T(8,128)}, u32[]{:S(2)}) copy-start(f32[24,128]{1,0:T(8,128)} %copy.168) | copy-start | bytes 36868
  244.0 25.2 %all-to-all-start.2 = ((bf16[16,352,128]{2,1,0:T(8,128)(2,1)}), bf16[16,352,128]{2,1,0:T(8,128)(2,1)}, u32[]{:S(2)}, u32[]{:S(2)}) async-start(bf16[16,352,128]{2,1,0:T(8,128)(2,1)} %pad_maximum_fusion.2), calls=%async_computation.2 | async-start | bytes 2883584 | tf_op jit(solution)/shard_map/all_to_all | solution.py:45
  270.3 14.1 %copy-start.63 = (f32[128,24]{0,1:T(8,128)S(1)}, f32[128,24]{0,1:T(8,128)}, u32[]{:S(2)}) copy-start(f32[128,24]{0,1:T(8,128)} %copy-done.62) | copy-start | bytes 36868
  271.3 14.2 %copy-start.40 = (bf16[128,1536]{0,1:T(8,128)(2,1)S(1)}, bf16[128,1536]{0,1:T(8,128)(2,1)}, u32[]{:S(2)}) copy-start(bf16[128,1536]{0,1:T(8,128)(2,1)} %copy.176) | copy-start | bytes 1179652
  271.3 13.1 %all-to-all-start.3 = ((bf16[16,96,128]{2,1,0:T(8,128)(2,1)}), bf16[16,96,128]{2,1,0:T(8,128)(2,1)S(1)}, u32[]{:S(2)}, u32[]{:S(2)}) async-start(bf16[16,96,128]{2,1,0:T(8,128)(2,1)} %state_prefix.3), calls=%async_computation.3 | async-start | bytes 786432 | tf_op jit(solution)/shard_map/all_to_all | solution.py:45
  277.1 109.0 %reduce-scatter.3.cloned.1.call-start = ((), (), s32[]{:S(2)}) async-start(), calls=%async_computation.12 | async-start | bytes 14155776 | tf_op jit(solution)/shard_map/reduce_scatter | solution.py:549
  278.8 5.6 %copy-start.46 = (f32[256,128]{1,0:T(8,128)}, f32[256,128]{1,0:T(8,128)S(1)}, u32[]{:S(2)}) copy-start(f32[256,128]{1,0:T(8,128)S(1)} %convert_reduce_fusion) | copy-start | bytes 393220
  290.0 8.6 %copy-start.70 = (bf16[128,2,32]{0,2,1:T(8,128)(2,1)S(1)}, bf16[128,2,32]{0,2,1:T(8,128)(2,1)}, u32[]{:S(2)}) copy-start(bf16[128,2,32]{0,2,1:T(8,128)(2,1)} %get-tuple-element.868) | copy-start | bytes 49156
  290.0 8.6 %copy-start.71 = (bf16[128,2,32]{0,2,1:T(8,128)(2,1)S(1)}, bf16[128,2,32]{0,2,1:T(8,128)(2,1)}, u32[]{:S(2)}) copy-start(bf16[128,2,32]{0,2,1:T(8,128)(2,1)} %get-tuple-element.869) | copy-start | bytes 49156
  291.8 9.5 %copy-start.58 = (f32[1792]{0:T(1024)S(1)}, f32[1792]{0:T(1024)}, u32[]{:S(2)}) copy-start(f32[1792]{0:T(1024)} %copy-done.57) | copy-start | bytes 21508
  291.8 9.5 %copy-start.60 = (f32[1792]{0:T(1024)S(1)}, f32[1792]{0:T(1024)}, u32[]{:S(2)}) copy-start(f32[1792]{0:T(1024)} %copy-done.59) | copy-start | bytes 21508
  291.8 12.5 %copy-start.44 = (bf16[128,512]{1,0:T(8,128)(2,1)S(1)}, bf16[128,512]{1,0:T(8,128)(2,1)}, u32[]{:S(2)}) copy-start(bf16[128,512]{1,0:T(8,128)(2,1)} %copy.189) | copy-start | bytes 393220
  295.7 5.6 %collective-permute-start.1 = (bf16[3,1792]{1,0:T(4,128)(2,1)S(1)}, bf16[3,1792]{1,0:T(4,128)(2,1)S(1)}, u32[]{:S(2)}, u32[]{:S(2)}) collective-permute-start(bf16[3,1792]{1,0:T(4,128)(2,1)S(1)} %slice.360), channel_id=1, source_target_pairs={{8,0},{16,8},{24,16},{32,24},{40,32},{48,40},{56,48},{64,56},{72,6... | collective-permute-start | bytes 32264 | tf_op jit(solution)/shard_map/ppermute | solution.py:41
  315.7 6.7 %copy-start.80 = (bf16[1024]{0:T(1024)(128)(2,1)S(1)}, bf16[1024]{0:T(1024)(128)(2,1)}, u32[]{:S(2)}) copy-start(bf16[1024]{0:T(1024)(128)(2,1)} %get-tuple-element.778) | copy-start | bytes 6148
  331.0 57.9 %all-to-all-start.7 = ((bf16[16,48,1024]{2,1,0:T(8,128)(2,1)}), bf16[16,48,1024]{2,1,0:T(8,128)(2,1)}, u32[]{:S(2)}, u32[]{:S(2)}) async-start(bf16[16,48,1024]{2,1,0:T(8,128)(2,1)} %bitcast.329), calls=%async_computation.9 | async-start | bytes 3145728 | tf_op jit(solution)/shard_map/all_to_all | solution.py:45
  389.0 34.9 %all-to-all-start.5 = ((bf16[16,49,1024]{2,1,0:T(8,128)(2,1)}), bf16[16,49,1024]{2,1,0:T(8,128)(2,1)}, u32[]{:S(2)}, u32[]{:S(2)}) async-start(bf16[16,49,1024]{2,1,0:T(8,128)(2,1)} %pad_maximum_fusion), calls=%async_computation.6 | async-start | bytes 3670016 | tf_op jit(solution)/shard_map/all_to_all | solution.py:45
  425.2 28.7 %all-to-all-start.8 = ((bf16[16,48,1024]{2,1,0:T(8,128)(2,1)}), bf16[16,48,1024]{2,1,0:T(8,128)(2,1)}, u32[]{:S(2)}, u32[]{:S(2)}) async-start(bf16[16,48,1024]{2,1,0:T(8,128)(2,1)} %broadcast_in_dim.138), calls=%async_computation.10 | async-start | bytes 3145728 | tf_op jit(solution)/shard_map/all_to_all | solution.py:45
  455.3 7.4 %copy-start.84 = (f32[136]{0:T(256)S(1)}, f32[136]{0:T(256)}, u32[]{:S(2)}) copy-start(f32[136]{0:T(256)} %copy-done.83) | copy-start | bytes 1636
  455.3 29.6 %all-to-all-start.6 = ((bf16[16,49,1024]{2,1,0:T(8,128)(2,1)}), bf16[16,49,1024]{2,1,0:T(8,128)(2,1)}, u32[]{:S(2)}, u32[]{:S(2)}) async-start(bf16[16,49,1024]{2,1,0:T(8,128)(2,1)} %broadcast_in_dim.84), calls=%async_computation.7 | async-start | bytes 3670016 | tf_op jit(solution)/shard_map/all_to_all | solution.py:45
  (48 other events, 130.5 us)
Sparse Core Ops, SparseCore 0:
  10.3 50.9 all-gather.6
  63.7 85.6 all-gather.8
  180.1 70.7 reduce-scatter.4
  314.8 71.2 reduce-scatter.2

commit v2 on v1

v2 whole, which is shorter than its diff:
```python
import functools

import jax
import jax.numpy as jnp
from jax import lax
from jax.experimental import pallas as pl
from jax.experimental.pallas import tpu as pltpu
from jax.sharding import PartitionSpec as P

D = 1024
QH = 8
KH = 2
HD = 64
MIXER_HEADS = 24
MP = 64
NS = 128
CONV = 4
FF = 2048
MI = MIXER_HEADS * MP
XBC = MI + 2 * NS
Q_WIDTH = QH * HD
KV_WIDTH = KH * HD
QKV = Q_WIDTH + 2 * KV_WIDTH
CTX = 16
OWNERS = 8
ROWS = 128
KEYS = CTX * ROWS
HALO = 16
PAIRS = MIXER_HEADS // 2
STATE_ROWS = MI // CTX
SENT_ROWS = STATE_ROWS + 2 * ROWS

epsilon = 1e-05
rope_base = 10000.0
masked_value = -1e30
score_scale = HD ** (-0.5)
bf16 = jnp.bfloat16
f32 = jnp.float32


def passed_along(value, axis, steps):
    count = lax.axis_size(axis)
    leading, last = (max(0, -steps), min(count, count - steps))
    return lax.ppermute(value, axis, [(source, source + steps) for source in range(leading, last)])


def swap(value, axis):
    return lax.all_to_all(value, axis, 0, 0, tiled=True)


def rms_back(grad_normed, normed, inverse, gain):
    scaled = grad_normed * gain
    return inverse * (scaled - normed * jnp.mean(scaled * normed, axis=-1, keepdims=True))


def params():
    return pltpu.CompilerParams(vmem_limit_bytes=60 * 1024 * 1024)


def whole(shape):
    return pl.BlockSpec(shape, lambda *_: (0,) * len(shape))


def struct(shape, dtype):
    return jax.ShapeDtypeStruct(shape, dtype)


def dot(left, right):
    return jnp.dot(left, right, preferred_element_type=f32)


def dot_last(left, right):
    return lax.dot_general(left, right, (((1,), (1,)), ((), ())), preferred_element_type=f32)


def dot_first(left, right):
    return lax.dot_general(left, right, (((0,), (0,)), ((), ())), preferred_element_type=f32)


def lanes(rows=ROWS):
    return lax.broadcasted_iota(jnp.int32, (rows, 128), 1)


def by_head(first, second):
    return jnp.where(lanes() < MP, first, second)


def turned(values):
    ahead = pltpu.roll(values, 96, 1)
    behind = pltpu.roll(values, 32, 1)
    return jnp.where(lax.rem(lanes(), HD) < HD // 2, -ahead, behind)


def half_filled(pair, head):
    group = head // (QH // KH)
    placed = pair if head % 2 == group else pltpu.roll(pair, 64, 1)
    return jnp.where(lanes() // HD == group, placed, 0.0).astype(bf16)


def state_pieces(block, store):
    for piece in range(4):
        row = ROWS * block[0] + 32 * piece
        store(row // STATE_ROWS, row % STATE_ROWS, block[1][32 * piece : 32 * (piece + 1)])


def enter_kernel(
    proj_ref,
    taps_ref,
    cum_ref,
    cum_t_ref,
    gate_ref,
    gate_t_ref,
    cos_ref,
    sin_ref,
    conv_in_ref,
    conv_out_ref,
    act_ref,
    local_ref,
    query_ref,
    sent_ref,
    ext_ref,
):
    for at in range(0, XBC, 256):
        cols = slice(at, at + 256)
        low = proj_ref[:, MI + at : MI + at + 256].astype(bf16)
        conv_in_ref[:, cols] = low
        ext_ref[...] = low.astype(f32)
        conv = jnp.zeros((ROWS, 256), f32)
        for tap in range(CONV):
            start = HALO - (CONV - 1) + tap
            conv = conv + ext_ref[start : start + ROWS, :] * taps_ref[tap : tap + 1, cols]
        conv_out_ref[:, cols] = conv
        act_ref[:, cols] = (conv * jax.nn.sigmoid(conv)).astype(bf16)

    cos, sin = cos_ref[...], sin_ref[...]
    for part in range(QKV // 128):
        at = MI + XBC + 128 * part
        values = proj_ref[HALO:, at : at + 128]
        if part < 5:
            values = values * cos + turned(values) * sin
        if part < 4:
            for head in (2 * part, 2 * part + 1):
                query_ref[head * ROWS : (head + 1) * ROWS] = half_filled(values, head)
        else:
            begin = STATE_ROWS + ROWS * (part - 4)
            low = values.astype(bf16)
            for to in range(CTX):
                sent_ref[to, begin : begin + ROWS] = low

    inputs_b = act_ref[:, MI : MI + NS]
    inputs_c = act_ref[:, MI + NS :]
    products = dot_last(inputs_c, inputs_b)
    row_ids = lax.broadcasted_iota(jnp.int32, (ROWS, ROWS), 0)
    causal = lanes() <= row_ids
    cum = cum_ref[...]
    remain_all = jnp.exp(cum[ROWS - 1 : ROWS] - cum) * gate_ref[...]

    def store(to, row, value):
        sent_ref[to, row : row + 32] = value

    for pair in range(PAIRS):
        cols = slice(128 * pair, 128 * (pair + 1))
        inputs_x = act_ref[:, cols]
        outs = []
        for head in (2 * pair, 2 * pair + 1):
            spread = cum[:, head : head + 1] - cum_t_ref[head : head + 1, :]
            weights = jnp.exp(jnp.where(causal, spread, masked_value))
            mixing = weights * products * gate_t_ref[head : head + 1, :]
            outs.append(dot(mixing.astype(bf16), inputs_x))
        local_ref[:, cols] = by_head(*outs)
        remain = by_head(*(remain_all[:, head : head + 1] for head in (2 * pair, 2 * pair + 1)))
        state = dot_first((inputs_x.astype(f32) * remain).astype(bf16), inputs_b).astype(bf16)
        state_pieces((pair, state), store)


def enter(projected, taps, cum, gates, cos, sin):
    return pl.pallas_call(
        enter_kernel,
        out_shape=(
            struct((ROWS + HALO, XBC), bf16),
            struct((ROWS, XBC), f32),
            struct((ROWS, XBC), bf16),
            struct((ROWS, MI), f32),
            struct((QH * ROWS, 128), bf16),
            struct((CTX, SENT_ROWS, NS), bf16),
        ),
        scratch_shapes=[pltpu.VMEM((ROWS + HALO, 256), f32)],
        compiler_params=params(),
        name="enter",
    )(projected, taps, cum, cum.T, gates, gates.T, cos, sin)


def prefix_kernel(reverse, parts_ref, decay_ref, out_ref):
    running = jnp.zeros(out_ref.shape[1:], f32)
    for at in range(CTX - 1, -1, -1) if reverse else range(CTX):
        out_ref[at] = running.astype(bf16)
        running = decay_ref[at] * running + parts_ref[at].astype(f32)


def prefix(got, decay_rows, reverse):
    return pl.pallas_call(
        functools.partial(prefix_kernel, reverse),
        grid=(1,),
        in_specs=[whole((CTX, STATE_ROWS, NS)), whole((CTX, STATE_ROWS, 1))],
        out_specs=whole((CTX, STATE_ROWS, NS)),
        out_shape=struct((CTX, STATE_ROWS, NS), bf16),
        compiler_params=params(),
        name="state_prefix",
    )(got, decay_rows)


def key_mask(first_row):
    keys = lax.broadcasted_iota(jnp.int32, (KEYS, 4 * ROWS), 0)
    queries = lax.rem(lax.broadcasted_iota(jnp.int32, (KEYS, 4 * ROWS), 1), ROWS)
    return keys <= queries + first_row


def attend_kernel(first_row_ref, query_ref, got_ref, attended_ref, total_ref):
    keys = got_ref[:, STATE_ROWS : STATE_ROWS + ROWS].reshape(KEYS, 128)
    values = got_ref[:, STATE_ROWS + ROWS :].reshape(KEYS, 128)
    allowed = key_mask(first_row_ref[0])
    for group in range(KH):
        queries = query_ref[512 * group : 512 * (group + 1)]
        scores = dot_last(keys, queries) * score_scale
        scores = jnp.where(allowed, scores, masked_value)
        top = jnp.max(scores, axis=0, keepdims=True)
        exponent = jnp.exp(scores - top)
        total = jnp.sum(exponent, axis=0, keepdims=True)
        probs = (exponent * (1.0 / total)).astype(bf16)
        total_ref[group] = jnp.broadcast_to(top + jnp.log(total), (8, 512))
        mixed = dot_first(values, probs)[64 * group : 64 * (group + 1)]
        for part in range(2):
            both = [mixed[:, 128 * (2 * part + k) : 128 * (2 * part + k + 1)] for k in range(2)]
            at = 256 * group + 128 * part
            attended_ref[:, at : at + 128] = jnp.concatenate(both, axis=0).T.astype(bf16)


def attend(first_row, queries, got):
    return pl.pallas_call(
        attend_kernel,
        in_specs=[
            pl.BlockSpec(memory_space=pltpu.SMEM),
            pl.BlockSpec(memory_space=pltpu.VMEM),
            pl.BlockSpec(memory_space=pltpu.VMEM),
        ],
        out_shape=(struct((ROWS, Q_WIDTH), bf16), struct((KH, 8, 512), f32)),
        compiler_params=params(),
        name="attend",
    )(first_row, queries, got)


def leave_kernel(local_ref, starts_ref, act_ref, cum_ref, gating_ref, ssd_ref, mamba_ref):
    inputs_c = act_ref[...]
    reach = jnp.exp(cum_ref[...])
    starts = starts_ref[...].reshape(MI, NS)
    for pair in range(PAIRS):
        cols = slice(128 * pair, 128 * (pair + 1))
        scale = by_head(*(reach[:, head : head + 1] for head in (2 * pair, 2 * pair + 1)))
        out = local_ref[:, cols] + scale * dot_last(inputs_c, starts[cols])
        ssd_ref[:, cols] = out
        gating = gating_ref[HALO:, cols]
        mamba_ref[:, cols] = (out * (gating * jax.nn.sigmoid(gating))).astype(bf16)


def leave(local_out, starts, activated, cum, projected):
    return pl.pallas_call(
        leave_kernel,
        grid=(1,),
        in_specs=[
            whole((ROWS, MI)),
            whole((CTX, STATE_ROWS, NS)),
            pl.BlockSpec((ROWS, NS), lambda i: (0, (MI + NS) // NS)),
            whole((ROWS, MIXER_HEADS)),
            whole((ROWS + HALO, MI)),
        ],
        out_specs=(whole((ROWS, MI)), whole((ROWS, MI))),
        out_shape=(struct((ROWS, MI), f32), struct((ROWS, MI), bf16)),
        compiler_params=params(),
        name="leave",
    )(local_out, starts, activated, cum, projected)


def middle_kernel(
    mamba_ref,
    attended_ref,
    tokens_ref,
    grad_out_ref,
    gain_ref,
    ssd_ref,
    gating_ref,
    rest_ref,
    down_hbm_ref,
    output_ref,
    grad_residual_ref,
    branch_ref,
    grad_gain_ref,
    grad_attended_ref,
    grad_ssd_ref,
    grad_gating_ref,
    early_ref,
    mout_ref,
    aout_ref,
    left_ref,
    right_ref,
    gu_ref,
    own_gu_ref,
    own_down_ref,
    own_mout_ref,
    own_aout_ref,
    sems,
    own_sems,
):
    def fetch(begin, rows, target, sem):
        copy = pltpu.make_async_copy(rest_ref.at[:, pl.ds(begin, rows)], target, sems.at[sem])
        copy.start()
        return copy

    get_mout = fetch(0, 192, mout_ref, 0)
    get_aout = fetch(192, 64, aout_ref, 1)
    get_gu = {}
    for order, block in enumerate((0, 2)):
        get_gu[block] = fetch(384 + 128 * block, 128, gu_ref.at[block], 2 + order)
    get_down = []
    for owner in range(OWNERS):
        source = down_hbm_ref.at[:, pl.ds(16 * owner, 16)]
        get_down.append(pltpu.make_async_copy(source, left_ref.at[owner], sems.at[8 + owner]))
    for side in range(2):
        source = rest_ref.at[:, pl.ds(256, 128), pl.ds(512 * side, 512)]
        target = right_ref.at[:, pl.ds(128 * side, 128)]
        get_down.append(pltpu.make_async_copy(source, target, sems.at[6 + side]))
    for copy in get_down:
        copy.start()
    for order, block in enumerate((1, 3)):
        get_gu[block] = fetch(384 + 128 * block, 128, gu_ref.at[block], 4 + order)

    get_mout.wait()
    mamba_out = dot(mamba_ref[...], mout_ref[...].reshape(MI, D))
    get_aout.wait()
    attn_out = dot(attended_ref[...], aout_ref[...].reshape(Q_WIDTH, D))
    residual = tokens_ref[...].astype(f32) + attn_out + mamba_out
    inverse = lax.rsqrt(jnp.mean(residual * residual, axis=-1, keepdims=True) + epsilon)
    normed = residual * inverse
    gain = gain_ref[...]
    second = (normed * gain).astype(bf16)
    second_turned = second.T
    sending = []

    def send(source, target, sem):
        copy = pltpu.make_async_copy(source, target, own_sems.at[sem])
        copy.start()
        sending.append(copy)

    grad_out = grad_out_ref[...]
    result = jnp.zeros((ROWS, D), f32)
    grad_second = jnp.zeros((ROWS, D), f32)
    for half in range(2):
        get_gu[half].wait()
        get_gu[2 + half].wait()
        w_gate = gu_ref[half].reshape(D, D)
        w_up = gu_ref[2 + half].reshape(D, D)
        gate = dot(second, w_gate)
        up = dot(second, w_up)
        logistic = jax.nn.sigmoid(gate)
        active = gate * logistic
        hidden = (active * up).astype(bf16)
        if half == 0:
            for copy in get_down:
                copy.wait()
        w_left = left_ref[4 * half : 4 * (half + 1)].reshape(D, 512)
        w_right = right_ref[4 * half : 4 * (half + 1)].reshape(D, 512)
        result = result + jnp.concatenate([dot(hidden, w_left), dot(hidden, w_right)], axis=1)
        grad_hidden = dot_last(grad_out[:, :512], w_left) + dot_last(grad_out[:, 512:], w_right)
        slope = logistic * (1.0 + gate * (1.0 - logistic))
        grad_gate = (grad_hidden * up * slope).astype(bf16)
        grad_up = (grad_hidden * active).astype(bf16)
        grad_second = grad_second + dot_last(grad_gate, w_gate) + dot_last(grad_up, w_up)
        while sending:
            sending.pop().wait()
        for side, grads in enumerate((grad_gate, grad_up)):
            own_gu_ref[side] = dot(second_turned, grads).astype(bf16).reshape(OWNERS, 128, D)
            begin = 512 + 128 * (half + 2 * side)
            send(own_gu_ref.at[side], early_ref.at[:, pl.ds(begin, 128)], side)
        own_down_ref[...] = dot_first(hidden, grad_out).astype(bf16).reshape(4, 256, D)
        send(own_down_ref, early_ref.at[pl.ds(4 * half, 4), pl.ds(256, 256)], 2)
    output_ref[...] = (residual + result).astype(bf16)
    grad_gain_ref[...] = jnp.broadcast_to(
        jnp.sum(grad_second * normed, axis=0, keepdims=True), (8, D)
    )
    grad_residual = grad_out.astype(f32) + rms_back(grad_second, normed, inverse, gain)
    grad_residual_ref[...] = grad_residual
    branch = grad_residual.astype(bf16)
    branch_ref[...] = branch
    own_mout_ref[...] = dot_first(mamba_ref[...], branch).astype(bf16).reshape(OWNERS, 192, D)
    send(own_mout_ref, early_ref.at[:, pl.ds(0, 192)], 3)
    own_aout_ref[...] = dot_first(attended_ref[...], branch).astype(bf16).reshape(OWNERS, 64, D)
    send(own_aout_ref, early_ref.at[:, pl.ds(192, 64)], 4)
    grad_attended_ref[...] = dot_last(branch, aout_ref[...].reshape(Q_WIDTH, D)).astype(bf16)
    for at in range(0, MI, 384):
        cols = slice(at, at + 384)
        w_part = mout_ref[at // 192 : at // 192 + 2].reshape(384, D)
        grad_mamba = dot_last(branch, w_part)
        gating = gating_ref[HALO:, cols]
        logistic = jax.nn.sigmoid(gating)
        grad_ssd_ref[:, cols] = (grad_mamba * (gating * logistic)).astype(bf16)
        slope = logistic * (1.0 + gating * (1.0 - logistic))
        grad_gating_ref[:, cols] = (grad_mamba * ssd_ref[:, cols] * slope).astype(bf16)
    while sending:
        sending.pop().wait()


def middle(
    mamba_in, attended, tokens, grad_out, gain, ssd_out, projected, rest_weights, down_weights
):
    return pl.pallas_call(
        middle_kernel,
        grid=(1,),
        in_specs=[
            whole((ROWS, MI)),
            whole((ROWS, Q_WIDTH)),
            whole((ROWS, D)),
            whole((ROWS, D)),
            whole((1, D)),
            whole((ROWS, MI)),
            whole((ROWS + HALO, MI)),
            pl.BlockSpec(memory_space=pl.ANY),
            pl.BlockSpec(memory_space=pl.ANY),
        ],
        out_specs=(
            whole((ROWS, D)),
            whole((ROWS, D)),
            whole((ROWS, D)),
            whole((8, D)),
            whole((ROWS, Q_WIDTH)),
            whole((ROWS, MI)),
            whole((ROWS, MI)),
            pl.BlockSpec(memory_space=pl.ANY),
        ),
        out_shape=(
            struct((ROWS, D), bf16),
            struct((ROWS, D), f32),
            struct((ROWS, D), bf16),
            struct((8, D), f32),
            struct((ROWS, Q_WIDTH), bf16),
            struct((ROWS, MI), bf16),
            struct((ROWS, MI), bf16),
            struct((OWNERS, D, D), bf16),
        ),
        scratch_shapes=[
            pltpu.VMEM((OWNERS, 192, D), bf16),
            pltpu.VMEM((OWNERS, 64, D), bf16),
            pltpu.VMEM((OWNERS, CTX, 16, 512), bf16),
            pltpu.VMEM((OWNERS, 256, 512), bf16),
            pltpu.VMEM((4, OWNERS, 128, D), bf16),
            pltpu.VMEM((2, OWNERS, 128, D), bf16),
            pltpu.VMEM((4, 256, D), bf16),
            pltpu.VMEM((OWNERS, 192, D), bf16),
            pltpu.VMEM((OWNERS, 64, D), bf16),
            pltpu.SemaphoreType.DMA((8 + OWNERS,)),
            pltpu.SemaphoreType.DMA((5,)),
        ],
        compiler_params=params(),
        name="middle",
    )(
        mamba_in,
        attended,
        tokens,
        grad_out,
        gain,
        ssd_out,
        projected,
        rest_weights,
        down_weights,
    )


def attend_back_kernel(
    first_row_ref,
    query_ref,
    got_ref,
    total_ref,
    grad_attended_ref,
    grad_ssd_ref,
    inputs_c_ref,
    cum_ref,
    grad_query_ref,
    sent_ref,
):
    keys = got_ref[:, STATE_ROWS : STATE_ROWS + ROWS].reshape(KEYS, 128)
    values = got_ref[:, STATE_ROWS + ROWS :].reshape(KEYS, 128)
    allowed = key_mask(first_row_ref[0])
    grad_keys = jnp.zeros((KEYS, 128), f32)
    grad_values = jnp.zeros((KEYS, 128), f32)
    for group in range(KH):
        queries = query_ref[512 * group : 512 * (group + 1)]
        grads = []
        for head in range(4 * group, 4 * group + 4):
            pair = grad_attended_ref[:, 128 * (head // 2) : 128 * (head // 2 + 1)].astype(f32)
            grads.append(half_filled(pair, head))
        grads = jnp.concatenate(grads, axis=0)
        scores = dot_last(keys, queries) * score_scale
        scores = jnp.where(allowed, scores, masked_value)
        probs = jnp.exp(scores - total_ref[group, 0:1, :])
        grad_probs = dot_last(values, grads)
        delta = jnp.sum(probs * grad_probs, axis=0, keepdims=True)
        grad_scores = (probs * (grad_probs - delta)).astype(bf16)
        grad_values = grad_values + dot(probs.astype(bf16), grads)
        grad_keys = grad_keys + dot(grad_scores, queries)
        turned_query = dot_first(keys, grad_scores)[64 * group : 64 * (group + 1)]
        for part in range(2):
            both = [
                turned_query[:, 128 * (2 * part + k) : 128 * (2 * part + k + 1)] for k in range(2)
            ]
            at = 256 * group + 128 * part
            grad_query_ref[:, at : at + 128] = jnp.concatenate(both, axis=0).T
    sent_ref[:, STATE_ROWS : STATE_ROWS + ROWS] = grad_keys.astype(bf16).reshape(CTX, ROWS, 128)
    sent_ref[:, STATE_ROWS + ROWS :] = grad_values.astype(bf16).reshape(CTX, ROWS, 128)

    def store(to, row, value):
        sent_ref[to, row : row + 32] = value

    inputs_c = inputs_c_ref[...]
    reach = jnp.exp(cum_ref[...])
    for pair in range(PAIRS):
        cols = slice(128 * pair, 128 * (pair + 1))
        scale = by_head(*(reach[:, head : head + 1] for head in (2 * pair, 2 * pair + 1)))
        scaled = (grad_ssd_ref[:, cols].astype(f32) * scale).astype(bf16)
        state_pieces((pair, dot_first(scaled, inputs_c).astype(bf16)), store)


def attend_back(first_row, queries, got, total, grad_attended, grad_ssd, activated, cum):
    return pl.pallas_call(
        attend_back_kernel,
        grid=(1,),
        in_specs=[
            pl.BlockSpec(memory_space=pltpu.SMEM),
            whole((QH * ROWS, 128)),
            whole((CTX, SENT_ROWS, 128)),
            whole((KH, 8, 512)),
            whole((ROWS, Q_WIDTH)),
            whole((ROWS, MI)),
            pl.BlockSpec((ROWS, NS), lambda i: (0, (MI + NS) // NS)),
            whole((ROWS, MIXER_HEADS)),
        ],
        out_specs=(whole((ROWS, Q_WIDTH)), whole((CTX, SENT_ROWS, NS))),
        out_shape=(struct((ROWS, Q_WIDTH), f32), struct((CTX, SENT_ROWS, NS), bf16)),
        compiler_params=params(),
        name="attend_back",
    )(first_row, queries, got, total, grad_attended, grad_ssd, activated, cum)


def ssd_back_kernel(
    grad_ssd_ref,
    act_ref,
    conv_out_ref,
    cum_ref,
    cum_t_ref,
    gate_ref,
    starts_ref,
    ends_ref,
    grad_query_ref,
    got_ref,
    cos_ref,
    sin_ref,
    grad_conv_ref,
    grad_a_ref,
):
    inputs_b = act_ref[:, MI : MI + NS]
    inputs_c = act_ref[:, MI + NS :]
    products = dot_last(inputs_b, inputs_c)
    row_ids = lax.broadcasted_iota(jnp.int32, (ROWS, ROWS), 0)
    causal = row_ids <= lanes()
    cum = cum_ref[...]
    reach = jnp.exp(cum)
    gates = gate_ref[...]
    remain_all = jnp.exp(cum[ROWS - 1 : ROWS] - cum) * gates
    starts = starts_ref[...].reshape(MI, NS)
    ends = ends_ref[...].reshape(MI, NS)
    grad_products = jnp.zeros((ROWS, ROWS), f32)
    grad_b = jnp.zeros((ROWS, NS), f32)
    grad_c = jnp.zeros((ROWS, NS), f32)

    def through(conv, grad):
        logistic = jax.nn.sigmoid(conv)
        return (grad * (logistic * (1.0 + conv * (1.0 - logistic)))).astype(bf16)

    for pair in range(PAIRS):
        cols = slice(128 * pair, 128 * (pair + 1))
        heads = (2 * pair, 2 * pair + 1)
        inputs_x = act_ref[:, cols]
        grads = grad_ssd_ref[:, cols]
        wide_x = inputs_x.astype(f32)
        back = []
        for side, head in enumerate(heads):
            spread = cum_t_ref[head : head + 1, :] - cum[:, head : head + 1]
            weights = jnp.exp(jnp.where(causal, spread, masked_value)) * gates[:, head : head + 1]
            back.append(dot((weights * products).astype(bf16), grads))
            own = jnp.where(lanes() // MP == side, wide_x, 0.0).astype(bf16)
            grad_products = grad_products + weights * dot_last(own, grads)
        remain = by_head(*(remain_all[:, head : head + 1] for head in heads))
        scale = by_head(*(reach[:, head : head + 1] for head in heads))
        grad_x = by_head(*back) + remain * dot_last(inputs_b, ends[cols])
        grad_conv_ref[:, cols] = through(conv_out_ref[:, cols], grad_x)
        grad_b = grad_b + dot((wide_x * remain).astype(bf16), ends[cols])
        grad_c = grad_c + dot((grads.astype(f32) * scale).astype(bf16), starts[cols])
    low = grad_products.astype(bf16)
    grad_b = grad_b + dot(low, inputs_c)
    grad_c = grad_c + dot_first(low, inputs_b)
    grad_conv_ref[:, MI : MI + NS] = through(conv_out_ref[:, MI : MI + NS], grad_b)
    grad_conv_ref[:, MI + NS :] = through(conv_out_ref[:, MI + NS :], grad_c)

    cos, sin = cos_ref[...], sin_ref[...]
    for part in range(QKV // 128):
        if part < 4:
            values = grad_query_ref[:, 128 * part : 128 * (part + 1)]
        else:
            begin = STATE_ROWS + ROWS * (part - 4)
            values = jnp.sum(got_ref[:, begin : begin + ROWS].astype(f32), axis=0)
        if part < 5:
            values = (values * cos - turned(values) * sin) * score_scale
        grad_a_ref[:, 128 * part : 128 * (part + 1)] = values.astype(bf16)


def ssd_back(grad_ssd, activated, conv_out, cum, gates, starts, ends, grad_query, got, cos, sin):
    return pl.pallas_call(
        ssd_back_kernel,
        out_shape=(struct((ROWS, XBC), bf16), struct((ROWS, QKV), bf16)),
        compiler_params=params(),
        name="ssd_back",
    )(grad_ssd, activated, conv_out, cum, cum.T, gates, starts, ends, grad_query, got, cos, sin)


def conv_back_kernel(grad_ref, ahead_ref, conv_in_ref, taps_ref, out_ref, grad_taps_ref, ext_ref, in_ref):
    for at in range(0, XBC, 256):
        cols = slice(at, at + 256)
        grads = grad_ref[:, cols].astype(f32)
        ext_ref[:ROWS] = grads
        ext_ref[ROWS:] = ahead_ref[:, cols].astype(f32)
        in_ref[...] = conv_in_ref[:, cols].astype(f32)
        total = jnp.zeros((ROWS, 256), f32)
        for tap in range(CONV):
            lead = CONV - 1 - tap
            total = total + ext_ref[lead : lead + ROWS, :] * taps_ref[tap : tap + 1, cols]
            start = HALO - lead
            grad_taps_ref[tap : tap + 1, cols] = jnp.sum(
                grads * in_ref[start : start + ROWS, :], axis=0, keepdims=True
            )
        out_ref[:, cols] = total.astype(bf16)


def conv_back(grad_conv_out, ahead, conv_in, taps):
    return pl.pallas_call(
        conv_back_kernel,
        out_shape=(struct((ROWS, XBC), bf16), struct((CONV, XBC), f32)),
        scratch_shapes=[pltpu.VMEM((ROWS + HALO, 256), f32), pltpu.VMEM((ROWS + HALO, 256), f32)],
        compiler_params=params(),
        name="conv_back",
    )(grad_conv_out, ahead, conv_in, taps)


def late_grads_kernel(shared_ref, grad_ref, out_ref):
    for block in range(4):
        part = dot_first(shared_ref[...], grad_ref[:, D * block : D * (block + 1)]).astype(bf16)
        for owner in range(2):
            out_ref[owner, 128 * block : 128 * (block + 1)] = part[128 * owner : 128 * (owner + 1)]


def late_grads(shared, grad_proj):
    return pl.pallas_call(
        late_grads_kernel,
        grid=(OWNERS // 2,),
        in_specs=[pl.BlockSpec((ROWS, 256), lambda f: (0, f)), whole((ROWS, 4 * D))],
        out_specs=pl.BlockSpec((2, 512, D), lambda f: (f, 0, 0)),
        out_shape=struct((OWNERS, 512, D), bf16),
        compiler_params=params(),
        name="late_grads",
    )(shared, grad_proj)


def fold_kernel(parts_ref, out_ref):
    total = parts_ref[0].astype(f32)
    for part in range(1, CTX):
        total = total + parts_ref[part].astype(f32)
    low = total.astype(bf16)
    for to in range(CTX):
        out_ref[to] = low


def fold(parts):
    rows = parts.shape[1]
    return pl.pallas_call(
        fold_kernel,
        grid=(rows // 16,),
        in_specs=[pl.BlockSpec((CTX, 16, D), lambda i: (0, i, 0))],
        out_specs=pl.BlockSpec((CTX, 16, D), lambda i: (0, i, 0)),
        out_shape=struct(parts.shape, bf16),
        compiler_params=params(),
        name="fold",
    )(parts)


def spread_kernel(parts_ref, mamba_ref, qkv_ref):
    for block in range(4):
        part = parts_ref[4 * block : 4 * (block + 1)].reshape(ROWS, D).astype(f32)
        if block < 3:
            mamba_ref[:, D * block : D * (block + 1)] = part
        else:
            mamba_ref[:, 3 * D :] = part[:, :256]
            qkv_ref[...] = part[:, 256:]


def spread(parts):
    return pl.pallas_call(
        spread_kernel,
        out_shape=(struct((ROWS, MI + XBC), f32), struct((ROWS, QKV), f32)),
        compiler_params=params(),
        name="spread",
    )(parts)


def widened(blocks):
    return blocks.reshape(4, ROWS, D).transpose(1, 0, 2).reshape(ROWS, 4 * D)


def on_device(
    tokens,
    gain_one,
    w_mamba_in,
    conv_weight,
    w_mamba_out,
    w_qkv,
    w_attn_out,
    gain_two,
    w_gate_up,
    w_down,
    decays,
    input_gates,
    grad_out,
):
    tokens = tokens[0]
    decays = decays[0]
    input_gates = input_gates[0]
    grad_out = grad_out[0]
    ctx_index = lax.axis_index("ctx")
    offset = ctx_index * ROWS
    first_row = offset.astype(jnp.int32).reshape(1)

    first_weights = lax.all_gather(
        jnp.concatenate([w_mamba_in, w_qkv], axis=1), "fsdp", axis=0, tiled=True
    )
    rest = jnp.concatenate(
        [
            w_mamba_out,
            w_attn_out,
            jnp.concatenate([w_down[:128, 512:], w_down[128:, 512:]], axis=1),
        ]
        + [w_gate_up[:, D * block : D * (block + 1)] for block in range(4)],
        axis=0,
    )
    small = jnp.concatenate(
        [gain_one, gain_two, conv_weight.T.reshape(-1), jnp.zeros((7 * D - 128,), bf16)]
    )
    piece = lax.dynamic_slice(w_down, (ctx_index * 16, 0), (16, 512))
    piece = jnp.concatenate([piece, small.reshape(16, 512)], axis=0)
    pieces = swap(jnp.broadcast_to(piece[None], (OWNERS, 32, 512)), "fsdp")
    small_all = pieces[:, 16:19].reshape(OWNERS, 3 * 512)[:, :1152]
    gain_first = small_all[:, :128].reshape(1, D).astype(f32)
    gain_second = small_all[:, 128:256].reshape(1, D).astype(f32)
    conv_taps = small_all[:, 256:].reshape(OWNERS, CONV, XBC // OWNERS).transpose(1, 0, 2)
    conv_taps = conv_taps.reshape(CONV, XBC).astype(f32)

    cumulative = jnp.cumsum(jnp.log(decays), axis=0)
    whole_decay = jnp.exp(cumulative[-1:])
    decay_parts = []
    for _ in range(3):
        decay_parts.append(whole_decay.astype(bf16))
        whole_decay = whole_decay - decay_parts[-1].astype(f32)
    decay_parts = jnp.pad(jnp.concatenate(decay_parts, axis=1), ((0, 15), (0, 512 - 72)))
    sent_down = jnp.concatenate([pieces[:, :16].reshape(ROWS, 512), decay_parts], axis=0)
    down_weights = swap(jnp.broadcast_to(sent_down[None], (CTX, ROWS + 16, 512)), "ctx")
    decay_parts = down_weights[:, ROWS, :72].astype(f32)
    decays_all = decay_parts[:, :24] + decay_parts[:, 24:48] + decay_parts[:, 48:]
    decay_rows = lax.dynamic_slice_in_dim(
        jnp.repeat(decays_all, MP, axis=1), ctx_index * STATE_ROWS, STATE_ROWS, 1
    )[:, :, None]

    halo = passed_along(tokens[ROWS - HALO :], "ctx", 1)
    hidden_ext = jnp.concatenate([halo, tokens], axis=0).astype(f32)
    inverse_ext = lax.rsqrt(jnp.mean(hidden_ext * hidden_ext, axis=-1, keepdims=True) + epsilon)
    normed_ext = hidden_ext * inverse_ext
    shared_ext = (normed_ext * gain_first).astype(bf16)
    inverse_one = inverse_ext[HALO:]
    normed, shared = normed_ext[HALO:], shared_ext[HALO:]

    half_dim = HD // 2
    frequency = jnp.exp(-jnp.log(rope_base) * (2.0 * jnp.arange(half_dim).astype(f32) / HD))
    positions = (offset + jnp.arange(ROWS)).astype(f32)
    angles = jnp.tile(positions[:, None] * frequency[None, :], (1, 4))
    cosine, sine = jnp.cos(angles), jnp.sin(angles)

    (
        first_weights,
        decay_rows,
        shared_ext,
        cosine,
        sine,
        conv_taps,
        cumulative,
        rest,
        down_weights,
    ) = lax.optimization_barrier(
        (
            first_weights,
            decay_rows,
            shared_ext,
            cosine,
            sine,
            conv_taps,
            cumulative,
            rest,
            down_weights,
        )
    )
    rest_weights = lax.all_gather(rest, "fsdp", axis=0, tiled=False)
    projected = dot(shared_ext, first_weights)
    conv_in, conv_out, activated, local_out, queries, sent = enter(
        projected, conv_taps, cumulative, input_gates, cosine, sine
    )
    got = swap(sent, "ctx")
    starts = swap(prefix(got, decay_rows, False), "ctx")
    attended, total = attend(first_row, queries, got)
    ssd_out, mamba_in = leave(local_out, starts, activated, cumulative, projected)
    (
        output,
        grad_residual,
        branch_grad,
        grad_g_two,
        grad_attended,
        grad_ssd,
        grad_gating,
        early,
    ) = middle(
        mamba_in,
        attended,
        tokens,
        grad_out,
        gain_second,
        ssd_out,
        projected,
        rest_weights,
        down_weights,
    )
    early_share = lax.psum_scatter(
        early, "fsdp", scatter_dimension=0, tiled=True
    )[0]
    grad_query, sent_back = attend_back(
        first_row, queries, got, total, grad_attended, grad_ssd, activated, cumulative
    )
    got_back = swap(sent_back, "ctx")
    ends = swap(prefix(got_back, decay_rows, True), "ctx")
    grad_conv_out, grad_proj_a = ssd_back(
        grad_ssd,
        activated,
        conv_out,
        cumulative,
        input_gates,
        starts,
        ends,
        grad_query,
        got_back,
        cosine,
        sine,
    )
    ahead = passed_along(grad_conv_out[:HALO], "ctx", -1)
    grad_conv_in, grad_conv = conv_back(grad_conv_out, ahead, conv_in, conv_taps)
    grad_proj = jnp.concatenate([grad_gating, grad_conv_in, grad_proj_a], axis=1)
    grad_shared = dot_last(grad_proj, first_weights)
    grad_g_one = jnp.sum(grad_shared * normed, axis=0)
    grad_tokens = grad_residual + rms_back(grad_shared, normed, inverse_one, gain_first)

    conv_owned = grad_conv.reshape(CONV, OWNERS, XBC // OWNERS).transpose(1, 0, 2)
    small_grads = jnp.concatenate(
        [
            grad_g_one.reshape(OWNERS, 128),
            conv_owned.reshape(OWNERS, 896),
            grad_g_two[0].reshape(OWNERS, 128),
            jnp.zeros((OWNERS, 896), f32),
        ],
        axis=1,
    ).astype(bf16).reshape(OWNERS, 2, D)
    small_got = jnp.sum(swap(small_grads, "fsdp").astype(f32), axis=0).astype(bf16)
    small_got, grad_proj = lax.optimization_barrier((small_got, grad_proj))
    small_sum = swap(jnp.broadcast_to(small_got[None], (CTX, 2, D)), "ctx").astype(f32)
    late_share = lax.psum_scatter(
        late_grads(shared, grad_proj), "fsdp", scatter_dimension=0, tiled=True
    )[0]
    early_share, small_sum = lax.optimization_barrier((early_share, jnp.sum(small_sum, axis=0)))
    early_got = swap(early_share.reshape(CTX, 64, D), "ctx")
    early_sum = swap(fold(early_got), "ctx")
    late_share, early_sum = lax.optimization_barrier((late_share, early_sum))
    late_sum = swap(fold(swap(late_share.reshape(CTX, 32, D), "ctx")), "ctx")
    grad_in, grad_qkv = spread(late_sum)
    early_sum = early_sum.reshape(D, D).astype(f32)
    return (
        output[None],
        grad_tokens[None],
        small_sum[0, :128],
        grad_in,
        small_sum[0, 128:].reshape(CONV, XBC // OWNERS).T,
        early_sum[:192],
        grad_qkv,
        early_sum[192:256],
        small_sum[1, :128],
        widened(early_sum[512:]),
        early_sum[256:512],
    )


def solution(mesh):
    in_specs = (
        P("fsdp", "ctx", None),
        P("fsdp"),
        P("fsdp", None),
        P("fsdp", None),
        P("fsdp", None),
        P("fsdp", None),
        P("fsdp", None),
        P("fsdp"),
        P("fsdp", None),
        P("fsdp", None),
        P("fsdp", "ctx", None),
        P("fsdp", "ctx", None),
        P("fsdp", "ctx", None),
    )
    out_specs = (
        P("fsdp", "ctx", None),
        P("fsdp", "ctx", None),
        P("fsdp"),
        P("fsdp", None),
        P("fsdp", None),
        P("fsdp", None),
        P("fsdp", None),
        P("fsdp", None),
        P("fsdp"),
        P("fsdp", None),
        P("fsdp", None),
    )
    return jax.shard_map(
        on_device, mesh=mesh, in_specs=in_specs, out_specs=out_specs, check_vma=False
    )
```

time: 511 us -> 399 us (0.78)
  the two profiles are of different devices: /device:TPU:38 before, /device:TPU:0 now
where the time goes in v2:
time: 399 us; the launch traced here: 392 us
  waiting for transfers between devices  129 us (32%)
  Pallas kernels  75 us (19%)
  blocking collectives  72.8 us (18%)
  starting transfers between devices  44.6 us (11%)
  local copies, waits for them, and re-layouts  31.7 us (8%)
  between operations  14.7 us (4%)
  matrix products  14.2 us (4%)
  other arithmetic  9.74 us (2%)
    all_to_all x9, waiting for transfers between devices, swap(): return lax.all_to_all(value, axis, 0, 0, tiled=True)  111 us
    all_to_all x3, blocking collectives, swap(): return lax.all_to_all(value, axis, 0, 0, tiled=True)  72.8 us
    all_to_all x9, starting transfers between devices, swap(): return lax.all_to_all(value, axis, 0, 0, tiled=True)  39.3 us
    pallas_call x1, Pallas kernels, middle(): pl.pallas_call(middle_kernel, grid=(1,), in_specs=[whole((ROWS, MI)), who...  20 us
    all_gather x1, waiting for transfers between devices, on_device(): rest_weights = lax.all_gather(rest, 'fsdp', axis=0, tiled=False)  14.7 us
    unnamed x50, local copies, waits for them, and re-layouts  11.6 us
    pallas_call x1, Pallas kernels, attend_back(): pl.pallas_call(attend_back_kernel, grid=(1,), in_specs=[pl.BlockSpec(memo...  10.2 us
  transfers between devices with their start and end apart: 15, of which 11 were waited for; matrix products, arithmetic and copies ran while one was open for 12% of the time, Pallas kernels for 13%

profile of v2, /device:TPU:0, one launch (start us, length us, event | category | flops | bytes accessed | tf_op | source)
XLA Modules:
  0.0 392.0 jit_solution(7036211070547939210)
XLA Ops:
  7.3 2.4 pad_maximum_fusion
  9.8 3.7 collective-permute-start
  14.4 5.3 %all-to-all-start = ((bf16[8,32,512]{2,1,0:T(8,128)(2,1)}), bf16[8,32,512]{2,1,0:T(8,128)(2,1)S(1)}, u32[]{:S(2)}, u32[]{:S(2)}) async-start(bf16[8,32,512]{2,1,0:T(8,128)(2,1)} %broadcast_in_dim.19), calls=%async_computation | async-start | bytes 524288 | tf_op jit(solution)/shard_map/all_to_all | solution.py:48
  20.1 0.8 constant_dynamic-update-slice_fusion.1
  21.6 0.7 maximum_dynamic-update-slice_fusion
  22.3 1.7 slice_dynamic-update-slice_fusion.3
  24.0 3.2 all-to-all-done
  27.3 1.6 broadcast_in_dim.20
  29.0 6.7 %all-to-all-start.1 = ((bf16[16,144,512]{2,1,0:T(8,128)(2,1)}), bf16[16,144,512]{2,1,0:T(8,128)(2,1)S(1)}, u32[]{:S(2)}, u32[]{:S(2)}) async-start(bf16[16,144,512]{2,1,0:T(8,128)(2,1)} %broadcast_in_dim.20), calls=%async_computation.1 | async-start | bytes 4718592 | tf_op jit(solution)/shard_map/all_to_all | solution.py:48
  35.8 1.7 slice_dynamic-update-slice_fusion.2
  37.4 1.7 slice_dynamic-update-slice_fusion.1
  39.1 1.7 slice_dynamic-update-slice_fusion
  40.8 0.8 multiply_sine_fusion
  43.7 0.8 convert_multiply_fusion
  44.5 24.2 %all-to-all-done.1.down_hbm_ref = bf16[16,144,512]{2,1,0:T(8,128)(2,1)S(1)} async-done(((bf16[16,144,512]{2,1,0:T(8,128)(2,1)}), bf16[16,144,512]{2,1,0:T(8,128)(2,1)S(1)}, u32[]{:S(2)}, u32[]{:S(2)}) %all-to-all-start.1) | async-done | bytes 2359328 | tf_op jit(solution)/shard_map/all_to_all | solution.py:48
  69.1 0.8 tile.10
  71.3 1.5 copy.87
  74.3 6.6 %fusion.15.proj_ref.gating_ref = f32[144,4096]{1,0:T(8,128)} fusion(bf16[144,1024]{1,0:T(8,128)(2,1)S(1)} %get-tuple-element.51, bf16[1024,4096]{1,0:T(8,128)(2,1)} %all-gather.4.cloned.1.call-done), kind=kOutput, calls=%fused_computation.67 | convolution fusion | flops 1207959552 | bytes 11042816 | tf_op jit(solution)/shard_map/dot_general | solution.py:69
  80.9 6.4 %enter.1 = (bf16[144,1792]{1,0:T(8,128)(2,1)}, f32[128,1792]{1,0:T(8,128)}, bf16[128,1792]{1,0:T(8,128)(2,1)}, f32[128,1536]{1,0:T(8,128)}, bf16[1024,128]{1,0:T(8,128)(2,1)}, /*index=5*/bf16[16,352,128]{2,1,0:T(8,128)(2,1)}) custom-call(f32[144,4096]{1,0:T(8,128)} %fusion.15.proj_ref.gating_ref, f32[4,1792]{1,0:T(4,128)} %reshape.196.taps_ref, ...), custom_call_target="tpu_custom_call" | custom-call | tf_op jit(solution)/shard_map/enter/pallas_call | solution.py:177
  87.2 3.7 all-to-all-start.2
  91.0 1.2 copy.92.decay_ref
  92.2 17.7 %all-to-all-done.2.parts_ref.got_ref = bf16[16,352,128]{2,1,0:T(8,128)(2,1)S(1)} async-done(((bf16[16,352,128]{2,1,0:T(8,128)(2,1)}), bf16[16,352,128]{2,1,0:T(8,128)(2,1)S(1)}, u32[]{:S(2)}, u32[]{:S(2)}) %all-to-all-start.2) | async-done | bytes 1441824 | tf_op jit(solution)/shard_map/all_to_all | solution.py:48
  109.8 1.1 copy-done
  110.9 2.3 state_prefix.2
  113.2 3.6 all-to-all-start.3
  117.0 6.5 %attend.1 = (bf16[128,512]{1,0:T(8,128)(2,1)}, f32[2,8,512]{2,1,0:T(8,128)}) custom-call(s32[1]{0:T(128)} %bitcast.15.first_row_ref, bf16[1024,128]{1,0:T(8,128)(2,1)} %get-tuple-element.62.query_ref, bf16[16,352,128]{2,1,0:T(8,128)(2,1)} %copy-done), custom_call_target="tpu_custom_call" | custom-call | tf_op jit(solution)/shard_map/attend/pallas_call | solution.py:239
  123.5 2.3 all-to-all-done.3.starts_ref
  125.8 0.7 copy-done.3
  126.6 3.2 leave.1
  129.8 14.7 %all-gather.6.cloned.1.call-done = bf16[7168,1024]{1,0:T(8,128)(2,1)} async-done(((bf16[896,1024]{1,0:T(8,128)(2,1)}), bf16[7168,1024]{1,0:T(8,128)(2,1)}) %all-gather.6.cloned.1.call-update) | async-done | bytes 14680080 | tf_op jit(solution)/shard_map/all_gather | solution.py:823
  144.5 20.0 %middle.1 = (bf16[128,1024]{1,0:T(8,128)(2,1)}, f32[128,1024]{1,0:T(8,128)}, bf16[128,1024]{1,0:T(8,128)(2,1)}, f32[8,1024]{1,0:T(8,128)}, bf16[128,512]{1,0:T(8...) custom-call(bf16[128,1536]{1,0:T(8,128)(2,1)} %get-tuple-element.61.mamba_ref, ...), custom_call_target="tpu_custom_call" | custom-call | tf_op jit(solution)/shard_map/middle/pallas_call | solution.py:414
  164.6 10.2 %attend_back.1 = (f32[128,512]{1,0:T(8,128)}, bf16[16,352,128]{2,1,0:T(8,128)(2,1)}) custom-call(s32[1]{0:T(128)} %bitcast.15.first_row_ref, bf16[1024,128]{1,0:T(8,128)(2,1)} %get-tuple-element.62.query_ref, bf16[16,352,128]{2,1,0:T(8,128)(2,1)} %copy-done, f32[2,8,512]{2,1,0:T(8,128)} %get-tuple-element.72.total_ref, ...), custom_call_target="tpu_custom_call" | custom-call | tf_op jit(solution)/shard_map/attend_back/pallas_call | solution.py:531
  174.8 28.4 %all_to_all.60.parts_ref.got_ref = bf16[16,352,128]{2,1,0:T(8,128)(2,1)} all-to-all(bf16[16,352,128]{2,1,0:T(8,128)(2,1)} %get-tuple-element.74), channel_id=1, replica_groups=mesh['ctx'=16,'fsdp'=8] {'ctx'}, dimensions={0} | all-to-all | bytes 2883584 | tf_op jit(solution)/shard_map/all_to_all | solution.py:48
  203.2 2.3 state_prefix.3
  205.5 4.0 %all-to-all-start.5 = ((bf16[16,96,128]{2,1,0:T(8,128)(2,1)}), bf16[16,96,128]{2,1,0:T(8,128)(2,1)S(1)}, u32[]{:S(2)}, u32[]{:S(2)}) async-start(bf16[16,96,128]{2,1,0:T(8,128)(2,1)} %state_prefix.3), calls=%async_computation.5 | async-start | bytes 786432 | tf_op jit(solution)/shard_map/all_to_all | solution.py:48
  209.6 9.0 %all-to-all-done.5.ends_ref = bf16[16,96,128]{2,1,0:T(8,128)(2,1)S(1)} async-done(((bf16[16,96,128]{2,1,0:T(8,128)(2,1)}), bf16[16,96,128]{2,1,0:T(8,128)(2,1)S(1)}, u32[]{:S(2)}, u32[]{:S(2)}) %all-to-all-start.5) | async-done | bytes 393248 | tf_op jit(solution)/shard_map/all_to_all | solution.py:48
  218.7 0.7 copy-done.7
  219.4 5.6 %ssd_back.1 = (bf16[128,1792]{1,0:T(8,128)(2,1)}, bf16[128,768]{1,0:T(8,128)(2,1)}) custom-call(bf16[128,1536]{1,0:T(8,128)(2,1)} %get-tuple-element.70.grad_ssd_ref, bf16[128,1792]{1,0:T(8,128)(2,1)} %get-tuple-element.60.act_ref.inputs_c_ref, f32[128,1792]{1,0:T(8,128)} %get-tuple-element.71.conv_out_ref, f32[128,24]{1,0:T(8,128)} %copy-done.5, ...), custom_call_target="tpu_custom_call" | custom-call | tf_op jit(solution)/shard_map/ssd_back/pallas_call | solution.py:624
  225.0 0.9 slice.125
  225.9 1.3 collective-permute-start.1
  227.2 0.8 fusion.10
  228.0 4.0 %collective-permute-done.1.ahead_ref = bf16[16,1792]{1,0:T(8,128)(2,1)S(1)} collective-permute-done((bf16[16,1792]{1,0:T(8,128)(2,1)S(1)}, bf16[16,1792]{1,0:T(8,128)(2,1)S(1)}, u32[]{:S(2)}, u32[]{:S(2)}) %collective-permute-start.1) | collective-permute-done | bytes 57376 | tf_op jit(solution)/shard_map/ppermute | solution.py:44
  232.6 3.4 conv_back.1
  235.9 0.8 convert.25
  236.9 1.1 constant_dynamic-update-slice_fusion.3
  238.0 7.6 %multiply_reduce_fusion = (bf16[1024]{0:T(1024)(128)(2,1)S(1)}, f32[128]{0:T(128)S(1)}, f32[128,1024]{1,0:T(8,128)}) fusion(f32[144,1024]{1,0:T(8,128)S(1)} %get-tuple-element.95, f32[1024]{0:T(1024)S(1)} %get-tuple-element.101, bf16[128,4096]{1,0:T(8,128)(2,1)S(1)} %constant_dynamic-update-slice_fusion.2.grad_ref, ...), kind=kOutput, calls=%fused_computation.5 | convolution fusion | flops 1074396032 | bytes 10492416 | tf_op jit(solution)/shard_map/dot_general | solution.py:73
  246.3 3.5 all-to-all-start.6
  250.5 4.9 %all-to-all-done.6 = bf16[8,2,1024]{2,1,0:T(2,128)(2,1)S(1)} async-done(((bf16[8,2,1024]{2,1,0:T(2,128)(2,1)}), bf16[8,2,1024]{2,1,0:T(2,128)(2,1)S(1)}, u32[]{:S(2)}, u32[]{:S(2)}) %all-to-all-start.6) | async-done | bytes 32800 | tf_op jit(solution)/shard_map/all_to_all | solution.py:48
  255.5 6.4 %late_grads.1 = bf16[8,512,1024]{2,1,0:T(8,128)(2,1)} custom-call(bf16[128,1024]{1,0:T(8,128)(2,1)} %slice.151.shared_ref, bf16[128,4096]{1,0:T(8,128)(2,1)} %copy-done.2), custom_call_target="tpu_custom_call" | custom-call | tf_op jit(solution)/shard_map/late_grads/pallas_call | solution.py:668
  262.0 12.9 %all_to_all.61 = bf16[16,2,1024]{2,1,0:T(2,128)(2,1)S(1)} all-to-all(bf16[16,2,1024]{2,1,0:T(2,128)(2,1)S(1)} %broadcast_in_dim.48), channel_id=1, replica_groups=mesh['ctx'=16,'fsdp'=8] {'ctx'}, dimensions={0} | all-to-all | bytes 131072 | tf_op jit(solution)/shard_map/all_to_all | solution.py:48
  275.0 31.5 %all_to_all.62.parts_ref = bf16[16,64,1024]{2,1,0:T(8,128)(2,1)} all-to-all(bf16[16,64,1024]{2,1,0:T(8,128)(2,1)} %bitcast.67), channel_id=1, replica_groups=mesh['ctx'=16,'fsdp'=8] {'ctx'}, dimensions={0} | all-to-all | bytes 4194304 | tf_op jit(solution)/shard_map/all_to_all | solution.py:48
  306.5 3.9 fold.2
  310.4 3.8 all-to-all-start.9
  314.2 27.9 %all-to-all-done.9 = bf16[16,64,1024]{2,1,0:T(8,128)(2,1)S(1)} async-done(((bf16[16,64,1024]{2,1,0:T(8,128)(2,1)}), bf16[16,64,1024]{2,1,0:T(8,128)(2,1)S(1)}, u32[]{:S(2)}, u32[]{:S(2)}) %all-to-all-start.9) | async-done | bytes 2097184 | tf_op jit(solution)/shard_map/all_to_all | solution.py:48
  342.1 4.3 %all-to-all-start.10 = ((bf16[16,32,1024]{2,1,0:T(8,128)(2,1)}), bf16[16,32,1024]{2,1,0:T(8,128)(2,1)}, u32[]{:S(2)}, u32[]{:S(2)}) async-start(bf16[16,32,1024]{2,1,0:T(8,128)(2,1)} %bitcast.69), calls=%async_computation.12 | async-start | bytes 2097152 | tf_op jit(solution)/shard_map/all_to_all | solution.py:48
  346.5 14.7 %all-to-all-done.10.parts_ref = bf16[16,32,1024]{2,1,0:T(8,128)(2,1)} async-done(((bf16[16,32,1024]{2,1,0:T(8,128)(2,1)}), bf16[16,32,1024]{2,1,0:T(8,128)(2,1)}, u32[]{:S(2)}, u32[]{:S(2)}) %all-to-all-start.10) | async-done | bytes 1048608 | tf_op jit(solution)/shard_map/all_to_all | solution.py:48
  361.2 2.1 fold.3
  363.3 4.3 %all-to-all-start.11 = ((bf16[16,32,1024]{2,1,0:T(8,128)(2,1)}), bf16[16,32,1024]{2,1,0:T(8,128)(2,1)}, u32[]{:S(2)}, u32[]{:S(2)}) async-start(bf16[16,32,1024]{2,1,0:T(8,128)(2,1)} %fold.3), calls=%async_computation.13 | async-start | bytes 2097152 | tf_op jit(solution)/shard_map/all_to_all | solution.py:48
  367.7 2.0 add_bitcast_fusion
  370.9 1.0 slice.152
  371.9 1.1 slice.155
  373.7 1.5 copy.101
  375.8 6.6 %all-to-all-done.11.parts_ref = bf16[16,32,1024]{2,1,0:T(8,128)(2,1)} async-done(((bf16[16,32,1024]{2,1,0:T(8,128)(2,1)}), bf16[16,32,1024]{2,1,0:T(8,128)(2,1)}, u32[]{:S(2)}, u32[]{:S(2)}) %all-to-all-start.11) | async-done | bytes 1048608 | tf_op jit(solution)/shard_map/all_to_all | solution.py:48
  382.4 2.6 spread.1
  (107 shorter events, 13.0 us)
Async XLA Ops:
  7.2 2.6 copy-start.4
  7.2 6.3 %copy-start.17 = (bf16[224,4]{0,1:T(4,128)(2,1)S(1)}, bf16[224,4]{0,1:T(4,128)(2,1)}, u32[]{:S(2)}) copy-start(bf16[224,4]{0,1:T(4,128)(2,1)} %param.16) | copy-start | bytes 5380
  7.2 6.4 %copy-start.18 = (bf16[128]{0:T(256)(128)(2,1)S(1)}, bf16[128]{0:T(256)(128)(2,1)}, u32[]{:S(2)}) copy-start(bf16[128]{0:T(256)(128)(2,1)} %param.20) | copy-start | bytes 772
  7.2 6.4 %copy-start.19 = (bf16[128]{0:T(256)(128)(2,1)S(1)}, bf16[128]{0:T(256)(128)(2,1)}, u32[]{:S(2)}) copy-start(bf16[128]{0:T(256)(128)(2,1)} %param.14) | copy-start | bytes 772
  7.2 6.4 %copy-start.11 = (bf16[256,1024]{1,0:T(8,128)(2,1)S(1)}, bf16[256,1024]{1,0:T(8,128)(2,1)}, u32[]{:S(2)}) copy-start(bf16[256,1024]{1,0:T(8,128)(2,1)} %param.22) | copy-start | bytes 1572868
  7.2 12.5 %copy-start.15 = (f32[1,128,24]{1,2,0:T(8,128)S(1)}, f32[1,128,24]{1,2,0:T(8,128)}, u32[]{:S(2)}) copy-start(f32[1,128,24]{1,2,0:T(8,128)} %param.23) | copy-start | bytes 36868
  7.2 12.9 %copy-start.8 = (bf16[192,1024]{1,0:T(8,128)(2,1)S(1)}, bf16[192,1024]{1,0:T(8,128)(2,1)}, u32[]{:S(2)}) copy-start(bf16[192,1024]{1,0:T(8,128)(2,1)} %param.17) | copy-start | bytes 1179652
  7.3 61.8 %all-gather.4.cloned.1.call-start = ((), (), s32[]{:S(2)}) async-start(), calls=%async_computation.14 | async-start | bytes 9437184 | tf_op jit(solution)/shard_map/all_gather | solution.py:747
  9.7 11.2 %copy-start.12 = (bf16[64,1024]{1,0:T(8,128)(2,1)S(1)}, bf16[64,1024]{1,0:T(8,128)(2,1)}, u32[]{:S(2)}) copy-start(bf16[64,1024]{1,0:T(8,128)(2,1)} %param.19) | copy-start | bytes 393220
  9.8 31.8 %collective-permute-start = (bf16[16,1024]{1,0:T(8,128)(2,1)S(1)}, bf16[16,1024]{1,0:T(8,128)(2,1)S(1)}, u32[]{:S(2)}, u32[]{:S(2)}) collective-permute-start(bf16[16,1024]{1,0:T(8,128)(2,1)S(1)} %slice_bitcast_fusion.2), channel_id=1, source_target_pairs={{0,8},{8,16},{16,24},{24,32},{32,40},{40,48},{48,56},{56,64},{64,7... | collective-permute-start | bytes 98312 | tf_op jit(solution)/shard_map/ppermute | solution.py:44
  14.4 12.9 %all-to-all-start = ((bf16[8,32,512]{2,1,0:T(8,128)(2,1)}), bf16[8,32,512]{2,1,0:T(8,128)(2,1)S(1)}, u32[]{:S(2)}, u32[]{:S(2)}) async-start(bf16[8,32,512]{2,1,0:T(8,128)(2,1)} %broadcast_in_dim.19), calls=%async_computation | async-start | bytes 524288 | tf_op jit(solution)/shard_map/all_to_all | solution.py:48
  20.0 8.9 %copy-start.5 = (f32[128,24]{1,0:T(8,128)}, f32[128,24]{1,0:T(8,128)S(1)}, u32[]{:S(2)}) copy-start(f32[128,24]{1,0:T(8,128)S(1)} %reduce_window_sum.11.cum_ref) | copy-start | bytes 36868
  29.0 39.7 %all-to-all-start.1 = ((bf16[16,144,512]{2,1,0:T(8,128)(2,1)}), bf16[16,144,512]{2,1,0:T(8,128)(2,1)S(1)}, u32[]{:S(2)}, u32[]{:S(2)}) async-start(bf16[16,144,512]{2,1,0:T(8,128)(2,1)} %broadcast_in_dim.20), calls=%async_computation.1 | async-start | bytes 4718592 | tf_op jit(solution)/shard_map/all_to_all | solution.py:48
  35.7 108.8 %all-gather.6.cloned.1.call-start = ((), (), s32[]{:S(2)}) async-start(), calls=%async_computation.17 | async-start | bytes 16515072 | tf_op jit(solution)/shard_map/all_gather | solution.py:823
  41.7 28.9 %copy-start.14 = (f32[1,128,24]{1,2,0:T(8,128)S(1)}, f32[1,128,24]{1,2,0:T(8,128)}, u32[]{:S(2)}) copy-start(f32[1,128,24]{1,2,0:T(8,128)} %param.24) | copy-start | bytes 36868
  68.7 12.2 %copy-start.1 = (bf16[16,144,512]{2,1,0:T(8,128)(2,1)}, bf16[16,144,512]{2,1,0:T(8,128)(2,1)S(1)}, u32[]{:S(2)}) copy-start(bf16[16,144,512]{2,1,0:T(8,128)(2,1)S(1)} %all-to-all-done.1.down_hbm_ref) | copy-start | bytes 7077892
  87.2 22.6 %all-to-all-start.2 = ((bf16[16,352,128]{2,1,0:T(8,128)(2,1)}), bf16[16,352,128]{2,1,0:T(8,128)(2,1)S(1)}, u32[]{:S(2)}, u32[]{:S(2)}) async-start(bf16[16,352,128]{2,1,0:T(8,128)(2,1)} %get-tuple-element.58), calls=%async_computation.2 | async-start | bytes 2883584 | tf_op jit(solution)/shard_map/all_to_all | solution.py:48
  109.8 1.1 copy-start
  113.2 12.6 %all-to-all-start.3 = ((bf16[16,96,128]{2,1,0:T(8,128)(2,1)}), bf16[16,96,128]{2,1,0:T(8,128)(2,1)S(1)}, u32[]{:S(2)}, u32[]{:S(2)}) async-start(bf16[16,96,128]{2,1,0:T(8,128)(2,1)} %state_prefix.2), calls=%async_computation.3 | async-start | bytes 786432 | tf_op jit(solution)/shard_map/all_to_all | solution.py:48
  116.8 158.2 %reduce-scatter.3.cloned.1.call-start = ((), (), s32[]{:S(2)}) async-start(), calls=%async_computation.15 | async-start | bytes 18874368 | tf_op jit(solution)/shard_map/reduce_scatter | solution.py:852
  125.8 0.7 copy-start.3
  203.2 6.4 %copy-start.9 = (bf16[128,1536]{1,0:T(8,128)(2,1)S(1)}, bf16[128,1536]{1,0:T(8,128)(2,1)}, u32[]{:S(2)}) copy-start(bf16[128,1536]{1,0:T(8,128)(2,1)} %get-tuple-element.69) | copy-start | bytes 1179652
  205.5 13.1 %all-to-all-start.5 = ((bf16[16,96,128]{2,1,0:T(8,128)(2,1)}), bf16[16,96,128]{2,1,0:T(8,128)(2,1)S(1)}, u32[]{:S(2)}, u32[]{:S(2)}) async-start(bf16[16,96,128]{2,1,0:T(8,128)(2,1)} %state_prefix.3), calls=%async_computation.5 | async-start | bytes 786432 | tf_op jit(solution)/shard_map/all_to_all | solution.py:48
  218.7 0.7 copy-start.7
  225.0 13.0 %copy-start.10 = (bf16[128,768]{1,0:T(8,128)(2,1)S(1)}, bf16[128,768]{1,0:T(8,128)(2,1)}, u32[]{:S(2)}) copy-start(bf16[128,768]{1,0:T(8,128)(2,1)} %get-tuple-element.79) | copy-start | bytes 589828
  225.9 6.1 %collective-permute-start.1 = (bf16[16,1792]{1,0:T(8,128)(2,1)S(1)}, bf16[16,1792]{1,0:T(8,128)(2,1)S(1)}, u32[]{:S(2)}, u32[]{:S(2)}) collective-permute-start(bf16[16,1792]{1,0:T(8,128)(2,1)S(1)} %slice.125), channel_id=1, source_target_pairs={{8,0},{16,8},{24,16},{32,24},{40,32},{48,40},{56,48},{64,56},{72,6... | collective-permute-start | bytes 172040 | tf_op jit(solution)/shard_map/ppermute | solution.py:44
  232.0 0.6 copy-start.13
  238.0 7.6 %copy-start.2 = (bf16[128,4096]{1,0:T(8,128)(2,1)}, bf16[128,4096]{1,0:T(8,128)(2,1)S(1)}, u32[]{:S(2)}) copy-start(bf16[128,4096]{1,0:T(8,128)(2,1)S(1)} %constant_dynamic-update-slice_fusion.2.grad_ref) | copy-start | bytes 3145732
  246.3 9.2 %all-to-all-start.6 = ((bf16[8,2,1024]{2,1,0:T(2,128)(2,1)}), bf16[8,2,1024]{2,1,0:T(2,128)(2,1)S(1)}, u32[]{:S(2)}, u32[]{:S(2)}) async-start(bf16[8,2,1024]{2,1,0:T(2,128)(2,1)} %copy.97), calls=%async_computation.7 | async-start | bytes 65536 | tf_op jit(solution)/shard_map/all_to_all | solution.py:48
  249.8 64.4 %reduce-scatter.5.cloned.1.call-start = ((), (), s32[]{:S(2)}) async-start(), calls=%async_computation.16 | async-start | bytes 9437184 | tf_op jit(solution)/shard_map/reduce_scatter | solution.py:893
  310.4 31.7 %all-to-all-start.9 = ((bf16[16,64,1024]{2,1,0:T(8,128)(2,1)}), bf16[16,64,1024]{2,1,0:T(8,128)(2,1)S(1)}, u32[]{:S(2)}, u32[]{:S(2)}) async-start(bf16[16,64,1024]{2,1,0:T(8,128)(2,1)} %fold.2), calls=%async_computation.11 | async-start | bytes 4194304 | tf_op jit(solution)/shard_map/all_to_all | solution.py:48
  314.2 32.2 %copy-start.16 = (f32[144]{0:T(256)S(1)}, f32[144]{0:T(256)}, u32[]{:S(2)}) copy-start(f32[144]{0:T(256)} %add_rsqrt_fusion) | copy-start | bytes 1732
  342.1 19.2 %all-to-all-start.10 = ((bf16[16,32,1024]{2,1,0:T(8,128)(2,1)}), bf16[16,32,1024]{2,1,0:T(8,128)(2,1)}, u32[]{:S(2)}, u32[]{:S(2)}) async-start(bf16[16,32,1024]{2,1,0:T(8,128)(2,1)} %bitcast.69), calls=%async_computation.12 | async-start | bytes 2097152 | tf_op jit(solution)/shard_map/all_to_all | solution.py:48
  346.5 21.2 %copy-start.6 = (f32[128,1024]{1,0:T(8,128)S(1)}, f32[128,1024]{1,0:T(8,128)}, u32[]{:S(2)}) copy-start(f32[128,1024]{1,0:T(8,128)} %get-tuple-element.106) | copy-start | bytes 1572868
  363.3 19.1 %all-to-all-start.11 = ((bf16[16,32,1024]{2,1,0:T(8,128)(2,1)}), bf16[16,32,1024]{2,1,0:T(8,128)(2,1)}, u32[]{:S(2)}, u32[]{:S(2)}) async-start(bf16[16,32,1024]{2,1,0:T(8,128)(2,1)} %fold.3), calls=%async_computation.13 | async-start | bytes 2097152 | tf_op jit(solution)/shard_map/all_to_all | solution.py:48
Sparse Core Ops, SparseCore 0:
  10.4 52.4 all-gather.3
  70.7 73.7 all-gather.5
  164.7 92.6 reduce-scatter.2
  262.1 50.5 reduce-scatter.4

commit v3 on v2

--- a/solution.py
+++ b/solution.py
@@ -103,12 +103,33 @@
         store(row // STATE_ROWS, row % STATE_ROWS, block[1][32 * piece : 32 * (piece + 1)])
 
 
+def pack_rest_kernel(mout_ref, aout_ref, down_ref, gu_ref, out_ref):
+    out_ref[:192] = mout_ref[...]
+    out_ref[192:256] = aout_ref[...]
+    for block in range(3):
+        for part in range(8):
+            rows = slice(256 + 32 * block, 288 + 32 * block)
+            out_ref[rows, 128 * part : 128 * (part + 1)] = down_ref[
+                32 * part : 32 * (part + 1), 640 + 128 * block : 768 + 128 * block
+            ]
+    for block in range(4):
+        rows = slice(352 + 128 * block, 480 + 128 * block)
+        out_ref[rows] = gu_ref[:, D * block : D * (block + 1)]
+
+
+def pack_rest(w_mamba_out, w_attn_out, w_down, w_gate_up):
+    return pl.pallas_call(
+        pack_rest_kernel,
+        out_shape=struct((864, D), bf16),
+        compiler_params=params(),
+        name="pack_rest",
+    )(w_mamba_out, w_attn_out, w_down, w_gate_up)
+
+
 def enter_kernel(
     proj_ref,
     taps_ref,
-    cum_ref,
     cum_t_ref,
-    gate_ref,
     gate_t_ref,
     cos_ref,
     sin_ref,
@@ -152,8 +173,8 @@
     products = dot_last(inputs_c, inputs_b)
     row_ids = lax.broadcasted_iota(jnp.int32, (ROWS, ROWS), 0)
     causal = lanes() <= row_ids
-    cum = cum_ref[...]
-    remain_all = jnp.exp(cum[ROWS - 1 : ROWS] - cum) * gate_ref[...]
+    cum = cum_t_ref[...].T
+    remain_all = jnp.exp(cum[ROWS - 1 : ROWS] - cum) * gate_t_ref[...].T
 
     def store(to, row, value):
         sent_ref[to, row : row + 32] = value
@@ -173,7 +194,7 @@
         state_pieces((pair, state), store)
 
 
-def enter(projected, taps, cum, gates, cos, sin):
+def enter(projected, taps, cum_t, gate_t, cos, sin):
     return pl.pallas_call(
         enter_kernel,
         out_shape=(
@@ -187,7 +208,7 @@
         scratch_shapes=[pltpu.VMEM((ROWS + HALO, 256), f32)],
         compiler_params=params(),
         name="enter",
-    )(projected, taps, cum, cum.T, gates, gates.T, cos, sin)
+    )(projected, taps, cum_t, gate_t, cos, sin)
 
 
 def prefix_kernel(reverse, parts_ref, decay_ref, out_ref):
@@ -249,9 +270,9 @@
     )(first_row, queries, got)
 
 
-def leave_kernel(local_ref, starts_ref, act_ref, cum_ref, gating_ref, ssd_ref, mamba_ref):
+def leave_kernel(local_ref, starts_ref, act_ref, cum_t_ref, gating_ref, ssd_ref, mamba_ref):
     inputs_c = act_ref[...]
-    reach = jnp.exp(cum_ref[...])
+    reach = jnp.exp(cum_t_ref[...]).T
     starts = starts_ref[...].reshape(MI, NS)
     for pair in range(PAIRS):
         cols = slice(128 * pair, 128 * (pair + 1))
@@ -270,7 +291,7 @@
             whole((ROWS, MI)),
             whole((CTX, STATE_ROWS, NS)),
             pl.BlockSpec((ROWS, NS), lambda i: (0, (MI + NS) // NS)),
-            whole((ROWS, MIXER_HEADS)),
+            whole((MIXER_HEADS, ROWS)),
             whole((ROWS + HALO, MI)),
         ],
         out_specs=(whole((ROWS, MI)), whole((ROWS, MI))),
@@ -290,6 +311,7 @@
     gating_ref,
     rest_ref,
     down_hbm_ref,
+    middle_hbm_ref,
     output_ref,
     grad_residual_ref,
     branch_ref,
@@ -301,6 +323,7 @@
     mout_ref,
     aout_ref,
     left_ref,
+    mid_ref,
     right_ref,
     gu_ref,
     own_gu_ref,
@@ -319,19 +342,23 @@
     get_aout = fetch(192, 64, aout_ref, 1)
     get_gu = {}
     for order, block in enumerate((0, 2)):
-        get_gu[block] = fetch(384 + 128 * block, 128, gu_ref.at[block], 2 + order)
+        get_gu[block] = fetch(352 + 128 * block, 128, gu_ref.at[block], 2 + order)
     get_down = []
     for owner in range(OWNERS):
         source = down_hbm_ref.at[:, pl.ds(16 * owner, 16)]
-        get_down.append(pltpu.make_async_copy(source, left_ref.at[owner], sems.at[8 + owner]))
-    for side in range(2):
-        source = rest_ref.at[:, pl.ds(256, 128), pl.ds(512 * side, 512)]
-        target = right_ref.at[:, pl.ds(128 * side, 128)]
-        get_down.append(pltpu.make_async_copy(source, target, sems.at[6 + side]))
+        get_down.append(pltpu.make_async_copy(source, left_ref.at[owner], sems.at[6 + owner]))
+        source = middle_hbm_ref.at[:, pl.ds(16 * owner, 16)]
+        get_down.append(pltpu.make_async_copy(source, mid_ref.at[owner], sems.at[14 + owner]))
+    for block in range(3):
+        for part in range(8):
+            source = rest_ref.at[:, pl.ds(256 + 32 * block, 32), pl.ds(128 * part, 128)]
+            target = right_ref.at[:, pl.ds(32 * part, 32), pl.ds(128 * block, 128)]
+            sem = sems.at[22 + 8 * block + part]
+            get_down.append(pltpu.make_async_copy(source, target, sem))
     for copy in get_down:
         copy.start()
     for order, block in enumerate((1, 3)):
-        get_gu[block] = fetch(384 + 128 * block, 128, gu_ref.at[block], 4 + order)
+        get_gu[block] = fetch(352 + 128 * block, 128, gu_ref.at[block], 4 + order)
 
     get_mout.wait()
     mamba_out = dot(mamba_ref[...], mout_ref[...].reshape(MI, D))
@@ -366,10 +393,17 @@
         if half == 0:
             for copy in get_down:
                 copy.wait()
-        w_left = left_ref[4 * half : 4 * (half + 1)].reshape(D, 512)
-        w_right = right_ref[4 * half : 4 * (half + 1)].reshape(D, 512)
-        result = result + jnp.concatenate([dot(hidden, w_left), dot(hidden, w_right)], axis=1)
-        grad_hidden = dot_last(grad_out[:, :512], w_left) + dot_last(grad_out[:, 512:], w_right)
+        w_left = left_ref[4 * half : 4 * (half + 1)].reshape(D, 384)
+        w_right = right_ref[4 * half : 4 * (half + 1)].reshape(D, 384)
+        w_mid = mid_ref[4 * half : 4 * (half + 1)].reshape(D, 256)
+        result = result + jnp.concatenate(
+            [dot(hidden, w_left), dot(hidden, w_mid), dot(hidden, w_right)], axis=1
+        )
+        grad_hidden = (
+            dot_last(grad_out[:, :384], w_left)
+            + dot_last(grad_out[:, 384:640], w_mid)
+            + dot_last(grad_out[:, 640:], w_right)
+        )
         slope = logistic * (1.0 + gate * (1.0 - logistic))
         grad_gate = (grad_hidden * up * slope).astype(bf16)
         grad_up = (grad_hidden * active).astype(bf16)
@@ -409,7 +443,16 @@
 
 
 def middle(
-    mamba_in, attended, tokens, grad_out, gain, ssd_out, projected, rest_weights, down_weights
+    mamba_in,
+    attended,
+    tokens,
+    grad_out,
+    gain,
+    ssd_out,
+    projected,
+    rest_weights,
+    down_weights,
+    middle_weights,
 ):
     return pl.pallas_call(
         middle_kernel,
@@ -422,6 +465,7 @@
             whole((1, D)),
             whole((ROWS, MI)),
             whole((ROWS + HALO, MI)),
+            pl.BlockSpec(memory_space=pl.ANY),
             pl.BlockSpec(memory_space=pl.ANY),
             pl.BlockSpec(memory_space=pl.ANY),
         ],
@@ -448,14 +492,15 @@
         scratch_shapes=[
             pltpu.VMEM((OWNERS, 192, D), bf16),
             pltpu.VMEM((OWNERS, 64, D), bf16),
-            pltpu.VMEM((OWNERS, CTX, 16, 512), bf16),
-            pltpu.VMEM((OWNERS, 256, 512), bf16),
+            pltpu.VMEM((OWNERS, CTX, 16, 384), bf16),
+            pltpu.VMEM((OWNERS, CTX, 16, 256), bf16),
+            pltpu.VMEM((OWNERS, 256, 384), bf16),
             pltpu.VMEM((4, OWNERS, 128, D), bf16),
             pltpu.VMEM((2, OWNERS, 128, D), bf16),
             pltpu.VMEM((4, 256, D), bf16),
             pltpu.VMEM((OWNERS, 192, D), bf16),
             pltpu.VMEM((OWNERS, 64, D), bf16),
-            pltpu.SemaphoreType.DMA((8 + OWNERS,)),
+            pltpu.SemaphoreType.DMA((46,)),
             pltpu.SemaphoreType.DMA((5,)),
         ],
         compiler_params=params(),
@@ -470,6 +515,7 @@
         projected,
         rest_weights,
         down_weights,
+        middle_weights,
     )
 
 
@@ -481,7 +527,7 @@
     grad_attended_ref,
     grad_ssd_ref,
     inputs_c_ref,
-    cum_ref,
+    cum_t_ref,
     grad_query_ref,
     sent_ref,
 ):
@@ -519,7 +565,7 @@
         sent_ref[to, row : row + 32] = value
 
     inputs_c = inputs_c_ref[...]
-    reach = jnp.exp(cum_ref[...])
+    reach = jnp.exp(cum_t_ref[...]).T
     for pair in range(PAIRS):
         cols = slice(128 * pair, 128 * (pair + 1))
         scale = by_head(*(reach[:, head : head + 1] for head in (2 * pair, 2 * pair + 1)))
@@ -539,7 +585,7 @@
             whole((ROWS, Q_WIDTH)),
             whole((ROWS, MI)),
             pl.BlockSpec((ROWS, NS), lambda i: (0, (MI + NS) // NS)),
-            whole((ROWS, MIXER_HEADS)),
+            whole((MIXER_HEADS, ROWS)),
         ],
         out_specs=(whole((ROWS, Q_WIDTH)), whole((CTX, SENT_ROWS, NS))),
         out_shape=(struct((ROWS, Q_WIDTH), f32), struct((CTX, SENT_ROWS, NS), bf16)),
@@ -552,9 +598,8 @@
     grad_ssd_ref,
     act_ref,
     conv_out_ref,
-    cum_ref,
     cum_t_ref,
-    gate_ref,
+    gate_t_ref,
     starts_ref,
     ends_ref,
     grad_query_ref,
@@ -569,9 +614,9 @@
     products = dot_last(inputs_b, inputs_c)
     row_ids = lax.broadcasted_iota(jnp.int32, (ROWS, ROWS), 0)
     causal = row_ids <= lanes()
-    cum = cum_ref[...]
+    cum = cum_t_ref[...].T
     reach = jnp.exp(cum)
-    gates = gate_ref[...]
+    gates = gate_t_ref[...].T
     remain_all = jnp.exp(cum[ROWS - 1 : ROWS] - cum) * gates
     starts = starts_ref[...].reshape(MI, NS)
     ends = ends_ref[...].reshape(MI, NS)
@@ -620,13 +665,15 @@
         grad_a_ref[:, 128 * part : 128 * (part + 1)] = values.astype(bf16)
 
 
-def ssd_back(grad_ssd, activated, conv_out, cum, gates, starts, ends, grad_query, got, cos, sin):
+def ssd_back(
+    grad_ssd, activated, conv_out, cum_t, gate_t, starts, ends, grad_query, got, cos, sin
+):
     return pl.pallas_call(
         ssd_back_kernel,
         out_shape=(struct((ROWS, XBC), bf16), struct((ROWS, QKV), bf16)),
         compiler_params=params(),
         name="ssd_back",
-    )(grad_ssd, activated, conv_out, cum, cum.T, gates, starts, ends, grad_query, got, cos, sin)
+    )(grad_ssd, activated, conv_out, cum_t, gate_t, starts, ends, grad_query, got, cos, sin)
 
 
 def conv_back_kernel(grad_ref, ahead_ref, conv_in_ref, taps_ref, out_ref, grad_taps_ref, ext_ref, in_ref):
@@ -676,25 +723,73 @@
     )(shared, grad_proj)
 
 
-def fold_kernel(parts_ref, out_ref):
+def summed(parts_ref):
     total = parts_ref[0].astype(f32)
     for part in range(1, CTX):
         total = total + parts_ref[part].astype(f32)
-    low = total.astype(bf16)
+    return total.astype(bf16)
+
+
+def early_fold_kernel(parts_ref, small_ref, out_ref):
+    out_ref[:64] = summed(parts_ref)
+    out_ref[64:] = small_ref[...]
+
+
+def early_fold(parts, small):
+    return pl.pallas_call(
+        early_fold_kernel,
+        out_shape=struct((80, D), bf16),
+        compiler_params=params(),
+        name="early_fold",
+    )(parts, small)
+
+
+def fold_kernel(parts_ref, out_ref):
+    low = summed(parts_ref)
     for to in range(CTX):
         out_ref[to] = low
 
 
 def fold(parts):
-    rows = parts.shape[1]
     return pl.pallas_call(
         fold_kernel,
-        grid=(rows // 16,),
-        in_specs=[pl.BlockSpec((CTX, 16, D), lambda i: (0, i, 0))],
-        out_specs=pl.BlockSpec((CTX, 16, D), lambda i: (0, i, 0)),
         out_shape=struct(parts.shape, bf16),
         compiler_params=params(),
         name="fold",
+    )(parts)
+
+
+def early_spread_kernel(parts_ref, mout_ref, aout_ref, down_ref, gu_ref, small_ref):
+    for part in range(CTX):
+        values = parts_ref[part, :64].astype(f32)
+        if part < 3:
+            mout_ref[64 * part : 64 * (part + 1)] = values
+        elif part < 4:
+            aout_ref[...] = values
+        elif part < 8:
+            down_ref[64 * (part - 4) : 64 * (part - 3)] = values
+        else:
+            at = D * ((part - 8) // 2)
+            row = 64 * (part % 2)
+            gu_ref[row : row + 64, at : at + D] = values
+    total = parts_ref[0, 64:].astype(f32)
+    for part in range(1, CTX):
+        total = total + parts_ref[part, 64:].astype(f32)
+    small_ref[...] = total
+
+
+def early_spread(parts):
+    return pl.pallas_call(
+        early_spread_kernel,
+        out_shape=(
+            struct((192, D), f32),
+            struct((64, D), f32),
+            struct((256, D), f32),
+            struct((ROWS, 2 * FF), f32),
+            struct((16, D), f32),
+        ),
+        compiler_params=params(),
+        name="early_spread",
     )(parts)
 
 
@@ -715,10 +810,6 @@
         compiler_params=params(),
         name="spread",
     )(parts)
-
-
-def widened(blocks):
-    return blocks.reshape(4, ROWS, D).transpose(1, 0, 2).reshape(ROWS, 4 * D)
 
 
 def on_device(
@@ -737,8 +828,8 @@
     grad_out,
 ):
     tokens = tokens[0]
-    decays = decays[0]
-    input_gates = input_gates[0]
+    decays = decays[0].T
+    input_gates = input_gates[0].T
     grad_out = grad_out[0]
     ctx_index = lax.axis_index("ctx")
     offset = ctx_index * ROWS
@@ -747,36 +838,28 @@
     first_weights = lax.all_gather(
         jnp.concatenate([w_mamba_in, w_qkv], axis=1), "fsdp", axis=0, tiled=True
     )
-    rest = jnp.concatenate(
-        [
-            w_mamba_out,
-            w_attn_out,
-            jnp.concatenate([w_down[:128, 512:], w_down[128:, 512:]], axis=1),
-        ]
-        + [w_gate_up[:, D * block : D * (block + 1)] for block in range(4)],
-        axis=0,
-    )
+    rest = pack_rest(w_mamba_out, w_attn_out, w_down, w_gate_up)
     small = jnp.concatenate(
-        [gain_one, gain_two, conv_weight.T.reshape(-1), jnp.zeros((7 * D - 128,), bf16)]
-    )
-    piece = lax.dynamic_slice(w_down, (ctx_index * 16, 0), (16, 512))
-    piece = jnp.concatenate([piece, small.reshape(16, 512)], axis=0)
-    pieces = swap(jnp.broadcast_to(piece[None], (OWNERS, 32, 512)), "fsdp")
-    small_all = pieces[:, 16:19].reshape(OWNERS, 3 * 512)[:, :1152]
+        [gain_one, gain_two, conv_weight.T.reshape(-1), jnp.zeros((16 * 640 - 1152,), bf16)]
+    )
+    piece = lax.dynamic_slice(w_down, (ctx_index * 16, 0), (16, 640))
+    piece = jnp.concatenate([piece, small.reshape(16, 640)], axis=0)
+    pieces = swap(jnp.broadcast_to(piece[None], (OWNERS, 32, 640)), "fsdp")
+    small_all = pieces[:, 16:18].reshape(OWNERS, 1280)[:, :1152]
     gain_first = small_all[:, :128].reshape(1, D).astype(f32)
     gain_second = small_all[:, 128:256].reshape(1, D).astype(f32)
     conv_taps = small_all[:, 256:].reshape(OWNERS, CONV, XBC // OWNERS).transpose(1, 0, 2)
     conv_taps = conv_taps.reshape(CONV, XBC).astype(f32)
 
-    cumulative = jnp.cumsum(jnp.log(decays), axis=0)
-    whole_decay = jnp.exp(cumulative[-1:])
+    cumulative = jnp.cumsum(jnp.log(decays), axis=1)
+    whole_decay = jnp.exp(cumulative[:, -1])[None]
     decay_parts = []
     for _ in range(3):
         decay_parts.append(whole_decay.astype(bf16))
         whole_decay = whole_decay - decay_parts[-1].astype(f32)
-    decay_parts = jnp.pad(jnp.concatenate(decay_parts, axis=1), ((0, 15), (0, 512 - 72)))
-    sent_down = jnp.concatenate([pieces[:, :16].reshape(ROWS, 512), decay_parts], axis=0)
-    down_weights = swap(jnp.broadcast_to(sent_down[None], (CTX, ROWS + 16, 512)), "ctx")
+    decay_parts = jnp.pad(jnp.concatenate(decay_parts, axis=1), ((0, 15), (0, 384 - 72)))
+    sent_down = jnp.concatenate([pieces[:, :16, :384].reshape(ROWS, 384), decay_parts], axis=0)
+    down_weights = swap(jnp.broadcast_to(sent_down[None], (CTX, ROWS + 16, 384)), "ctx")
     decay_parts = down_weights[:, ROWS, :72].astype(f32)
     decays_all = decay_parts[:, :24] + decay_parts[:, 24:48] + decay_parts[:, 48:]
     decay_rows = lax.dynamic_slice_in_dim(
@@ -791,10 +874,10 @@
     inverse_one = inverse_ext[HALO:]
     normed, shared = normed_ext[HALO:], shared_ext[HALO:]
 
-    half_dim = HD // 2
-    frequency = jnp.exp(-jnp.log(rope_base) * (2.0 * jnp.arange(half_dim).astype(f32) / HD))
+    pair_index = jnp.remainder(jnp.arange(128), HD // 2).astype(f32)
+    frequency = jnp.exp(-jnp.log(rope_base) * (2.0 * pair_index / HD))
     positions = (offset + jnp.arange(ROWS)).astype(f32)
-    angles = jnp.tile(positions[:, None] * frequency[None, :], (1, 4))
+    angles = positions[:, None] * frequency[None, :]
     cosine, sine = jnp.cos(angles), jnp.sin(angles)
 
     (
@@ -807,6 +890,7 @@
         cumulative,
         rest,
         down_weights,
+        pieces,
     ) = lax.optimization_barrier(
         (
             first_weights,
@@ -818,8 +902,11 @@
             cumulative,
             rest,
             down_weights,
+            pieces,
         )
     )
+    sent_middle = jnp.broadcast_to(pieces[None, :, :16, 384:], (CTX, OWNERS, 16, 256))
+    middle_weights = swap(sent_middle.reshape(CTX, ROWS, 256), "ctx")
     rest_weights = lax.all_gather(rest, "fsdp", axis=0, tiled=False)
     projected = dot(shared_ext, first_weights)
     conv_in, conv_out, activated, local_out, queries, sent = enter(
@@ -848,6 +935,7 @@
         projected,
         rest_weights,
         down_weights,
+        middle_weights,
     )
     early_share = lax.psum_scatter(
         early, "fsdp", scatter_dimension=0, tiled=True
@@ -888,30 +976,30 @@
         axis=1,
     ).astype(bf16).reshape(OWNERS, 2, D)
     small_got = jnp.sum(swap(small_grads, "fsdp").astype(f32), axis=0).astype(bf16)
-    small_got, grad_proj = lax.optimization_barrier((small_got, grad_proj))
-    small_sum = swap(jnp.broadcast_to(small_got[None], (CTX, 2, D)), "ctx").astype(f32)
     late_share = lax.psum_scatter(
         late_grads(shared, grad_proj), "fsdp", scatter_dimension=0, tiled=True
     )[0]
-    early_share, small_sum = lax.optimization_barrier((early_share, jnp.sum(small_sum, axis=0)))
+    early_share, small_got = lax.optimization_barrier((early_share, small_got))
     early_got = swap(early_share.reshape(CTX, 64, D), "ctx")
-    early_sum = swap(fold(early_got), "ctx")
-    late_share, early_sum = lax.optimization_barrier((late_share, early_sum))
+    small_rows = jnp.concatenate([small_got, jnp.zeros((14, D), bf16)], axis=0)
+    early_mine = early_fold(early_got, small_rows)
+    late_share, early_mine = lax.optimization_barrier((late_share, early_mine))
+    early_sum = lax.all_gather(early_mine, "ctx", axis=0, tiled=False)
     late_sum = swap(fold(swap(late_share.reshape(CTX, 32, D), "ctx")), "ctx")
+    grad_mout, grad_aout, grad_down, grad_gate_up, small_sum = early_spread(early_sum)
     grad_in, grad_qkv = spread(late_sum)
-    early_sum = early_sum.reshape(D, D).astype(f32)
     return (
         output[None],
         grad_tokens[None],
         small_sum[0, :128],
         grad_in,
         small_sum[0, 128:].reshape(CONV, XBC // OWNERS).T,
-        early_sum[:192],
+        grad_mout,
         grad_qkv,
-        early_sum[192:256],
+        grad_aout,
         small_sum[1, :128],
-        widened(early_sum[512:]),
-        early_sum[256:512],
+        grad_gate_up,
+        grad_down,
     )
 
 

time: 399 us -> 383 us (0.960)
  the two profiles are of different devices: /device:TPU:0 before, /device:TPU:38 now
where the time goes in v3:
time: 383 us; the launch traced here: 376 us
  waiting for transfers between devices  125 us (33%)
  Pallas kernels  80.7 us (21%)
  blocking collectives  60 us (16%)
  starting transfers between devices  57.3 us (15%)
  local copies, waits for them, and re-layouts  20.6 us (5%)
  between operations  14.6 us (4%)
  matrix products  12.7 us (3%)
  other arithmetic  5.72 us (1%)
    all_to_all x8, waiting for transfers between devices, swap(): return lax.all_to_all(value, axis, 0, 0, tiled=True)  90.7 us
    all_to_all x3, blocking collectives, swap(): return lax.all_to_all(value, axis, 0, 0, tiled=True)  60 us
    all_to_all x8, starting transfers between devices, swap(): return lax.all_to_all(value, axis, 0, 0, tiled=True)  50.5 us
    pallas_call x1, Pallas kernels, middle(): pl.pallas_call(middle_kernel, grid=(1,), in_specs=[whole((ROWS, MI)), who...  20 us
    ppermute x2, waiting for transfers between devices, passed_along(): lax.ppermute(value, axis, [(source, source + steps) for source in range(l...  19.1 us
    reduce_scatter x1, waiting for transfers between devices, on_device(): lax.psum_scatter(late_grads(shared, grad_proj), 'fsdp', scatter_dimension...  11.7 us
    pallas_call x1, Pallas kernels, attend_back(): pl.pallas_call(attend_back_kernel, grid=(1,), in_specs=[pl.BlockSpec(memo...  10.2 us
    unnamed x44, local copies, waits for them, and re-layouts  7.89 us
  transfers between devices with their start and end apart: 15, of which 12 were waited for; matrix products, arithmetic and copies ran while one was open for 7% of the time, Pallas kernels for 15%

profile of v3, /device:TPU:38, one launch (start us, length us, event | category | flops | bytes accessed | tf_op | source)
XLA Modules:
  0.0 376.4 jit_solution(14808932593098340851)
XLA Ops:
  7.3 2.3 pad_maximum_fusion
  9.8 0.7 constant_dynamic-slice_fusion
  10.6 0.8 broadcast_in_dim.21
  11.3 5.4 %all-to-all-start = ((bf16[8,32,640]{2,1,0:T(8,128)(2,1)}), bf16[8,32,640]{2,1,0:T(8,128)(2,1)S(1)}, u32[]{:S(2)}, u32[]{:S(2)}) async-start(bf16[8,32,640]{2,1,0:T(8,128)(2,1)} %broadcast_in_dim.21), calls=%async_computation | async-start | bytes 655360 | tf_op jit(solution)/shard_map/all_to_all | solution.py:48
  17.3 6.2 %all-to-all-done = bf16[8,32,640]{2,1,0:T(8,128)(2,1)S(1)} async-done(((bf16[8,32,640]{2,1,0:T(8,128)(2,1)}), bf16[8,32,640]{2,1,0:T(8,128)(2,1)S(1)}, u32[]{:S(2)}, u32[]{:S(2)}) %all-to-all-start) | async-done | bytes 327712 | tf_op jit(solution)/shard_map/all_to_all | solution.py:48
  23.6 1.4 broadcast_in_dim.22
  24.9 7.6 %all-to-all-start.1 = ((bf16[16,144,384]{2,1,0:T(8,128)(2,1)}), bf16[16,144,384]{2,1,0:T(8,128)(2,1)S(1)}, u32[]{:S(2)}, u32[]{:S(2)}) async-start(bf16[16,144,384]{2,1,0:T(8,128)(2,1)} %broadcast_in_dim.22), calls=%async_computation.1 | async-start | bytes 3538944 | tf_op jit(solution)/shard_map/all_to_all | solution.py:48
  32.5 3.4 collective-permute-start
  36.0 1.0 multiply_sine_fusion
  36.9 3.0 pack_rest.1
  39.9 16.1 %collective-permute-done = bf16[16,1024]{1,0:T(8,128)(2,1)S(1)} collective-permute-done((bf16[16,1024]{1,0:T(8,128)(2,1)S(1)}, bf16[16,1024]{1,0:T(8,128)(2,1)S(1)}, u32[]{:S(2)}, u32[]{:S(2)}) %collective-permute-start) | collective-permute-done | bytes 32800 | tf_op jit(solution)/shard_map/ppermute | solution.py:44
  56.3 0.7 reshape.206.taps_ref
  58.1 3.2 all-gather.6.cloned.1.call-done
  61.3 6.2 %fusion.17.proj_ref.gating_ref = f32[144,4096]{1,0:T(8,128)} fusion(bf16[144,1024]{1,0:T(8,128)(2,1)S(1)} %get-tuple-element.55, bf16[1024,4096]{1,0:T(8,128)(2,1)} %all-gather.6.cloned.1.call-done), kind=kOutput, calls=%fused_computation.61 | convolution fusion | flops 1207959552 | bytes 11042816 | tf_op jit(solution)/shard_map/dot_general | solution.py:69
  67.6 5.9 %enter.1 = (bf16[144,1792]{1,0:T(8,128)(2,1)}, f32[128,1792]{1,0:T(8,128)}, bf16[128,1792]{1,0:T(8,128)(2,1)}, f32[128,1536]{1,0:T(8,128)}, bf16[1024,128]{1,0:T(8,128)(2,1)}, /*index=5*/bf16[16,352,128]{2,1,0:T(8,128)(2,1)}) custom-call(f32[144,4096]{1,0:T(8,128)} %fusion.17.proj_ref.gating_ref, f32[4,1792]{1,0:T(4,128)} %reshape.206.taps_ref, ...), custom_call_target="tpu_custom_call" | custom-call | tf_op jit(solution)/shard_map/enter/pallas_call | solution.py:198
  73.4 7.3 %all-to-all-start.2 = ((bf16[16,352,128]{2,1,0:T(8,128)(2,1)}), bf16[16,352,128]{2,1,0:T(8,128)(2,1)S(1)}, u32[]{:S(2)}, u32[]{:S(2)}) async-start(bf16[16,352,128]{2,1,0:T(8,128)(2,1)} %get-tuple-element.62), calls=%async_computation.2 | async-start | bytes 2883584 | tf_op jit(solution)/shard_map/all_to_all | solution.py:48
  80.7 1.3 copy.31.decay_ref
  82.0 19.2 %all-to-all-done.2.parts_ref.got_ref = bf16[16,352,128]{2,1,0:T(8,128)(2,1)S(1)} async-done(((bf16[16,352,128]{2,1,0:T(8,128)(2,1)}), bf16[16,352,128]{2,1,0:T(8,128)(2,1)S(1)}, u32[]{:S(2)}, u32[]{:S(2)}) %all-to-all-start.2) | async-done | bytes 1441824 | tf_op jit(solution)/shard_map/all_to_all | solution.py:48
  101.1 1.1 copy-done
  102.2 2.3 state_prefix.2
  104.5 6.2 %all-to-all-start.3 = ((bf16[16,96,128]{2,1,0:T(8,128)(2,1)}), bf16[16,96,128]{2,1,0:T(8,128)(2,1)S(1)}, u32[]{:S(2)}, u32[]{:S(2)}) async-start(bf16[16,96,128]{2,1,0:T(8,128)(2,1)} %state_prefix.2), calls=%async_computation.3 | async-start | bytes 786432 | tf_op jit(solution)/shard_map/all_to_all | solution.py:48
  110.7 7.3 %all-to-all-done.3.starts_ref = bf16[16,96,128]{2,1,0:T(8,128)(2,1)S(1)} async-done(((bf16[16,96,128]{2,1,0:T(8,128)(2,1)}), bf16[16,96,128]{2,1,0:T(8,128)(2,1)S(1)}, u32[]{:S(2)}, u32[]{:S(2)}) %all-to-all-start.3) | async-done | bytes 393248 | tf_op jit(solution)/shard_map/all_to_all | solution.py:48
  117.9 1.1 broadcast_in_dim.50
  119.0 5.6 %all-to-all-start.4 = ((bf16[16,128,256]{2,1,0:T(8,128)(2,1)}), bf16[16,128,256]{2,1,0:T(8,128)(2,1)S(1)}, u32[]{:S(2)}, u32[]{:S(2)}) async-start(bf16[16,128,256]{2,1,0:T(8,128)(2,1)} %broadcast_in_dim.50), calls=%async_computation.4 | async-start | bytes 2097152 | tf_op jit(solution)/shard_map/all_to_all | solution.py:48
  124.8 6.6 %attend.1 = (bf16[128,512]{1,0:T(8,128)(2,1)}, f32[2,8,512]{2,1,0:T(8,128)}) custom-call(s32[1]{0:T(128)} %bitcast.12.first_row_ref, bf16[1024,128]{1,0:T(8,128)(2,1)} %get-tuple-element.66.query_ref, bf16[16,352,128]{2,1,0:T(8,128)(2,1)} %copy-done), custom_call_target="tpu_custom_call" | custom-call | tf_op jit(solution)/shard_map/attend/pallas_call | solution.py:260
  131.4 3.4 leave.1
  134.8 2.6 all-to-all-done.4.middle_hbm_ref
  137.5 0.9 copy-done.5
  138.4 20.0 %middle.1 = (bf16[128,1024]{1,0:T(8,128)(2,1)}, f32[128,1024]{1,0:T(8,128)}, bf16[128,1024]{1,0:T(8,128)(2,1)}, f32[8,1024]{1,0:T(8,128)}, bf16[128,512]{1,0:T(8...) custom-call(bf16[128,1536]{1,0:T(8,128)(2,1)} %get-tuple-element.65.mamba_ref, ...), custom_call_target="tpu_custom_call" | custom-call | tf_op jit(solution)/shard_map/middle/pallas_call | solution.py:457
  158.5 10.2 %attend_back.1 = (f32[128,512]{1,0:T(8,128)}, bf16[16,352,128]{2,1,0:T(8,128)(2,1)}) custom-call(s32[1]{0:T(128)} %bitcast.12.first_row_ref, bf16[1024,128]{1,0:T(8,128)(2,1)} %get-tuple-element.66.query_ref, bf16[16,352,128]{2,1,0:T(8,128)(2,1)} %copy-done, f32[2,8,512]{2,1,0:T(8,128)} %get-tuple-element.77.total_ref, ...), custom_call_target="tpu_custom_call" | custom-call | tf_op jit(solution)/shard_map/attend_back/pallas_call | solution.py:577
  168.7 26.1 %all_to_all.55.parts_ref.got_ref = bf16[16,352,128]{2,1,0:T(8,128)(2,1)} all-to-all(bf16[16,352,128]{2,1,0:T(8,128)(2,1)} %get-tuple-element.79), channel_id=1, replica_groups=mesh['ctx'=16,'fsdp'=8] {'ctx'}, dimensions={0} | all-to-all | bytes 2883584 | tf_op jit(solution)/shard_map/all_to_all | solution.py:48
  194.8 2.3 state_prefix.3
  197.1 5.6 %all-to-all-start.6 = ((bf16[16,96,128]{2,1,0:T(8,128)(2,1)}), bf16[16,96,128]{2,1,0:T(8,128)(2,1)S(1)}, u32[]{:S(2)}, u32[]{:S(2)}) async-start(bf16[16,96,128]{2,1,0:T(8,128)(2,1)} %state_prefix.3), calls=%async_computation.6 | async-start | bytes 786432 | tf_op jit(solution)/shard_map/all_to_all | solution.py:48
  202.8 0.7 slice.101.shared_ref
  203.5 6.5 %all-to-all-done.6.ends_ref = bf16[16,96,128]{2,1,0:T(8,128)(2,1)S(1)} async-done(((bf16[16,96,128]{2,1,0:T(8,128)(2,1)}), bf16[16,96,128]{2,1,0:T(8,128)(2,1)S(1)}, u32[]{:S(2)}, u32[]{:S(2)}) %all-to-all-start.6) | async-done | bytes 393248 | tf_op jit(solution)/shard_map/all_to_all | solution.py:48
  210.0 0.7 copy-done.9
  210.8 5.8 %ssd_back.1 = (bf16[128,1792]{1,0:T(8,128)(2,1)}, bf16[128,768]{1,0:T(8,128)(2,1)}) custom-call(bf16[128,1536]{1,0:T(8,128)(2,1)} %get-tuple-element.75.grad_ssd_ref, bf16[128,1792]{1,0:T(8,128)(2,1)} %get-tuple-element.64.act_ref.inputs_c_ref, f32[128,1792]{1,0:T(8,128)} %get-tuple-element.76.conv_out_ref, f32[24,128]{1,0:T(8,128)} %copy-done.11, ...), custom_call_target="tpu_custom_call" | custom-call | tf_op jit(solution)/shard_map/ssd_back/pallas_call | solution.py:671
  216.6 0.9 slice.83
  217.4 3.0 collective-permute-start.1
  220.5 3.0 collective-permute-done.1.ahead_ref
  224.1 3.4 conv_back.1
  227.5 1.1 constant_dynamic-update-slice_fusion.1
  228.6 1.0 copy-done.3
  229.5 6.4 %late_grads.1 = bf16[8,512,1024]{2,1,0:T(8,128)(2,1)} custom-call(bf16[128,1024]{1,0:T(8,128)(2,1)} %slice.101.shared_ref, bf16[128,4096]{1,0:T(8,128)(2,1)} %copy-done.3), custom_call_target="tpu_custom_call" | custom-call | tf_op jit(solution)/shard_map/late_grads/pallas_call | solution.py:715
  236.1 0.9 fusion.11
  237.3 6.5 %multiply_reduce_fusion = (bf16[1024]{0:T(1024)(128)(2,1)S(1)}, f32[128]{0:T(128)S(1)}, f32[128,1024]{1,0:T(8,128)S(1)}) fusion(f32[144,1024]{1,0:T(8,128)S(1)} %get-tuple-element.101, f32[1024]{0:T(1024)S(1)} %get-tuple-element.106, bf16[128,4096]{1,0:T(8,128)(2,1)S(1)} %copy-done.4, bf16[1024,4096]{1,0:T(8,128)(2,1)} %all-gather.6.cloned.1.call-done), kind=kOutput, calls=%fused_computation.5 | convolution fusion | flops 1074396032 | bytes 10492416 | tf_op jit(solution)/shard_map/dot_general | solution.py:73
  243.8 8.4 %all_to_all.56 = bf16[8,2,1024]{2,1,0:T(2,128)(2,1)S(1)} all-to-all(bf16[8,2,1024]{2,1,0:T(2,128)(2,1)S(1)} %copy.34), channel_id=1, replica_groups=mesh['ctx'=16,'fsdp'=8] {'fsdp'}, dimensions={0} | all-to-all | bytes 65536 | tf_op jit(solution)/shard_map/all_to_all | solution.py:48
  252.3 7.3 %all-to-all-start.8 = ((bf16[16,64,1024]{2,1,0:T(8,128)(2,1)}), bf16[16,64,1024]{2,1,0:T(8,128)(2,1)S(1)}, u32[]{:S(2)}, u32[]{:S(2)}) async-start(bf16[16,64,1024]{2,1,0:T(8,128)(2,1)} %bitcast.72), calls=%async_computation.10 | async-start | bytes 4194304 | tf_op jit(solution)/shard_map/all_to_all | solution.py:48
  259.7 0.6 concatenate.36.small_ref
  260.3 26.9 %all-to-all-done.8.parts_ref = bf16[16,64,1024]{2,1,0:T(8,128)(2,1)S(1)} async-done(((bf16[16,64,1024]{2,1,0:T(8,128)(2,1)}), bf16[16,64,1024]{2,1,0:T(8,128)(2,1)S(1)}, u32[]{:S(2)}, u32[]{:S(2)}) %all-to-all-start.8) | async-done | bytes 2097184 | tf_op jit(solution)/shard_map/all_to_all | solution.py:48
  287.2 1.3 copy-done.1
  288.5 2.6 early_fold.1
  291.1 11.7 %reduce-scatter.3.cloned.1.call-done = bf16[1,512,1024]{2,1,0:T(8,128)(2,1)} async-done(((bf16[8,512,1024]{2,1,0:T(8,128)(2,1)}), bf16[1,512,1024]{2,1,0:T(8,128)(2,1)}) %reduce-scatter.3.cloned.1.call-update) | async-done | bytes 1048592 | tf_op jit(solution)/shard_map/reduce_scatter | solution.py:979
  302.8 25.5 %all_to_all.57.parts_ref = bf16[16,32,1024]{2,1,0:T(8,128)(2,1)} all-to-all(bf16[16,32,1024]{2,1,0:T(8,128)(2,1)} %bitcast.73), channel_id=1, replica_groups=mesh['ctx'=16,'fsdp'=8] {'ctx'}, dimensions={0} | all-to-all | bytes 2097152 | tf_op jit(solution)/shard_map/all_to_all | solution.py:48
  328.3 2.4 fold.1
  330.7 5.6 %all-to-all-start.10 = ((bf16[16,32,1024]{2,1,0:T(8,128)(2,1)}), bf16[16,32,1024]{2,1,0:T(8,128)(2,1)S(1)}, u32[]{:S(2)}, u32[]{:S(2)}) async-start(bf16[16,32,1024]{2,1,0:T(8,128)(2,1)} %fold.1), calls=%async_computation.12 | async-start | bytes 2097152 | tf_op jit(solution)/shard_map/all_to_all | solution.py:48
  336.4 1.0 add_bitcast_fusion
  337.4 21.9 %all-to-all-done.10.parts_ref = bf16[16,32,1024]{2,1,0:T(8,128)(2,1)S(1)} async-done(((bf16[16,32,1024]{2,1,0:T(8,128)(2,1)}), bf16[16,32,1024]{2,1,0:T(8,128)(2,1)S(1)}, u32[]{:S(2)}, u32[]{:S(2)}) %all-to-all-start.10) | async-done | bytes 1048608 | tf_op jit(solution)/shard_map/all_to_all | solution.py:48
  359.3 1.0 copy-done.6
  360.3 2.6 spread.1
  362.9 3.8 %early_spread.1 = (f32[192,1024]{1,0:T(8,128)}, f32[64,1024]{1,0:T(8,128)}, f32[256,1024]{1,0:T(8,128)}, f32[128,4096]{1,0:T(8,128)}, f32[16,1024]{1,0:T(8,128)}) custom-call(bf16[16,80,1024]{2,1,0:T(8,128)(2,1)} %bitcast.68), custom_call_target="tpu_custom_call" | custom-call | tf_op jit(solution)/shard_map/early_spread/pallas_call | solution.py:782
  366.7 1.3 slice_bitcast_fusion.3
  368.0 0.8 slice_reduce_fusion
  368.7 0.7 reshape_squeeze.8
  (92 shorter events, 3.9 us)
Async XLA Ops:
  7.2 2.5 copy-start.17
  7.2 2.6 copy-start.18
  7.2 2.6 copy-start.19
  7.2 9.5 %copy-start.16 = (f32[1,128,24]{1,2,0:T(8,128)S(1)}, f32[1,128,24]{1,2,0:T(8,128)}, u32[]{:S(2)}) copy-start(f32[1,128,24]{1,2,0:T(8,128)} %param.23) | copy-start | bytes 36868
  7.2 54.1 %all-gather.6.cloned.1.call-start = ((), (), s32[]{:S(2)}) async-start(), calls=%async_computation.13 | async-start | bytes 9437184 | tf_op jit(solution)/shard_map/all_gather | solution.py:838
  11.3 12.2 %all-to-all-start = ((bf16[8,32,640]{2,1,0:T(8,128)(2,1)}), bf16[8,32,640]{2,1,0:T(8,128)(2,1)S(1)}, u32[]{:S(2)}, u32[]{:S(2)}) async-start(bf16[8,32,640]{2,1,0:T(8,128)(2,1)} %broadcast_in_dim.21), calls=%async_computation | async-start | bytes 655360 | tf_op jit(solution)/shard_map/all_to_all | solution.py:48
  17.0 7.9 %copy-start.11 = (f32[24,128]{1,0:T(8,128)}, f32[24,128]{1,0:T(8,128)S(1)}, u32[]{:S(2)}) copy-start(f32[24,128]{1,0:T(8,128)S(1)} %reduce_window_sum.11.cum_t_ref) | copy-start | bytes 36868
  24.9 7.6 %copy-start.8 = (bf16[1,128,1024]{2,1,0:T(8,128)(2,1)S(1)}, bf16[1,128,1024]{2,1,0:T(8,128)(2,1)}, u32[]{:S(2)}) copy-start(bf16[1,128,1024]{2,1,0:T(8,128)(2,1)} %param.13) | copy-start | bytes 786436
  24.9 32.8 %all-to-all-start.1 = ((bf16[16,144,384]{2,1,0:T(8,128)(2,1)}), bf16[16,144,384]{2,1,0:T(8,128)(2,1)S(1)}, u32[]{:S(2)}, u32[]{:S(2)}) async-start(bf16[16,144,384]{2,1,0:T(8,128)(2,1)} %broadcast_in_dim.22), calls=%async_computation.1 | async-start | bytes 3538944 | tf_op jit(solution)/shard_map/all_to_all | solution.py:48
  32.5 105.0 %all-gather.8.cloned.1.call-start = ((), (), s32[]{:S(2)}) async-start(), calls=%async_computation.16 | async-start | bytes 15925248 | tf_op jit(solution)/shard_map/all_gather | solution.py:910
  32.5 23.4 %collective-permute-start = (bf16[16,1024]{1,0:T(8,128)(2,1)S(1)}, bf16[16,1024]{1,0:T(8,128)(2,1)S(1)}, u32[]{:S(2)}, u32[]{:S(2)}) collective-permute-start(bf16[16,1024]{1,0:T(8,128)(2,1)S(1)} %slice_bitcast_fusion), channel_id=1, source_target_pairs={{0,8},{8,16},{16,24},{24,32},{32,40},{40,48},{48,56},{56,64},{64,7... | collective-permute-start | bytes 98312 | tf_op jit(solution)/shard_map/ppermute | solution.py:44
  57.7 9.8 %copy-start.2 = (bf16[16,144,384]{2,1,0:T(8,128)(2,1)}, bf16[16,144,384]{2,1,0:T(8,128)(2,1)S(1)}, u32[]{:S(2)}) copy-start(bf16[16,144,384]{2,1,0:T(8,128)(2,1)S(1)} %all-to-all-done.1.down_hbm_ref) | copy-start | bytes 5308420
  73.4 27.7 %all-to-all-start.2 = ((bf16[16,352,128]{2,1,0:T(8,128)(2,1)}), bf16[16,352,128]{2,1,0:T(8,128)(2,1)S(1)}, u32[]{:S(2)}, u32[]{:S(2)}) async-start(bf16[16,352,128]{2,1,0:T(8,128)(2,1)} %get-tuple-element.62), calls=%async_computation.2 | async-start | bytes 2883584 | tf_op jit(solution)/shard_map/all_to_all | solution.py:48
  101.1 1.1 copy-start
  104.5 13.4 %all-to-all-start.3 = ((bf16[16,96,128]{2,1,0:T(8,128)(2,1)}), bf16[16,96,128]{2,1,0:T(8,128)(2,1)S(1)}, u32[]{:S(2)}, u32[]{:S(2)}) async-start(bf16[16,96,128]{2,1,0:T(8,128)(2,1)} %state_prefix.2), calls=%async_computation.3 | async-start | bytes 786432 | tf_op jit(solution)/shard_map/all_to_all | solution.py:48
  117.9 13.4 %copy-start.7 = (bf16[16,96,128]{2,1,0:T(8,128)(2,1)}, bf16[16,96,128]{2,1,0:T(8,128)(2,1)S(1)}, u32[]{:S(2)}) copy-start(bf16[16,96,128]{2,1,0:T(8,128)(2,1)S(1)} %all-to-all-done.3.starts_ref) | copy-start | bytes 1179652
  119.0 18.4 %all-to-all-start.4 = ((bf16[16,128,256]{2,1,0:T(8,128)(2,1)}), bf16[16,128,256]{2,1,0:T(8,128)(2,1)S(1)}, u32[]{:S(2)}, u32[]{:S(2)}) async-start(bf16[16,128,256]{2,1,0:T(8,128)(2,1)} %broadcast_in_dim.50), calls=%async_computation.4 | async-start | bytes 2097152 | tf_op jit(solution)/shard_map/all_to_all | solution.py:48
  124.6 127.7 %reduce-scatter.5.cloned.1.call-start = ((), (), s32[]{:S(2)}) async-start(), calls=%async_computation.15 | async-start | bytes 18874368 | tf_op jit(solution)/shard_map/reduce_scatter | solution.py:940
  137.4 1.0 copy-start.5
  197.1 12.9 %all-to-all-start.6 = ((bf16[16,96,128]{2,1,0:T(8,128)(2,1)}), bf16[16,96,128]{2,1,0:T(8,128)(2,1)S(1)}, u32[]{:S(2)}, u32[]{:S(2)}) async-start(bf16[16,96,128]{2,1,0:T(8,128)(2,1)} %state_prefix.3), calls=%async_computation.6 | async-start | bytes 786432 | tf_op jit(solution)/shard_map/all_to_all | solution.py:48
  202.7 100.1 %reduce-scatter.3.cloned.1.call-start = ((), (), s32[]{:S(2)}) async-start(), calls=%async_computation.14 | async-start | bytes 9437184 | tf_op jit(solution)/shard_map/reduce_scatter | solution.py:979
  210.0 0.7 copy-start.9
  210.8 9.7 %copy-start.12 = (bf16[128,1536]{1,0:T(8,128)(2,1)S(1)}, bf16[128,1536]{1,0:T(8,128)(2,1)}, u32[]{:S(2)}) copy-start(bf16[128,1536]{1,0:T(8,128)(2,1)} %get-tuple-element.74) | copy-start | bytes 1179652
  216.6 12.0 %copy-start.13 = (bf16[128,768]{1,0:T(8,128)(2,1)S(1)}, bf16[128,768]{1,0:T(8,128)(2,1)}, u32[]{:S(2)}) copy-start(bf16[128,768]{1,0:T(8,128)(2,1)} %get-tuple-element.84) | copy-start | bytes 589828
  217.4 6.1 %collective-permute-start.1 = (bf16[16,1792]{1,0:T(8,128)(2,1)S(1)}, bf16[16,1792]{1,0:T(8,128)(2,1)S(1)}, u32[]{:S(2)}, u32[]{:S(2)}) collective-permute-start(bf16[16,1792]{1,0:T(8,128)(2,1)S(1)} %slice.83), channel_id=1, source_target_pairs={{8,0},{16,8},{24,16},{32,24},{40,32},{48,40},{56,48},{64,56},{72,6... | collective-permute-start | bytes 172040 | tf_op jit(solution)/shard_map/ppermute | solution.py:44
  223.5 0.6 copy-start.14
  228.6 1.0 copy-start.3
  236.0 0.9 copy-start.15
  236.0 1.3 copy-start.4
  252.3 34.9 %all-to-all-start.8 = ((bf16[16,64,1024]{2,1,0:T(8,128)(2,1)}), bf16[16,64,1024]{2,1,0:T(8,128)(2,1)S(1)}, u32[]{:S(2)}, u32[]{:S(2)}) async-start(bf16[16,64,1024]{2,1,0:T(8,128)(2,1)} %bitcast.72), calls=%async_computation.10 | async-start | bytes 4194304 | tf_op jit(solution)/shard_map/all_to_all | solution.py:48
  259.6 103.3 %all-gather.10.cloned.1.call-start = ((), (), s32[]{:S(2)}) async-start(), calls=%async_computation.17 | async-start | bytes 2785280 | tf_op jit(solution)/shard_map/all_gather | solution.py:987
  287.2 1.3 copy-start.1
  328.3 8.1 %copy-start.10 = (f32[128,1024]{1,0:T(8,128)S(1)}, f32[128,1024]{1,0:T(8,128)}, u32[]{:S(2)}) copy-start(f32[128,1024]{1,0:T(8,128)} %get-tuple-element.73) | copy-start | bytes 1572868
  330.7 28.6 %all-to-all-start.10 = ((bf16[16,32,1024]{2,1,0:T(8,128)(2,1)}), bf16[16,32,1024]{2,1,0:T(8,128)(2,1)S(1)}, u32[]{:S(2)}, u32[]{:S(2)}) async-start(bf16[16,32,1024]{2,1,0:T(8,128)(2,1)} %fold.1), calls=%async_computation.12 | async-start | bytes 2097152 | tf_op jit(solution)/shard_map/all_to_all | solution.py:48
  359.3 1.0 copy-start.6
Sparse Core Ops, SparseCore 0:
  10.3 50.9 all-gather.5
  63.0 74.4 all-gather.7
  158.6 89.5 reduce-scatter.4
  250.4 52.3 reduce-scatter.2
  305.4 56.7 all-gather.9

commit v4 on v3

--- a/solution.py
+++ b/solution.py
@@ -307,18 +307,14 @@
     tokens_ref,
     grad_out_ref,
     gain_ref,
-    ssd_ref,
-    gating_ref,
     rest_ref,
     down_hbm_ref,
     middle_hbm_ref,
-    output_ref,
+    residual_ref,
+    hidden_ref,
     grad_residual_ref,
     branch_ref,
     grad_gain_ref,
-    grad_attended_ref,
-    grad_ssd_ref,
-    grad_gating_ref,
     early_ref,
     mout_ref,
     aout_ref,
@@ -378,7 +374,7 @@
         sending.append(copy)
 
     grad_out = grad_out_ref[...]
-    result = jnp.zeros((ROWS, D), f32)
+    residual_ref[...] = residual
     grad_second = jnp.zeros((ROWS, D), f32)
     for half in range(2):
         get_gu[half].wait()
@@ -396,9 +392,7 @@
         w_left = left_ref[4 * half : 4 * (half + 1)].reshape(D, 384)
         w_right = right_ref[4 * half : 4 * (half + 1)].reshape(D, 384)
         w_mid = mid_ref[4 * half : 4 * (half + 1)].reshape(D, 256)
-        result = result + jnp.concatenate(
-            [dot(hidden, w_left), dot(hidden, w_mid), dot(hidden, w_right)], axis=1
-        )
+        hidden_ref[:, D * half : D * (half + 1)] = hidden
         grad_hidden = (
             dot_last(grad_out[:, :384], w_left)
             + dot_last(grad_out[:, 384:640], w_mid)
@@ -416,7 +410,6 @@
             send(own_gu_ref.at[side], early_ref.at[:, pl.ds(begin, 128)], side)
         own_down_ref[...] = dot_first(hidden, grad_out).astype(bf16).reshape(4, 256, D)
         send(own_down_ref, early_ref.at[pl.ds(4 * half, 4), pl.ds(256, 256)], 2)
-    output_ref[...] = (residual + result).astype(bf16)
     grad_gain_ref[...] = jnp.broadcast_to(
         jnp.sum(grad_second * normed, axis=0, keepdims=True), (8, D)
     )
@@ -428,16 +421,6 @@
     send(own_mout_ref, early_ref.at[:, pl.ds(0, 192)], 3)
     own_aout_ref[...] = dot_first(attended_ref[...], branch).astype(bf16).reshape(OWNERS, 64, D)
     send(own_aout_ref, early_ref.at[:, pl.ds(192, 64)], 4)
-    grad_attended_ref[...] = dot_last(branch, aout_ref[...].reshape(Q_WIDTH, D)).astype(bf16)
-    for at in range(0, MI, 384):
-        cols = slice(at, at + 384)
-        w_part = mout_ref[at // 192 : at // 192 + 2].reshape(384, D)
-        grad_mamba = dot_last(branch, w_part)
-        gating = gating_ref[HALO:, cols]
-        logistic = jax.nn.sigmoid(gating)
-        grad_ssd_ref[:, cols] = (grad_mamba * (gating * logistic)).astype(bf16)
-        slope = logistic * (1.0 + gating * (1.0 - logistic))
-        grad_gating_ref[:, cols] = (grad_mamba * ssd_ref[:, cols] * slope).astype(bf16)
     while sending:
         sending.pop().wait()
 
@@ -448,8 +431,6 @@
     tokens,
     grad_out,
     gain,
-    ssd_out,
-    projected,
     rest_weights,
     down_weights,
     middle_weights,
@@ -463,30 +444,24 @@
             whole((ROWS, D)),
             whole((ROWS, D)),
             whole((1, D)),
-            whole((ROWS, MI)),
-            whole((ROWS + HALO, MI)),
             pl.BlockSpec(memory_space=pl.ANY),
             pl.BlockSpec(memory_space=pl.ANY),
             pl.BlockSpec(memory_space=pl.ANY),
         ],
         out_specs=(
             whole((ROWS, D)),
+            whole((ROWS, FF)),
             whole((ROWS, D)),
             whole((ROWS, D)),
             whole((8, D)),
-            whole((ROWS, Q_WIDTH)),
-            whole((ROWS, MI)),
-            whole((ROWS, MI)),
             pl.BlockSpec(memory_space=pl.ANY),
         ),
         out_shape=(
-            struct((ROWS, D), bf16),
+            struct((ROWS, D), f32),
+            struct((ROWS, FF), bf16),
             struct((ROWS, D), f32),
             struct((ROWS, D), bf16),
             struct((8, D), f32),
-            struct((ROWS, Q_WIDTH), bf16),
-            struct((ROWS, MI), bf16),
-            struct((ROWS, MI), bf16),
             struct((OWNERS, D, D), bf16),
         ),
         scratch_shapes=[
@@ -511,12 +486,128 @@
         tokens,
         grad_out,
         gain,
-        ssd_out,
-        projected,
         rest_weights,
         down_weights,
         middle_weights,
     )
+
+
+def branch_back_kernel(
+    branch_ref,
+    ssd_ref,
+    gating_ref,
+    rest_ref,
+    grad_attended_ref,
+    grad_ssd_ref,
+    grad_gating_ref,
+    mout_ref,
+    aout_ref,
+    sems,
+):
+    get_mout = pltpu.make_async_copy(rest_ref.at[:, pl.ds(0, 192)], mout_ref, sems.at[0])
+    get_aout = pltpu.make_async_copy(rest_ref.at[:, pl.ds(192, 64)], aout_ref, sems.at[1])
+    get_mout.start()
+    get_aout.start()
+    branch = branch_ref[...]
+    get_mout.wait()
+    get_aout.wait()
+    grad_attended_ref[...] = dot_last(branch, aout_ref[...].reshape(Q_WIDTH, D)).astype(bf16)
+    for at in range(0, MI, 384):
+        cols = slice(at, at + 384)
+        w_part = mout_ref[at // 192 : at // 192 + 2].reshape(384, D)
+        grad_mamba = dot_last(branch, w_part)
+        gating = gating_ref[HALO:, cols]
+        logistic = jax.nn.sigmoid(gating)
+        grad_ssd_ref[:, cols] = (grad_mamba * (gating * logistic)).astype(bf16)
+        slope = logistic * (1.0 + gating * (1.0 - logistic))
+        grad_gating_ref[:, cols] = (grad_mamba * ssd_ref[:, cols] * slope).astype(bf16)
+
+
+def branch_back(branch_grad, ssd_out, projected, rest_weights):
+    return pl.pallas_call(
+        branch_back_kernel,
+        grid=(1,),
+        in_specs=[
+            whole((ROWS, D)),
+            whole((ROWS, MI)),
+            whole((ROWS + HALO, MI)),
+            pl.BlockSpec(memory_space=pl.ANY),
+        ],
+        out_specs=(whole((ROWS, Q_WIDTH)), whole((ROWS, MI)), whole((ROWS, MI))),
+        out_shape=(
+            struct((ROWS, Q_WIDTH), bf16),
+            struct((ROWS, MI), bf16),
+            struct((ROWS, MI), bf16),
+        ),
+        scratch_shapes=[
+            pltpu.VMEM((OWNERS, 192, D), bf16),
+            pltpu.VMEM((OWNERS, 64, D), bf16),
+            pltpu.SemaphoreType.DMA((2,)),
+        ],
+        compiler_params=params(),
+        name="branch_back",
+    )(branch_grad, ssd_out, projected, rest_weights)
+
+
+def finish_kernel(
+    hidden_ref,
+    residual_ref,
+    rest_ref,
+    left_hbm_ref,
+    mid_hbm_ref,
+    output_ref,
+    left_ref,
+    mid_ref,
+    right_ref,
+    sems,
+):
+    copies = []
+    for owner in range(OWNERS):
+        rows = pl.ds(16 * owner, 16)
+        sem = sems.at[owner]
+        copies.append(pltpu.make_async_copy(left_hbm_ref.at[:, rows], left_ref.at[owner], sem))
+        sem = sems.at[OWNERS + owner]
+        copies.append(pltpu.make_async_copy(mid_hbm_ref.at[:, rows], mid_ref.at[owner], sem))
+    for block in range(3):
+        for part in range(8):
+            source = rest_ref.at[:, pl.ds(256 + 32 * block, 32), pl.ds(128 * part, 128)]
+            target = right_ref.at[:, pl.ds(32 * part, 32), pl.ds(128 * block, 128)]
+            sem = sems.at[2 * OWNERS + 8 * block + part]
+            copies.append(pltpu.make_async_copy(source, target, sem))
+    for copy in copies:
+        copy.start()
+    hidden = hidden_ref[...]
+    residual = residual_ref[...]
+    for copy in copies:
+        copy.wait()
+    left = dot(hidden, left_ref[...].reshape(FF, 384))
+    mid = dot(hidden, mid_ref[...].reshape(FF, 256))
+    right = dot(hidden, right_ref[...].reshape(FF, 384))
+    output_ref[...] = (residual + jnp.concatenate([left, mid, right], axis=1)).astype(bf16)
+
+
+def finish(hidden_act, residual, rest_weights, down_weights, middle_weights):
+    return pl.pallas_call(
+        finish_kernel,
+        grid=(1,),
+        in_specs=[
+            whole((ROWS, FF)),
+            whole((ROWS, D)),
+            pl.BlockSpec(memory_space=pl.ANY),
+            pl.BlockSpec(memory_space=pl.ANY),
+            pl.BlockSpec(memory_space=pl.ANY),
+        ],
+        out_specs=whole((ROWS, D)),
+        out_shape=struct((ROWS, D), bf16),
+        scratch_shapes=[
+            pltpu.VMEM((OWNERS, CTX, 16, 384), bf16),
+            pltpu.VMEM((OWNERS, CTX, 16, 256), bf16),
+            pltpu.VMEM((OWNERS, 256, 384), bf16),
+            pltpu.SemaphoreType.DMA((40,)),
+        ],
+        compiler_params=params(),
+        name="finish",
+    )(hidden_act, residual, rest_weights, down_weights, middle_weights)
 
 
 def attend_back_kernel(
@@ -916,23 +1007,12 @@
     starts = swap(prefix(got, decay_rows, False), "ctx")
     attended, total = attend(first_row, queries, got)
     ssd_out, mamba_in = leave(local_out, starts, activated, cumulative, projected)
-    (
-        output,
-        grad_residual,
-        branch_grad,
-        grad_g_two,
-        grad_attended,
-        grad_ssd,
-        grad_gating,
-        early,
-    ) = middle(
+    residual, hidden_act, grad_residual, branch_grad, grad_g_two, early = middle(
         mamba_in,
         attended,
         tokens,
         grad_out,
         gain_second,
-        ssd_out,
-        projected,
         rest_weights,
         down_weights,
         middle_weights,
@@ -940,6 +1020,9 @@
     early_share = lax.psum_scatter(
         early, "fsdp", scatter_dimension=0, tiled=True
     )[0]
+    grad_attended, grad_ssd, grad_gating = branch_back(
+        branch_grad, ssd_out, projected, rest_weights
+    )
     grad_query, sent_back = attend_back(
         first_row, queries, got, total, grad_attended, grad_ssd, activated, cumulative
     )
@@ -979,7 +1062,10 @@
     late_share = lax.psum_scatter(
         late_grads(shared, grad_proj), "fsdp", scatter_dimension=0, tiled=True
     )[0]
-    early_share, small_got = lax.optimization_barrier((early_share, small_got))
+    early_share, small_got, hidden_act = lax.optimization_barrier(
+        (early_share, small_got, hidden_act)
+    )
+    output = finish(hidden_act, residual, rest_weights, down_weights, middle_weights)
     early_got = swap(early_share.reshape(CTX, 64, D), "ctx")
     small_rows = jnp.concatenate([small_got, jnp.zeros((14, D), bf16)], axis=0)
     early_mine = early_fold(early_got, small_rows)

time: 383 us -> 382 us (level)
  waiting for transfers between devices: 125 us -> 113 us
  Pallas kernels: 80.7 us -> 90.8 us
    pallas_call x0 -> x2, Pallas kernels: none -> 11.4 us  [the longest x1 6 us: branch_back(): pl.pallas_call(branch_back_kernel, grid=(1,), in_specs=[whole((ROWS, D)),...]
    reduce_scatter x1, waiting for transfers between devices: 11.7 us -> 5.71 us  [on_device(): lax.psum_scatter(late_grads(shared, grad_proj), 'fsdp', scatter_dimension...]
    all_to_all x8, waiting for transfers between devices: 90.7 us -> 85.2 us  [swap(): return lax.all_to_all(value, axis, 0, 0, tiled=True)]
  transfers between devices with their start and end apart: 15 -> 15, of which waited for: 12 -> 12; matrix products, arithmetic and copies ran while one was open for 7% -> 7% of each run, Pallas kernels for 15% -> 18%
where the time goes in v4:
time: 382 us; the launch traced here: 375 us
  waiting for transfers between devices  113 us (30%)
  Pallas kernels  90.8 us (24%)
  blocking collectives  60 us (16%)
  starting transfers between devices  57.4 us (15%)
  local copies, waits for them, and re-layouts  20.5 us (5%)
  between operations  14.6 us (4%)
  matrix products  12.8 us (3%)
  other arithmetic  5.72 us (1%)
    all_to_all x8, waiting for transfers between devices, swap(): return lax.all_to_all(value, axis, 0, 0, tiled=True)  85.2 us
    all_to_all x3, blocking collectives, swap(): return lax.all_to_all(value, axis, 0, 0, tiled=True)  60 us
    all_to_all x8, starting transfers between devices, swap(): return lax.all_to_all(value, axis, 0, 0, tiled=True)  50.4 us
    ppermute x2, waiting for transfers between devices, passed_along(): lax.ppermute(value, axis, [(source, source + steps) for source in range(l...  19.1 us
    pallas_call x1, Pallas kernels, middle(): pl.pallas_call(middle_kernel, grid=(1,), in_specs=[whole((ROWS, MI)), who...  19 us
    pallas_call x1, Pallas kernels, attend_back(): pl.pallas_call(attend_back_kernel, grid=(1,), in_specs=[pl.BlockSpec(memo...  10.2 us
    unnamed x44, local copies, waits for them, and re-layouts  7.88 us
  transfers between devices with their start and end apart: 15, of which 12 were waited for; matrix products, arithmetic and copies ran while one was open for 7% of the time, Pallas kernels for 18%

profile of v4, /device:TPU:38, one launch (start us, length us, event | category | flops | bytes accessed | tf_op | source)
XLA Modules:
  0.0 375.1 jit_solution(10303922389409414692)
XLA Ops:
  7.3 2.3 pad_maximum_fusion
  9.8 0.7 constant_dynamic-slice_fusion
  10.6 0.8 broadcast_in_dim.21
  11.3 5.4 %all-to-all-start = ((bf16[8,32,640]{2,1,0:T(8,128)(2,1)}), bf16[8,32,640]{2,1,0:T(8,128)(2,1)S(1)}, u32[]{:S(2)}, u32[]{:S(2)}) async-start(bf16[8,32,640]{2,1,0:T(8,128)(2,1)} %broadcast_in_dim.21), calls=%async_computation | async-start | bytes 655360 | tf_op jit(solution)/shard_map/all_to_all | solution.py:48
  17.3 6.2 %all-to-all-done = bf16[8,32,640]{2,1,0:T(8,128)(2,1)S(1)} async-done(((bf16[8,32,640]{2,1,0:T(8,128)(2,1)}), bf16[8,32,640]{2,1,0:T(8,128)(2,1)S(1)}, u32[]{:S(2)}, u32[]{:S(2)}) %all-to-all-start) | async-done | bytes 327712 | tf_op jit(solution)/shard_map/all_to_all | solution.py:48
  23.6 1.4 broadcast_in_dim.22
  24.9 7.6 %all-to-all-start.1 = ((bf16[16,144,384]{2,1,0:T(8,128)(2,1)}), bf16[16,144,384]{2,1,0:T(8,128)(2,1)S(1)}, u32[]{:S(2)}, u32[]{:S(2)}) async-start(bf16[16,144,384]{2,1,0:T(8,128)(2,1)} %broadcast_in_dim.22), calls=%async_computation.1 | async-start | bytes 3538944 | tf_op jit(solution)/shard_map/all_to_all | solution.py:48
  32.5 3.4 collective-permute-start
  36.0 1.0 multiply_sine_fusion
  36.9 3.0 pack_rest.1
  39.9 16.1 %collective-permute-done = bf16[16,1024]{1,0:T(8,128)(2,1)S(1)} collective-permute-done((bf16[16,1024]{1,0:T(8,128)(2,1)S(1)}, bf16[16,1024]{1,0:T(8,128)(2,1)S(1)}, u32[]{:S(2)}, u32[]{:S(2)}) %collective-permute-start) | collective-permute-done | bytes 32800 | tf_op jit(solution)/shard_map/ppermute | solution.py:44
  56.3 0.7 reshape.206.taps_ref
  58.1 3.2 all-gather.6.cloned.1.call-done
  61.3 6.2 %fusion.17.proj_ref.gating_ref = f32[144,4096]{1,0:T(8,128)} fusion(bf16[144,1024]{1,0:T(8,128)(2,1)S(1)} %get-tuple-element.58, bf16[1024,4096]{1,0:T(8,128)(2,1)} %all-gather.6.cloned.1.call-done), kind=kOutput, calls=%fused_computation.61 | convolution fusion | flops 1207959552 | bytes 11042816 | tf_op jit(solution)/shard_map/dot_general | solution.py:69
  67.6 5.9 %enter.1 = (bf16[144,1792]{1,0:T(8,128)(2,1)}, f32[128,1792]{1,0:T(8,128)}, bf16[128,1792]{1,0:T(8,128)(2,1)}, f32[128,1536]{1,0:T(8,128)}, bf16[1024,128]{1,0:T(8,128)(2,1)}, /*index=5*/bf16[16,352,128]{2,1,0:T(8,128)(2,1)}) custom-call(f32[144,4096]{1,0:T(8,128)} %fusion.17.proj_ref.gating_ref, f32[4,1792]{1,0:T(4,128)} %reshape.206.taps_ref, ...), custom_call_target="tpu_custom_call" | custom-call | tf_op jit(solution)/shard_map/enter/pallas_call | solution.py:198
  73.4 7.3 %all-to-all-start.2 = ((bf16[16,352,128]{2,1,0:T(8,128)(2,1)}), bf16[16,352,128]{2,1,0:T(8,128)(2,1)S(1)}, u32[]{:S(2)}, u32[]{:S(2)}) async-start(bf16[16,352,128]{2,1,0:T(8,128)(2,1)} %get-tuple-element.65), calls=%async_computation.2 | async-start | bytes 2883584 | tf_op jit(solution)/shard_map/all_to_all | solution.py:48
  80.7 1.2 copy.31.decay_ref
  81.9 19.2 %all-to-all-done.2.parts_ref.got_ref = bf16[16,352,128]{2,1,0:T(8,128)(2,1)S(1)} async-done(((bf16[16,352,128]{2,1,0:T(8,128)(2,1)}), bf16[16,352,128]{2,1,0:T(8,128)(2,1)S(1)}, u32[]{:S(2)}, u32[]{:S(2)}) %all-to-all-start.2) | async-done | bytes 1441824 | tf_op jit(solution)/shard_map/all_to_all | solution.py:48
  101.1 1.1 copy-done
  102.2 2.3 state_prefix.2
  104.5 6.2 %all-to-all-start.3 = ((bf16[16,96,128]{2,1,0:T(8,128)(2,1)}), bf16[16,96,128]{2,1,0:T(8,128)(2,1)S(1)}, u32[]{:S(2)}, u32[]{:S(2)}) async-start(bf16[16,96,128]{2,1,0:T(8,128)(2,1)} %state_prefix.2), calls=%async_computation.3 | async-start | bytes 786432 | tf_op jit(solution)/shard_map/all_to_all | solution.py:48
  110.7 7.3 %all-to-all-done.3.starts_ref = bf16[16,96,128]{2,1,0:T(8,128)(2,1)S(1)} async-done(((bf16[16,96,128]{2,1,0:T(8,128)(2,1)}), bf16[16,96,128]{2,1,0:T(8,128)(2,1)S(1)}, u32[]{:S(2)}, u32[]{:S(2)}) %all-to-all-start.3) | async-done | bytes 393248 | tf_op jit(solution)/shard_map/all_to_all | solution.py:48
  118.0 1.1 broadcast_in_dim.50
  119.0 5.6 %all-to-all-start.4 = ((bf16[16,128,256]{2,1,0:T(8,128)(2,1)}), bf16[16,128,256]{2,1,0:T(8,128)(2,1)S(1)}, u32[]{:S(2)}, u32[]{:S(2)}) async-start(bf16[16,128,256]{2,1,0:T(8,128)(2,1)} %broadcast_in_dim.50), calls=%async_computation.4 | async-start | bytes 2097152 | tf_op jit(solution)/shard_map/all_to_all | solution.py:48
  124.8 6.6 %attend.1 = (bf16[128,512]{1,0:T(8,128)(2,1)}, f32[2,8,512]{2,1,0:T(8,128)}) custom-call(s32[1]{0:T(128)} %bitcast.12.first_row_ref, bf16[1024,128]{1,0:T(8,128)(2,1)} %get-tuple-element.69.query_ref, bf16[16,352,128]{2,1,0:T(8,128)(2,1)} %copy-done), custom_call_target="tpu_custom_call" | custom-call | tf_op jit(solution)/shard_map/attend/pallas_call | solution.py:260
  131.4 3.3 leave.1
  134.7 2.7 all-to-all-done.4.middle_hbm_ref.mid_hbm_ref
  137.5 0.9 copy-done.2
  138.4 19.0 %middle.1 = (f32[128,1024]{1,0:T(8,128)}, bf16[128,2048]{1,0:T(8,128)(2,1)}, f32[128,1024]{1,0:T(8,128)}, bf16[128,1024]{1,0:T(8,128)(2,1)}, f32[8,1024]{1,0:T(8,128)}, /*index=5*/bf16[8,1024,1024]{2,1,0:T(8,128)(2,1)}) custom-call(bf16[128,1536]{1,0:T(8,128)(2,1)} %get-tuple-element.68.mamba_ref, bf16[128,512]{1,0:T(8,128)(2,1)} %get-tuple-element.70.attended_ref, ...), custom_call_target="tpu_custom_call" | custom-call | tf_op jit(solution)/shard_map/middle/pallas_call | solution.py:438
  157.4 6.0 %branch_back.1 = (bf16[128,512]{1,0:T(8,128)(2,1)}, bf16[128,1536]{1,0:T(8,128)(2,1)}, bf16[128,1536]{1,0:T(8,128)(2,1)}) custom-call(bf16[128,1024]{1,0:T(8,128)(2,1)} %get-tuple-element.75.branch_ref, f32[128,1536]{1,0:T(8,128)} %get-tuple-element.76.ssd_ref, f32[144,4096]{1,0:T(8,128)} %fusion.17.proj_ref.gating_ref, bf16[8,864,1024]{2,1,0:T(8,128)(2,1)} %bitcast.68), custom_call_target="tpu_custom_call" | custom-call | tf_op jit(solution)/shard_map/branch_back/pallas_call | solution.py:527
  163.4 10.2 %attend_back.1 = (f32[128,512]{1,0:T(8,128)}, bf16[16,352,128]{2,1,0:T(8,128)(2,1)}) custom-call(s32[1]{0:T(128)} %bitcast.12.first_row_ref, bf16[1024,128]{1,0:T(8,128)(2,1)} %get-tuple-element.69.query_ref, bf16[16,352,128]{2,1,0:T(8,128)(2,1)} %copy-done, f32[2,8,512]{2,1,0:T(8,128)} %get-tuple-element.80.total_ref, ...), custom_call_target="tpu_custom_call" | custom-call | tf_op jit(solution)/shard_map/attend_back/pallas_call | solution.py:668
  173.6 26.1 %all_to_all.55.parts_ref.got_ref = bf16[16,352,128]{2,1,0:T(8,128)(2,1)} all-to-all(bf16[16,352,128]{2,1,0:T(8,128)(2,1)} %get-tuple-element.82), channel_id=1, replica_groups=mesh['ctx'=16,'fsdp'=8] {'ctx'}, dimensions={0} | all-to-all | bytes 2883584 | tf_op jit(solution)/shard_map/all_to_all | solution.py:48
  199.7 2.3 state_prefix.3
  202.0 5.6 %all-to-all-start.6 = ((bf16[16,96,128]{2,1,0:T(8,128)(2,1)}), bf16[16,96,128]{2,1,0:T(8,128)(2,1)S(1)}, u32[]{:S(2)}, u32[]{:S(2)}) async-start(bf16[16,96,128]{2,1,0:T(8,128)(2,1)} %state_prefix.3), calls=%async_computation.7 | async-start | bytes 786432 | tf_op jit(solution)/shard_map/all_to_all | solution.py:48
  207.9 0.7 slice.102.shared_ref
  208.7 6.3 %all-to-all-done.6.ends_ref = bf16[16,96,128]{2,1,0:T(8,128)(2,1)S(1)} async-done(((bf16[16,96,128]{2,1,0:T(8,128)(2,1)}), bf16[16,96,128]{2,1,0:T(8,128)(2,1)S(1)}, u32[]{:S(2)}, u32[]{:S(2)}) %all-to-all-start.6) | async-done | bytes 393248 | tf_op jit(solution)/shard_map/all_to_all | solution.py:48
  214.9 0.7 copy-done.9
  215.7 5.8 %ssd_back.1 = (bf16[128,1792]{1,0:T(8,128)(2,1)}, bf16[128,768]{1,0:T(8,128)(2,1)}) custom-call(bf16[128,1536]{1,0:T(8,128)(2,1)} %get-tuple-element.78.grad_ssd_ref, bf16[128,1792]{1,0:T(8,128)(2,1)} %get-tuple-element.67.act_ref.inputs_c_ref, f32[128,1792]{1,0:T(8,128)} %get-tuple-element.79.conv_out_ref, f32[24,128]{1,0:T(8,128)} %copy-done.11, ...), custom_call_target="tpu_custom_call" | custom-call | tf_op jit(solution)/shard_map/ssd_back/pallas_call | solution.py:762
  221.5 0.9 slice.82
  222.3 3.0 collective-permute-start.1
  225.4 3.0 collective-permute-done.1.ahead_ref
  229.0 3.4 conv_back.1
  232.4 1.1 constant_dynamic-update-slice_fusion.1
  233.5 1.0 copy-done.4
  234.4 6.3 %late_grads.1 = bf16[8,512,1024]{2,1,0:T(8,128)(2,1)} custom-call(bf16[128,1024]{1,0:T(8,128)(2,1)} %slice.102.shared_ref, bf16[128,4096]{1,0:T(8,128)(2,1)} %copy-done.4), custom_call_target="tpu_custom_call" | custom-call | tf_op jit(solution)/shard_map/late_grads/pallas_call | solution.py:806
  240.8 0.9 fusion.11
  242.0 6.5 %multiply_reduce_fusion = (f32[128]{0:T(128)S(1)}, bf16[1024]{0:T(1024)(128)(2,1)S(1)}, f32[128,1024]{1,0:T(8,128)S(1)}) fusion(f32[144,1024]{1,0:T(8,128)S(1)} %get-tuple-element.107, f32[1024]{0:T(1024)S(1)} %get-tuple-element.112, bf16[128,4096]{1,0:T(8,128)(2,1)S(1)} %copy-done.5, bf16[1024,4096]{1,0:T(8,128)(2,1)} %all-gather.6.cloned.1.call-done), kind=kOutput, calls=%fused_computation.6 | convolution fusion | flops 1074396032 | bytes 10492416 | tf_op jit(solution)/shard_map/dot_general | solution.py:73
  248.6 8.4 %all_to_all.56 = bf16[8,2,1024]{2,1,0:T(2,128)(2,1)S(1)} all-to-all(bf16[8,2,1024]{2,1,0:T(2,128)(2,1)S(1)} %copy.34), channel_id=1, replica_groups=mesh['ctx'=16,'fsdp'=8] {'fsdp'}, dimensions={0} | all-to-all | bytes 65536 | tf_op jit(solution)/shard_map/all_to_all | solution.py:48
  257.1 7.2 %all-to-all-start.8 = ((bf16[16,64,1024]{2,1,0:T(8,128)(2,1)}), bf16[16,64,1024]{2,1,0:T(8,128)(2,1)S(1)}, u32[]{:S(2)}, u32[]{:S(2)}) async-start(bf16[16,64,1024]{2,1,0:T(8,128)(2,1)} %bitcast.74), calls=%async_computation.10 | async-start | bytes 4194304 | tf_op jit(solution)/shard_map/all_to_all | solution.py:48
  265.0 26.9 %all-to-all-done.8.parts_ref = bf16[16,64,1024]{2,1,0:T(8,128)(2,1)S(1)} async-done(((bf16[16,64,1024]{2,1,0:T(8,128)(2,1)}), bf16[16,64,1024]{2,1,0:T(8,128)(2,1)S(1)}, u32[]{:S(2)}, u32[]{:S(2)}) %all-to-all-start.8) | async-done | bytes 2097184 | tf_op jit(solution)/shard_map/all_to_all | solution.py:48
  291.9 1.3 copy-done.3
  293.2 2.6 early_fold.1
  295.8 5.7 %reduce-scatter.5.cloned.1.call-done = bf16[1,512,1024]{2,1,0:T(8,128)(2,1)} async-done(((bf16[8,512,1024]{2,1,0:T(8,128)(2,1)}), bf16[1,512,1024]{2,1,0:T(8,128)(2,1)}) %reduce-scatter.5.cloned.1.call-update) | async-done | bytes 1048592 | tf_op jit(solution)/shard_map/reduce_scatter | solution.py:1062
  301.5 25.5 %all_to_all.57.parts_ref = bf16[16,32,1024]{2,1,0:T(8,128)(2,1)} all-to-all(bf16[16,32,1024]{2,1,0:T(8,128)(2,1)} %bitcast.75), channel_id=1, replica_groups=mesh['ctx'=16,'fsdp'=8] {'ctx'}, dimensions={0} | all-to-all | bytes 2097152 | tf_op jit(solution)/shard_map/all_to_all | solution.py:48
  327.0 2.4 fold.1
  329.4 5.6 %all-to-all-start.10 = ((bf16[16,32,1024]{2,1,0:T(8,128)(2,1)}), bf16[16,32,1024]{2,1,0:T(8,128)(2,1)S(1)}, u32[]{:S(2)}, u32[]{:S(2)}) async-start(bf16[16,32,1024]{2,1,0:T(8,128)(2,1)} %fold.1), calls=%async_computation.12 | async-start | bytes 2097152 | tf_op jit(solution)/shard_map/all_to_all | solution.py:48
  335.1 1.0 add_bitcast_fusion
  336.1 5.4 %finish.1 = bf16[128,1024]{1,0:T(8,128)(2,1)} custom-call(bf16[128,2048]{1,0:T(8,128)(2,1)} %get-tuple-element.91.hidden_ref, f32[128,1024]{1,0:T(8,128)} %get-tuple-element.92.residual_ref, bf16[8,864,1024]{2,1,0:T(8,128)(2,1)} %bitcast.69, bf16[16,144,384]{2,1,0:T(8,128)(2,1)} %copy-done.1, bf16[16,128,256]{2,1,0:T(8,128)(2,1)} %copy-done.2), custom_call_target="tpu_custom_call" | custom-call | tf_op jit(solution)/shard_map/finish/pallas_call | solution.py:590
  341.4 16.6 %all-to-all-done.10.parts_ref = bf16[16,32,1024]{2,1,0:T(8,128)(2,1)S(1)} async-done(((bf16[16,32,1024]{2,1,0:T(8,128)(2,1)}), bf16[16,32,1024]{2,1,0:T(8,128)(2,1)S(1)}, u32[]{:S(2)}, u32[]{:S(2)}) %all-to-all-start.10) | async-done | bytes 1048608 | tf_op jit(solution)/shard_map/all_to_all | solution.py:48
  358.0 1.0 copy-done.6
  359.0 2.6 spread.1
  361.6 3.8 %early_spread.1 = (f32[192,1024]{1,0:T(8,128)}, f32[64,1024]{1,0:T(8,128)}, f32[256,1024]{1,0:T(8,128)}, f32[128,4096]{1,0:T(8,128)}, f32[16,1024]{1,0:T(8,128)}) custom-call(bf16[16,80,1024]{2,1,0:T(8,128)(2,1)} %bitcast.70), custom_call_target="tpu_custom_call" | custom-call | tf_op jit(solution)/shard_map/early_spread/pallas_call | solution.py:873
  365.4 1.3 slice_bitcast_fusion.3
  366.7 0.8 slice_reduce_fusion
  (94 shorter events, 5.4 us)
Async XLA Ops:
  7.2 2.5 copy-start.17
  7.2 2.6 copy-start.18
  7.2 2.6 copy-start.19
  7.2 9.5 %copy-start.16 = (f32[1,128,24]{1,2,0:T(8,128)S(1)}, f32[1,128,24]{1,2,0:T(8,128)}, u32[]{:S(2)}) copy-start(f32[1,128,24]{1,2,0:T(8,128)} %param.23) | copy-start | bytes 36868
  7.2 54.1 %all-gather.6.cloned.1.call-start = ((), (), s32[]{:S(2)}) async-start(), calls=%async_computation.13 | async-start | bytes 9437184 | tf_op jit(solution)/shard_map/all_gather | solution.py:929
  11.3 12.2 %all-to-all-start = ((bf16[8,32,640]{2,1,0:T(8,128)(2,1)}), bf16[8,32,640]{2,1,0:T(8,128)(2,1)S(1)}, u32[]{:S(2)}, u32[]{:S(2)}) async-start(bf16[8,32,640]{2,1,0:T(8,128)(2,1)} %broadcast_in_dim.21), calls=%async_computation | async-start | bytes 655360 | tf_op jit(solution)/shard_map/all_to_all | solution.py:48
  17.0 7.9 %copy-start.11 = (f32[24,128]{1,0:T(8,128)}, f32[24,128]{1,0:T(8,128)S(1)}, u32[]{:S(2)}) copy-start(f32[24,128]{1,0:T(8,128)S(1)} %reduce_window_sum.11.cum_t_ref) | copy-start | bytes 36868
  24.9 7.6 %copy-start.8 = (bf16[1,128,1024]{2,1,0:T(8,128)(2,1)S(1)}, bf16[1,128,1024]{2,1,0:T(8,128)(2,1)}, u32[]{:S(2)}) copy-start(bf16[1,128,1024]{2,1,0:T(8,128)(2,1)} %param.13) | copy-start | bytes 786436
  24.9 32.8 %all-to-all-start.1 = ((bf16[16,144,384]{2,1,0:T(8,128)(2,1)}), bf16[16,144,384]{2,1,0:T(8,128)(2,1)S(1)}, u32[]{:S(2)}, u32[]{:S(2)}) async-start(bf16[16,144,384]{2,1,0:T(8,128)(2,1)} %broadcast_in_dim.22), calls=%async_computation.1 | async-start | bytes 3538944 | tf_op jit(solution)/shard_map/all_to_all | solution.py:48
  32.5 105.0 %all-gather.8.cloned.1.call-start = ((), (), s32[]{:S(2)}) async-start(), calls=%async_computation.16 | async-start | bytes 15925248 | tf_op jit(solution)/shard_map/all_gather | solution.py:1001
  32.5 23.4 %collective-permute-start = (bf16[16,1024]{1,0:T(8,128)(2,1)S(1)}, bf16[16,1024]{1,0:T(8,128)(2,1)S(1)}, u32[]{:S(2)}, u32[]{:S(2)}) collective-permute-start(bf16[16,1024]{1,0:T(8,128)(2,1)S(1)} %slice_bitcast_fusion), channel_id=1, source_target_pairs={{0,8},{8,16},{16,24},{24,32},{32,40},{40,48},{48,56},{56,64},{64,7... | collective-permute-start | bytes 98312 | tf_op jit(solution)/shard_map/ppermute | solution.py:44
  57.7 9.8 %copy-start.1 = (bf16[16,144,384]{2,1,0:T(8,128)(2,1)}, bf16[16,144,384]{2,1,0:T(8,128)(2,1)S(1)}, u32[]{:S(2)}) copy-start(bf16[16,144,384]{2,1,0:T(8,128)(2,1)S(1)} %all-to-all-done.1.down_hbm_ref.left_hbm_ref) | copy-start | bytes 5308420
  73.4 27.7 %all-to-all-start.2 = ((bf16[16,352,128]{2,1,0:T(8,128)(2,1)}), bf16[16,352,128]{2,1,0:T(8,128)(2,1)S(1)}, u32[]{:S(2)}, u32[]{:S(2)}) async-start(bf16[16,352,128]{2,1,0:T(8,128)(2,1)} %get-tuple-element.65), calls=%async_computation.2 | async-start | bytes 2883584 | tf_op jit(solution)/shard_map/all_to_all | solution.py:48
  101.1 1.1 copy-start
  104.5 13.4 %all-to-all-start.3 = ((bf16[16,96,128]{2,1,0:T(8,128)(2,1)}), bf16[16,96,128]{2,1,0:T(8,128)(2,1)S(1)}, u32[]{:S(2)}, u32[]{:S(2)}) async-start(bf16[16,96,128]{2,1,0:T(8,128)(2,1)} %state_prefix.2), calls=%async_computation.3 | async-start | bytes 786432 | tf_op jit(solution)/shard_map/all_to_all | solution.py:48
  118.0 13.4 %copy-start.7 = (bf16[16,96,128]{2,1,0:T(8,128)(2,1)}, bf16[16,96,128]{2,1,0:T(8,128)(2,1)S(1)}, u32[]{:S(2)}) copy-start(bf16[16,96,128]{2,1,0:T(8,128)(2,1)S(1)} %all-to-all-done.3.starts_ref) | copy-start | bytes 1179652
  119.0 18.4 %all-to-all-start.4 = ((bf16[16,128,256]{2,1,0:T(8,128)(2,1)}), bf16[16,128,256]{2,1,0:T(8,128)(2,1)S(1)}, u32[]{:S(2)}, u32[]{:S(2)}) async-start(bf16[16,128,256]{2,1,0:T(8,128)(2,1)} %broadcast_in_dim.50), calls=%async_computation.4 | async-start | bytes 2097152 | tf_op jit(solution)/shard_map/all_to_all | solution.py:48
  124.6 132.5 %reduce-scatter.3.cloned.1.call-start = ((), (), s32[]{:S(2)}) async-start(), calls=%async_computation.14 | async-start | bytes 18874368 | tf_op jit(solution)/shard_map/reduce_scatter | solution.py:1020
  137.4 1.0 copy-start.2
  202.0 12.9 %all-to-all-start.6 = ((bf16[16,96,128]{2,1,0:T(8,128)(2,1)}), bf16[16,96,128]{2,1,0:T(8,128)(2,1)S(1)}, u32[]{:S(2)}, u32[]{:S(2)}) async-start(bf16[16,96,128]{2,1,0:T(8,128)(2,1)} %state_prefix.3), calls=%async_computation.7 | async-start | bytes 786432 | tf_op jit(solution)/shard_map/all_to_all | solution.py:48
  207.6 93.9 %reduce-scatter.5.cloned.1.call-start = ((), (), s32[]{:S(2)}) async-start(), calls=%async_computation.15 | async-start | bytes 9437184 | tf_op jit(solution)/shard_map/reduce_scatter | solution.py:1062
  214.9 0.7 copy-start.9
  215.7 9.7 %copy-start.12 = (bf16[128,1536]{1,0:T(8,128)(2,1)S(1)}, bf16[128,1536]{1,0:T(8,128)(2,1)}, u32[]{:S(2)}) copy-start(bf16[128,1536]{1,0:T(8,128)(2,1)} %get-tuple-element.77) | copy-start | bytes 1179652
  221.5 12.0 %copy-start.13 = (bf16[128,768]{1,0:T(8,128)(2,1)S(1)}, bf16[128,768]{1,0:T(8,128)(2,1)}, u32[]{:S(2)}) copy-start(bf16[128,768]{1,0:T(8,128)(2,1)} %get-tuple-element.87) | copy-start | bytes 589828
  222.3 6.1 %collective-permute-start.1 = (bf16[16,1792]{1,0:T(8,128)(2,1)S(1)}, bf16[16,1792]{1,0:T(8,128)(2,1)S(1)}, u32[]{:S(2)}, u32[]{:S(2)}) collective-permute-start(bf16[16,1792]{1,0:T(8,128)(2,1)S(1)} %slice.82), channel_id=1, source_target_pairs={{8,0},{16,8},{24,16},{32,24},{40,32},{48,40},{56,48},{64,56},{72,6... | collective-permute-start | bytes 172040 | tf_op jit(solution)/shard_map/ppermute | solution.py:44
  228.4 0.6 copy-start.14
  233.5 1.0 copy-start.4
  240.8 0.9 copy-start.15
  240.8 1.3 copy-start.5
  257.1 34.8 %all-to-all-start.8 = ((bf16[16,64,1024]{2,1,0:T(8,128)(2,1)}), bf16[16,64,1024]{2,1,0:T(8,128)(2,1)S(1)}, u32[]{:S(2)}, u32[]{:S(2)}) async-start(bf16[16,64,1024]{2,1,0:T(8,128)(2,1)} %bitcast.74), calls=%async_computation.10 | async-start | bytes 4194304 | tf_op jit(solution)/shard_map/all_to_all | solution.py:48
  264.3 97.3 %all-gather.10.cloned.1.call-start = ((), (), s32[]{:S(2)}) async-start(), calls=%async_computation.17 | async-start | bytes 2785280 | tf_op jit(solution)/shard_map/all_gather | solution.py:1073
  291.9 1.3 copy-start.3
  327.0 8.1 %copy-start.10 = (f32[128,1024]{1,0:T(8,128)S(1)}, f32[128,1024]{1,0:T(8,128)}, u32[]{:S(2)}) copy-start(f32[128,1024]{1,0:T(8,128)} %get-tuple-element.93) | copy-start | bytes 1572868
  329.4 28.6 %all-to-all-start.10 = ((bf16[16,32,1024]{2,1,0:T(8,128)(2,1)}), bf16[16,32,1024]{2,1,0:T(8,128)(2,1)S(1)}, u32[]{:S(2)}, u32[]{:S(2)}) async-start(bf16[16,32,1024]{2,1,0:T(8,128)(2,1)} %fold.1), calls=%async_computation.12 | async-start | bytes 2097152 | tf_op jit(solution)/shard_map/all_to_all | solution.py:48
  358.0 1.0 copy-start.6
Sparse Core Ops, SparseCore 0:
  10.3 50.9 all-gather.5
  63.0 74.4 all-gather.7
  157.5 89.5 reduce-scatter.2
  249.4 52.0 reduce-scatter.4
  304.1 56.7 all-gather.9

commit v5 on v4

--- a/solution.py
+++ b/solution.py
@@ -850,7 +850,7 @@
     )(parts)
 
 
-def early_spread_kernel(parts_ref, mout_ref, aout_ref, down_ref, gu_ref, small_ref):
+def early_spread_kernel(parts_ref, mout_ref, aout_ref, down_ref, gu_ref, conv_ref, one_ref, two_ref):
     for part in range(CTX):
         values = parts_ref[part, :64].astype(f32)
         if part < 3:
@@ -866,7 +866,9 @@
     total = parts_ref[0, 64:].astype(f32)
     for part in range(1, CTX):
         total = total + parts_ref[part, 64:].astype(f32)
-    small_ref[...] = total
+    conv_ref[...] = total[:CONV, : XBC // OWNERS]
+    one_ref[...] = total[4:5, :128]
+    two_ref[...] = total[4:5, 128:256]
 
 
 def early_spread(parts):
@@ -877,7 +879,9 @@
             struct((64, D), f32),
             struct((256, D), f32),
             struct((ROWS, 2 * FF), f32),
-            struct((16, D), f32),
+            struct((CONV, XBC // OWNERS), f32),
+            struct((1, 128), f32),
+            struct((1, 128), f32),
         ),
         compiler_params=params(),
         name="early_spread",
@@ -1049,15 +1053,17 @@
     grad_tokens = grad_residual + rms_back(grad_shared, normed, inverse_one, gain_first)
 
     conv_owned = grad_conv.reshape(CONV, OWNERS, XBC // OWNERS).transpose(1, 0, 2)
+    gain_grads = jnp.concatenate(
+        [grad_g_one.reshape(OWNERS, 1, 128), grad_g_two[0].reshape(OWNERS, 1, 128)], axis=2
+    )
     small_grads = jnp.concatenate(
         [
-            grad_g_one.reshape(OWNERS, 128),
-            conv_owned.reshape(OWNERS, 896),
-            grad_g_two[0].reshape(OWNERS, 128),
-            jnp.zeros((OWNERS, 896), f32),
+            jnp.pad(conv_owned, ((0, 0), (0, 0), (0, 32))),
+            gain_grads,
+            jnp.zeros((OWNERS, 3, 256), f32),
         ],
         axis=1,
-    ).astype(bf16).reshape(OWNERS, 2, D)
+    ).astype(bf16)
     small_got = jnp.sum(swap(small_grads, "fsdp").astype(f32), axis=0).astype(bf16)
     late_share = lax.psum_scatter(
         late_grads(shared, grad_proj), "fsdp", scatter_dimension=0, tiled=True
@@ -1067,23 +1073,23 @@
     )
     output = finish(hidden_act, residual, rest_weights, down_weights, middle_weights)
     early_got = swap(early_share.reshape(CTX, 64, D), "ctx")
-    small_rows = jnp.concatenate([small_got, jnp.zeros((14, D), bf16)], axis=0)
+    small_rows = jnp.pad(small_got, ((0, 8), (0, D - 256)))
     early_mine = early_fold(early_got, small_rows)
     late_share, early_mine = lax.optimization_barrier((late_share, early_mine))
     early_sum = lax.all_gather(early_mine, "ctx", axis=0, tiled=False)
     late_sum = swap(fold(swap(late_share.reshape(CTX, 32, D), "ctx")), "ctx")
-    grad_mout, grad_aout, grad_down, grad_gate_up, small_sum = early_spread(early_sum)
+    grad_mout, grad_aout, grad_down, grad_gate_up, conv_sum, one_sum, two_sum = early_spread(early_sum)
     grad_in, grad_qkv = spread(late_sum)
     return (
         output[None],
         grad_tokens[None],
-        small_sum[0, :128],
+        one_sum.reshape(128),
         grad_in,
-        small_sum[0, 128:].reshape(CONV, XBC // OWNERS).T,
+        conv_sum.T,
         grad_mout,
         grad_qkv,
         grad_aout,
-        small_sum[1, :128],
+        two_sum.reshape(128),
         grad_gate_up,
         grad_down,
     )

time: 382 us -> 379 us (level)
  no operation moved by 1% of the time
where the time goes in v5:
time: 379 us; the launch traced here: 372 us
  waiting for transfers between devices  113 us (30%)
  Pallas kernels  90.8 us (24%)
  blocking collectives  60 us (16%)
  starting transfers between devices  57.4 us (15%)
  local copies, waits for them, and re-layouts  17.8 us (5%)
  between operations  14.6 us (4%)
  matrix products  12.7 us (3%)
  other arithmetic  5.75 us (2%)
    all_to_all x8, waiting for transfers between devices, swap(): return lax.all_to_all(value, axis, 0, 0, tiled=True)  85.2 us
    all_to_all x3, blocking collectives, swap(): return lax.all_to_all(value, axis, 0, 0, tiled=True)  60 us
    all_to_all x8, starting transfers between devices, swap(): return lax.all_to_all(value, axis, 0, 0, tiled=True)  50.4 us
    ppermute x2, waiting for transfers between devices, passed_along(): lax.ppermute(value, axis, [(source, source + steps) for source in range(l...  19.1 us
    pallas_call x1, Pallas kernels, middle(): pl.pallas_call(middle_kernel, grid=(1,), in_specs=[whole((ROWS, MI)), who...  18.9 us
    pallas_call x1, Pallas kernels, attend_back(): pl.pallas_call(attend_back_kernel, grid=(1,), in_specs=[pl.BlockSpec(memo...  10.2 us
    unnamed x44, local copies, waits for them, and re-layouts  7.92 us
  transfers between devices with their start and end apart: 15, of which 12 were waited for; matrix products, arithmetic and copies ran while one was open for 7% of the time, Pallas kernels for 18%

profile of v5, /device:TPU:38, one launch (start us, length us, event | category | flops | bytes accessed | tf_op | source)
XLA Modules:
  0.0 372.4 jit_solution(3934012073630412962)
XLA Ops:
  7.3 2.3 pad_maximum_fusion
  9.8 0.7 constant_dynamic-slice_fusion
  10.6 0.8 broadcast_in_dim.21
  11.3 5.4 %all-to-all-start = ((bf16[8,32,640]{2,1,0:T(8,128)(2,1)}), bf16[8,32,640]{2,1,0:T(8,128)(2,1)S(1)}, u32[]{:S(2)}, u32[]{:S(2)}) async-start(bf16[8,32,640]{2,1,0:T(8,128)(2,1)} %broadcast_in_dim.21), calls=%async_computation | async-start | bytes 655360 | tf_op jit(solution)/shard_map/all_to_all | solution.py:48
  17.3 6.2 %all-to-all-done = bf16[8,32,640]{2,1,0:T(8,128)(2,1)S(1)} async-done(((bf16[8,32,640]{2,1,0:T(8,128)(2,1)}), bf16[8,32,640]{2,1,0:T(8,128)(2,1)S(1)}, u32[]{:S(2)}, u32[]{:S(2)}) %all-to-all-start) | async-done | bytes 327712 | tf_op jit(solution)/shard_map/all_to_all | solution.py:48
  23.6 1.4 broadcast_in_dim.22
  24.9 7.6 %all-to-all-start.1 = ((bf16[16,144,384]{2,1,0:T(8,128)(2,1)}), bf16[16,144,384]{2,1,0:T(8,128)(2,1)S(1)}, u32[]{:S(2)}, u32[]{:S(2)}) async-start(bf16[16,144,384]{2,1,0:T(8,128)(2,1)} %broadcast_in_dim.22), calls=%async_computation.1 | async-start | bytes 3538944 | tf_op jit(solution)/shard_map/all_to_all | solution.py:48
  32.5 3.4 collective-permute-start
  36.0 1.0 multiply_sine_fusion
  36.9 3.0 pack_rest.1
  39.9 16.1 %collective-permute-done = bf16[16,1024]{1,0:T(8,128)(2,1)S(1)} collective-permute-done((bf16[16,1024]{1,0:T(8,128)(2,1)S(1)}, bf16[16,1024]{1,0:T(8,128)(2,1)S(1)}, u32[]{:S(2)}, u32[]{:S(2)}) %collective-permute-start) | collective-permute-done | bytes 32800 | tf_op jit(solution)/shard_map/ppermute | solution.py:44
  56.3 0.7 reshape.206.taps_ref
  58.1 3.2 all-gather.6.cloned.1.call-done
  61.3 6.2 %fusion.20.proj_ref.gating_ref = f32[144,4096]{1,0:T(8,128)} fusion(bf16[144,1024]{1,0:T(8,128)(2,1)S(1)} %get-tuple-element.60, bf16[1024,4096]{1,0:T(8,128)(2,1)} %all-gather.6.cloned.1.call-done), kind=kOutput, calls=%fused_computation.62 | convolution fusion | flops 1207959552 | bytes 11042816 | tf_op jit(solution)/shard_map/dot_general | solution.py:69
  67.6 5.9 %enter.1 = (bf16[144,1792]{1,0:T(8,128)(2,1)}, f32[128,1792]{1,0:T(8,128)}, bf16[128,1792]{1,0:T(8,128)(2,1)}, f32[128,1536]{1,0:T(8,128)}, bf16[1024,128]{1,0:T(8,128)(2,1)}, /*index=5*/bf16[16,352,128]{2,1,0:T(8,128)(2,1)}) custom-call(f32[144,4096]{1,0:T(8,128)} %fusion.20.proj_ref.gating_ref, f32[4,1792]{1,0:T(4,128)} %reshape.206.taps_ref, ...), custom_call_target="tpu_custom_call" | custom-call | tf_op jit(solution)/shard_map/enter/pallas_call | solution.py:198
  73.4 7.3 %all-to-all-start.2 = ((bf16[16,352,128]{2,1,0:T(8,128)(2,1)}), bf16[16,352,128]{2,1,0:T(8,128)(2,1)S(1)}, u32[]{:S(2)}, u32[]{:S(2)}) async-start(bf16[16,352,128]{2,1,0:T(8,128)(2,1)} %get-tuple-element.67), calls=%async_computation.2 | async-start | bytes 2883584 | tf_op jit(solution)/shard_map/all_to_all | solution.py:48
  80.7 1.2 copy.35.decay_ref
  81.9 19.2 %all-to-all-done.2.parts_ref.got_ref = bf16[16,352,128]{2,1,0:T(8,128)(2,1)S(1)} async-done(((bf16[16,352,128]{2,1,0:T(8,128)(2,1)}), bf16[16,352,128]{2,1,0:T(8,128)(2,1)S(1)}, u32[]{:S(2)}, u32[]{:S(2)}) %all-to-all-start.2) | async-done | bytes 1441824 | tf_op jit(solution)/shard_map/all_to_all | solution.py:48
  101.1 1.1 copy-done
  102.2 2.3 state_prefix.2
  104.5 6.2 %all-to-all-start.3 = ((bf16[16,96,128]{2,1,0:T(8,128)(2,1)}), bf16[16,96,128]{2,1,0:T(8,128)(2,1)S(1)}, u32[]{:S(2)}, u32[]{:S(2)}) async-start(bf16[16,96,128]{2,1,0:T(8,128)(2,1)} %state_prefix.2), calls=%async_computation.3 | async-start | bytes 786432 | tf_op jit(solution)/shard_map/all_to_all | solution.py:48
  110.7 7.3 %all-to-all-done.3.starts_ref = bf16[16,96,128]{2,1,0:T(8,128)(2,1)S(1)} async-done(((bf16[16,96,128]{2,1,0:T(8,128)(2,1)}), bf16[16,96,128]{2,1,0:T(8,128)(2,1)S(1)}, u32[]{:S(2)}, u32[]{:S(2)}) %all-to-all-start.3) | async-done | bytes 393248 | tf_op jit(solution)/shard_map/all_to_all | solution.py:48
  117.9 1.1 broadcast_in_dim.49
  119.0 5.6 %all-to-all-start.4 = ((bf16[16,128,256]{2,1,0:T(8,128)(2,1)}), bf16[16,128,256]{2,1,0:T(8,128)(2,1)S(1)}, u32[]{:S(2)}, u32[]{:S(2)}) async-start(bf16[16,128,256]{2,1,0:T(8,128)(2,1)} %broadcast_in_dim.49), calls=%async_computation.4 | async-start | bytes 2097152 | tf_op jit(solution)/shard_map/all_to_all | solution.py:48
  124.8 6.5 %attend.1 = (bf16[128,512]{1,0:T(8,128)(2,1)}, f32[2,8,512]{2,1,0:T(8,128)}) custom-call(s32[1]{0:T(128)} %bitcast.12.first_row_ref, bf16[1024,128]{1,0:T(8,128)(2,1)} %get-tuple-element.71.query_ref, bf16[16,352,128]{2,1,0:T(8,128)(2,1)} %copy-done), custom_call_target="tpu_custom_call" | custom-call | tf_op jit(solution)/shard_map/attend/pallas_call | solution.py:260
  131.4 3.3 leave.1
  134.7 2.7 all-to-all-done.4.middle_hbm_ref.mid_hbm_ref
  137.5 0.9 copy-done.2
  138.4 18.9 %middle.1 = (f32[128,1024]{1,0:T(8,128)}, bf16[128,2048]{1,0:T(8,128)(2,1)}, f32[128,1024]{1,0:T(8,128)}, bf16[128,1024]{1,0:T(8,128)(2,1)}, f32[8,1024]{1,0:T(8,128)}, /*index=5*/bf16[8,1024,1024]{2,1,0:T(8,128)(2,1)}) custom-call(bf16[128,1536]{1,0:T(8,128)(2,1)} %get-tuple-element.70.mamba_ref, bf16[128,512]{1,0:T(8,128)(2,1)} %get-tuple-element.72.attended_ref, ...), custom_call_target="tpu_custom_call" | custom-call | tf_op jit(solution)/shard_map/middle/pallas_call | solution.py:438
  157.4 6.0 %branch_back.1 = (bf16[128,512]{1,0:T(8,128)(2,1)}, bf16[128,1536]{1,0:T(8,128)(2,1)}, bf16[128,1536]{1,0:T(8,128)(2,1)}) custom-call(bf16[128,1024]{1,0:T(8,128)(2,1)} %get-tuple-element.77.branch_ref, f32[128,1536]{1,0:T(8,128)} %get-tuple-element.78.ssd_ref, f32[144,4096]{1,0:T(8,128)} %fusion.20.proj_ref.gating_ref, bf16[8,864,1024]{2,1,0:T(8,128)(2,1)} %bitcast.65), custom_call_target="tpu_custom_call" | custom-call | tf_op jit(solution)/shard_map/branch_back/pallas_call | solution.py:527
  163.4 10.2 %attend_back.1 = (f32[128,512]{1,0:T(8,128)}, bf16[16,352,128]{2,1,0:T(8,128)(2,1)}) custom-call(s32[1]{0:T(128)} %bitcast.12.first_row_ref, bf16[1024,128]{1,0:T(8,128)(2,1)} %get-tuple-element.71.query_ref, bf16[16,352,128]{2,1,0:T(8,128)(2,1)} %copy-done, f32[2,8,512]{2,1,0:T(8,128)} %get-tuple-element.81.total_ref, ...), custom_call_target="tpu_custom_call" | custom-call | tf_op jit(solution)/shard_map/attend_back/pallas_call | solution.py:668
  173.6 26.1 %all_to_all.55.parts_ref.got_ref = bf16[16,352,128]{2,1,0:T(8,128)(2,1)} all-to-all(bf16[16,352,128]{2,1,0:T(8,128)(2,1)} %get-tuple-element.83), channel_id=1, replica_groups=mesh['ctx'=16,'fsdp'=8] {'ctx'}, dimensions={0} | all-to-all | bytes 2883584 | tf_op jit(solution)/shard_map/all_to_all | solution.py:48
  199.8 2.3 state_prefix.3
  202.0 5.6 %all-to-all-start.6 = ((bf16[16,96,128]{2,1,0:T(8,128)(2,1)}), bf16[16,96,128]{2,1,0:T(8,128)(2,1)S(1)}, u32[]{:S(2)}, u32[]{:S(2)}) async-start(bf16[16,96,128]{2,1,0:T(8,128)(2,1)} %state_prefix.3), calls=%async_computation.7 | async-start | bytes 786432 | tf_op jit(solution)/shard_map/all_to_all | solution.py:48
  208.0 0.7 slice.90.shared_ref
  208.7 6.3 %all-to-all-done.6.ends_ref = bf16[16,96,128]{2,1,0:T(8,128)(2,1)S(1)} async-done(((bf16[16,96,128]{2,1,0:T(8,128)(2,1)}), bf16[16,96,128]{2,1,0:T(8,128)(2,1)S(1)}, u32[]{:S(2)}, u32[]{:S(2)}) %all-to-all-start.6) | async-done | bytes 393248 | tf_op jit(solution)/shard_map/all_to_all | solution.py:48
  214.9 0.7 copy-done.9
  215.7 5.8 %ssd_back.1 = (bf16[128,1792]{1,0:T(8,128)(2,1)}, bf16[128,768]{1,0:T(8,128)(2,1)}) custom-call(bf16[128,1536]{1,0:T(8,128)(2,1)} %get-tuple-element.79.grad_ssd_ref, bf16[128,1792]{1,0:T(8,128)(2,1)} %get-tuple-element.69.act_ref.inputs_c_ref, f32[128,1792]{1,0:T(8,128)} %get-tuple-element.80.conv_out_ref, f32[24,128]{1,0:T(8,128)} %copy-done.11, ...), custom_call_target="tpu_custom_call" | custom-call | tf_op jit(solution)/shard_map/ssd_back/pallas_call | solution.py:762
  221.5 0.9 slice.73
  222.4 3.0 collective-permute-start.1
  225.5 3.0 collective-permute-done.1.ahead_ref
  228.4 0.6 copy-done.14
  229.0 3.4 conv_back.1
  232.4 1.1 constant_dynamic-update-slice_fusion.1
  233.5 1.0 copy-done.4
  234.5 6.3 %late_grads.1 = bf16[8,512,1024]{2,1,0:T(8,128)(2,1)} custom-call(bf16[128,1024]{1,0:T(8,128)(2,1)} %slice.90.shared_ref, bf16[128,4096]{1,0:T(8,128)(2,1)} %copy-done.4), custom_call_target="tpu_custom_call" | custom-call | tf_op jit(solution)/shard_map/late_grads/pallas_call | solution.py:806
  240.9 0.8 fusion.14
  242.1 6.5 %multiply_reduce_fusion = (f32[128]{0:T(128)S(1)}, bf16[1024]{0:T(1024)(128)(2,1)S(1)}, f32[128,1024]{1,0:T(8,128)S(1)}) fusion(f32[144,1024]{1,0:T(8,128)S(1)} %get-tuple-element.111, f32[1024]{0:T(1024)S(1)} %get-tuple-element.114, bf16[128,4096]{1,0:T(8,128)(2,1)S(1)} %copy-done.5, bf16[1024,4096]{1,0:T(8,128)(2,1)} %all-gather.6.cloned.1.call-done), kind=kOutput, calls=%fused_computation.6 | convolution fusion | flops 1074396032 | bytes 10492416 | tf_op jit(solution)/shard_map/dot_general | solution.py:73
  248.7 8.4 %all_to_all.56 = bf16[8,8,256]{2,1,0:T(8,128)(2,1)S(1)} all-to-all(bf16[8,8,256]{2,1,0:T(8,128)(2,1)S(1)} %fusion.3), channel_id=1, replica_groups=mesh['ctx'=16,'fsdp'=8] {'fsdp'}, dimensions={0} | all-to-all | bytes 65536 | tf_op jit(solution)/shard_map/all_to_all | solution.py:48
  257.1 7.2 %all-to-all-start.8 = ((bf16[16,64,1024]{2,1,0:T(8,128)(2,1)}), bf16[16,64,1024]{2,1,0:T(8,128)(2,1)S(1)}, u32[]{:S(2)}, u32[]{:S(2)}) async-start(bf16[16,64,1024]{2,1,0:T(8,128)(2,1)} %bitcast.71), calls=%async_computation.10 | async-start | bytes 4194304 | tf_op jit(solution)/shard_map/all_to_all | solution.py:48
  264.4 0.6 pad.15.small_ref
  265.0 26.9 %all-to-all-done.8.parts_ref = bf16[16,64,1024]{2,1,0:T(8,128)(2,1)S(1)} async-done(((bf16[16,64,1024]{2,1,0:T(8,128)(2,1)}), bf16[16,64,1024]{2,1,0:T(8,128)(2,1)S(1)}, u32[]{:S(2)}, u32[]{:S(2)}) %all-to-all-start.8) | async-done | bytes 2097184 | tf_op jit(solution)/shard_map/all_to_all | solution.py:48
  292.0 1.3 copy-done.3
  293.3 2.6 early_fold.1
  295.8 5.7 %reduce-scatter.5.cloned.1.call-done = bf16[1,512,1024]{2,1,0:T(8,128)(2,1)} async-done(((bf16[8,512,1024]{2,1,0:T(8,128)(2,1)}), bf16[1,512,1024]{2,1,0:T(8,128)(2,1)}) %reduce-scatter.5.cloned.1.call-update) | async-done | bytes 1048592 | tf_op jit(solution)/shard_map/reduce_scatter | solution.py:1068
  301.5 25.4 %all_to_all.57.parts_ref = bf16[16,32,1024]{2,1,0:T(8,128)(2,1)} all-to-all(bf16[16,32,1024]{2,1,0:T(8,128)(2,1)} %bitcast.72), channel_id=1, replica_groups=mesh['ctx'=16,'fsdp'=8] {'ctx'}, dimensions={0} | all-to-all | bytes 2097152 | tf_op jit(solution)/shard_map/all_to_all | solution.py:48
  327.0 2.4 fold.1
  329.4 5.6 %all-to-all-start.10 = ((bf16[16,32,1024]{2,1,0:T(8,128)(2,1)}), bf16[16,32,1024]{2,1,0:T(8,128)(2,1)S(1)}, u32[]{:S(2)}, u32[]{:S(2)}) async-start(bf16[16,32,1024]{2,1,0:T(8,128)(2,1)} %fold.1), calls=%async_computation.12 | async-start | bytes 2097152 | tf_op jit(solution)/shard_map/all_to_all | solution.py:48
  335.1 1.0 add_bitcast_fusion
  336.1 5.4 %finish.1 = bf16[128,1024]{1,0:T(8,128)(2,1)} custom-call(bf16[128,2048]{1,0:T(8,128)(2,1)} %get-tuple-element.93.hidden_ref, f32[128,1024]{1,0:T(8,128)} %get-tuple-element.94.residual_ref, bf16[8,864,1024]{2,1,0:T(8,128)(2,1)} %bitcast.66, bf16[16,144,384]{2,1,0:T(8,128)(2,1)} %copy-done.1, bf16[16,128,256]{2,1,0:T(8,128)(2,1)} %copy-done.2), custom_call_target="tpu_custom_call" | custom-call | tf_op jit(solution)/shard_map/finish/pallas_call | solution.py:590
  341.4 16.6 %all-to-all-done.10.parts_ref = bf16[16,32,1024]{2,1,0:T(8,128)(2,1)S(1)} async-done(((bf16[16,32,1024]{2,1,0:T(8,128)(2,1)}), bf16[16,32,1024]{2,1,0:T(8,128)(2,1)S(1)}, u32[]{:S(2)}, u32[]{:S(2)}) %all-to-all-start.10) | async-done | bytes 1048608 | tf_op jit(solution)/shard_map/all_to_all | solution.py:48
  358.0 1.0 copy-done.6
  359.0 2.6 spread.1
  361.6 3.8 %early_spread.1 = (f32[192,1024]{1,0:T(8,128)}, f32[64,1024]{1,0:T(8,128)}, f32[256,1024]{1,0:T(8,128)}, f32[128,4096]{1,0:T(8,128)}, f32[4,224]{1,0:T(4,128)}, /*index=5*/f32[1,128]{1,0:T(1,128)}, f32[1,128]{1,0:T(1,128)}) custom-call(bf16[16,80,1024]{2,1,0:T(8,128)(2,1)} %bitcast.67), custom_call_target="tpu_custom_call" | custom-call | tf_op jit(solution)/shard_map/early_spread/pallas_call | solution.py:875
  (91 shorter events, 3.6 us)
Async XLA Ops:
  7.2 2.5 copy-start.17
  7.2 2.6 copy-start.18
  7.2 2.6 copy-start.19
  7.2 9.5 %copy-start.16 = (f32[1,128,24]{1,2,0:T(8,128)S(1)}, f32[1,128,24]{1,2,0:T(8,128)}, u32[]{:S(2)}) copy-start(f32[1,128,24]{1,2,0:T(8,128)} %param.23) | copy-start | bytes 36868
  7.2 54.1 %all-gather.6.cloned.1.call-start = ((), (), s32[]{:S(2)}) async-start(), calls=%async_computation.13 | async-start | bytes 9437184 | tf_op jit(solution)/shard_map/all_gather | solution.py:933
  11.3 12.2 %all-to-all-start = ((bf16[8,32,640]{2,1,0:T(8,128)(2,1)}), bf16[8,32,640]{2,1,0:T(8,128)(2,1)S(1)}, u32[]{:S(2)}, u32[]{:S(2)}) async-start(bf16[8,32,640]{2,1,0:T(8,128)(2,1)} %broadcast_in_dim.21), calls=%async_computation | async-start | bytes 655360 | tf_op jit(solution)/shard_map/all_to_all | solution.py:48
  17.0 7.9 %copy-start.11 = (f32[24,128]{1,0:T(8,128)}, f32[24,128]{1,0:T(8,128)S(1)}, u32[]{:S(2)}) copy-start(f32[24,128]{1,0:T(8,128)S(1)} %reduce_window_sum.11.cum_t_ref) | copy-start | bytes 36868
  24.9 7.6 %copy-start.8 = (bf16[1,128,1024]{2,1,0:T(8,128)(2,1)S(1)}, bf16[1,128,1024]{2,1,0:T(8,128)(2,1)}, u32[]{:S(2)}) copy-start(bf16[1,128,1024]{2,1,0:T(8,128)(2,1)} %param.13) | copy-start | bytes 786436
  24.9 32.8 %all-to-all-start.1 = ((bf16[16,144,384]{2,1,0:T(8,128)(2,1)}), bf16[16,144,384]{2,1,0:T(8,128)(2,1)S(1)}, u32[]{:S(2)}, u32[]{:S(2)}) async-start(bf16[16,144,384]{2,1,0:T(8,128)(2,1)} %broadcast_in_dim.22), calls=%async_computation.1 | async-start | bytes 3538944 | tf_op jit(solution)/shard_map/all_to_all | solution.py:48
  32.5 105.0 %all-gather.8.cloned.1.call-start = ((), (), s32[]{:S(2)}) async-start(), calls=%async_computation.16 | async-start | bytes 15925248 | tf_op jit(solution)/shard_map/all_gather | solution.py:1005
  32.5 23.4 %collective-permute-start = (bf16[16,1024]{1,0:T(8,128)(2,1)S(1)}, bf16[16,1024]{1,0:T(8,128)(2,1)S(1)}, u32[]{:S(2)}, u32[]{:S(2)}) collective-permute-start(bf16[16,1024]{1,0:T(8,128)(2,1)S(1)} %slice_bitcast_fusion), channel_id=1, source_target_pairs={{0,8},{8,16},{16,24},{24,32},{32,40},{40,48},{48,56},{56,64},{64,7... | collective-permute-start | bytes 98312 | tf_op jit(solution)/shard_map/ppermute | solution.py:44
  57.7 9.8 %copy-start.1 = (bf16[16,144,384]{2,1,0:T(8,128)(2,1)}, bf16[16,144,384]{2,1,0:T(8,128)(2,1)S(1)}, u32[]{:S(2)}) copy-start(bf16[16,144,384]{2,1,0:T(8,128)(2,1)S(1)} %all-to-all-done.1.down_hbm_ref.left_hbm_ref) | copy-start | bytes 5308420
  73.4 27.7 %all-to-all-start.2 = ((bf16[16,352,128]{2,1,0:T(8,128)(2,1)}), bf16[16,352,128]{2,1,0:T(8,128)(2,1)S(1)}, u32[]{:S(2)}, u32[]{:S(2)}) async-start(bf16[16,352,128]{2,1,0:T(8,128)(2,1)} %get-tuple-element.67), calls=%async_computation.2 | async-start | bytes 2883584 | tf_op jit(solution)/shard_map/all_to_all | solution.py:48
  101.1 1.1 copy-start
  104.5 13.4 %all-to-all-start.3 = ((bf16[16,96,128]{2,1,0:T(8,128)(2,1)}), bf16[16,96,128]{2,1,0:T(8,128)(2,1)S(1)}, u32[]{:S(2)}, u32[]{:S(2)}) async-start(bf16[16,96,128]{2,1,0:T(8,128)(2,1)} %state_prefix.2), calls=%async_computation.3 | async-start | bytes 786432 | tf_op jit(solution)/shard_map/all_to_all | solution.py:48
  117.9 13.4 %copy-start.7 = (bf16[16,96,128]{2,1,0:T(8,128)(2,1)}, bf16[16,96,128]{2,1,0:T(8,128)(2,1)S(1)}, u32[]{:S(2)}) copy-start(bf16[16,96,128]{2,1,0:T(8,128)(2,1)S(1)} %all-to-all-done.3.starts_ref) | copy-start | bytes 1179652
  119.0 18.4 %all-to-all-start.4 = ((bf16[16,128,256]{2,1,0:T(8,128)(2,1)}), bf16[16,128,256]{2,1,0:T(8,128)(2,1)S(1)}, u32[]{:S(2)}, u32[]{:S(2)}) async-start(bf16[16,128,256]{2,1,0:T(8,128)(2,1)} %broadcast_in_dim.49), calls=%async_computation.4 | async-start | bytes 2097152 | tf_op jit(solution)/shard_map/all_to_all | solution.py:48
  124.6 132.5 %reduce-scatter.3.cloned.1.call-start = ((), (), s32[]{:S(2)}) async-start(), calls=%async_computation.14 | async-start | bytes 18874368 | tf_op jit(solution)/shard_map/reduce_scatter | solution.py:1024
  137.4 1.0 copy-start.2
  202.0 12.9 %all-to-all-start.6 = ((bf16[16,96,128]{2,1,0:T(8,128)(2,1)}), bf16[16,96,128]{2,1,0:T(8,128)(2,1)S(1)}, u32[]{:S(2)}, u32[]{:S(2)}) async-start(bf16[16,96,128]{2,1,0:T(8,128)(2,1)} %state_prefix.3), calls=%async_computation.7 | async-start | bytes 786432 | tf_op jit(solution)/shard_map/all_to_all | solution.py:48
  207.7 93.9 %reduce-scatter.5.cloned.1.call-start = ((), (), s32[]{:S(2)}) async-start(), calls=%async_computation.15 | async-start | bytes 9437184 | tf_op jit(solution)/shard_map/reduce_scatter | solution.py:1068
  214.9 0.7 copy-start.9
  215.7 9.7 %copy-start.12 = (bf16[128,1536]{1,0:T(8,128)(2,1)S(1)}, bf16[128,1536]{1,0:T(8,128)(2,1)}, u32[]{:S(2)}) copy-start(bf16[128,1536]{1,0:T(8,128)(2,1)} %get-tuple-element.88) | copy-start | bytes 1179652
  221.5 12.0 %copy-start.13 = (bf16[128,768]{1,0:T(8,128)(2,1)S(1)}, bf16[128,768]{1,0:T(8,128)(2,1)}, u32[]{:S(2)}) copy-start(bf16[128,768]{1,0:T(8,128)(2,1)} %get-tuple-element.90) | copy-start | bytes 589828
  222.4 6.1 %collective-permute-start.1 = (bf16[16,1792]{1,0:T(8,128)(2,1)S(1)}, bf16[16,1792]{1,0:T(8,128)(2,1)S(1)}, u32[]{:S(2)}, u32[]{:S(2)}) collective-permute-start(bf16[16,1792]{1,0:T(8,128)(2,1)S(1)} %slice.73), channel_id=1, source_target_pairs={{8,0},{16,8},{24,16},{32,24},{40,32},{48,40},{56,48},{64,56},{72,6... | collective-permute-start | bytes 172040 | tf_op jit(solution)/shard_map/ppermute | solution.py:44
  228.4 0.6 copy-start.14
  233.5 1.0 copy-start.4
  240.8 1.0 copy-start.15
  240.8 1.3 copy-start.5
  257.1 34.8 %all-to-all-start.8 = ((bf16[16,64,1024]{2,1,0:T(8,128)(2,1)}), bf16[16,64,1024]{2,1,0:T(8,128)(2,1)S(1)}, u32[]{:S(2)}, u32[]{:S(2)}) async-start(bf16[16,64,1024]{2,1,0:T(8,128)(2,1)} %bitcast.71), calls=%async_computation.10 | async-start | bytes 4194304 | tf_op jit(solution)/shard_map/all_to_all | solution.py:48
  264.4 97.3 %all-gather.10.cloned.1.call-start = ((), (), s32[]{:S(2)}) async-start(), calls=%async_computation.17 | async-start | bytes 2785280 | tf_op jit(solution)/shard_map/all_gather | solution.py:1079
  292.0 1.3 copy-start.3
  327.0 8.1 %copy-start.10 = (f32[128,1024]{1,0:T(8,128)S(1)}, f32[128,1024]{1,0:T(8,128)}, u32[]{:S(2)}) copy-start(f32[128,1024]{1,0:T(8,128)} %get-tuple-element.95) | copy-start | bytes 1572868
  329.4 28.6 %all-to-all-start.10 = ((bf16[16,32,1024]{2,1,0:T(8,128)(2,1)}), bf16[16,32,1024]{2,1,0:T(8,128)(2,1)S(1)}, u32[]{:S(2)}, u32[]{:S(2)}) async-start(bf16[16,32,1024]{2,1,0:T(8,128)(2,1)} %fold.1), calls=%async_computation.12 | async-start | bytes 2097152 | tf_op jit(solution)/shard_map/all_to_all | solution.py:48
  358.0 1.0 copy-start.6
Sparse Core Ops, SparseCore 0:
  10.3 50.9 all-gather.5
  63.0 74.4 all-gather.7
  157.5 89.5 reduce-scatter.2
  249.4 52.0 reduce-scatter.4
  304.1 56.7 all-gather.9
